TPU v7x, 32 devices: a whole 2x2x4 slice. The times are simulated.
32 devices in a mesh: dp: 4 (over z), ctx: 2 (over y), tensor: 4 (over x, core).
Axes of the slice: x: 2, y: 2, z: 4, core: 2. Of those that a mesh axis runs over, the one named last changes fastest.
Arguments:
- tokens: bfloat16 [4, 1024, 1024], P('dp', 'ctx')
- segments: int32 [4, 1024], P('dp', 'ctx'), may hold values from 0 to 767, as said below
- padding: int32 [4, 1024], P('dp', 'ctx'), may hold values from 0 to 1, as said below
- cotangent: bfloat16 [4, 1024, 1024], P('dp', 'ctx'), may hold values from -6 to 6
- norm1_gain: float32 [1024], replicated, may hold values from 0.5 to 1.5
- norm1_shift: float32 [1024], replicated, may hold values from -2 to 2
- norm2_gain: float32 [1024], replicated, may hold values from 0.5 to 1.5
- norm2_shift: float32 [1024], replicated, may hold values from -2 to 2
- qkv_weight: bfloat16 [1024, 3, 1024], P(None, None, 'tensor'), may hold values from -0.1875 to 0.1875
- qkv_bias: float32 [3, 1024], P(None, 'tensor'), may hold values from -3 to 3
- out_weight: bfloat16 [1024, 1024], P('tensor'), may hold values from -1 to 1
- out_bias: float32 [1024], replicated, may hold values from -2 to 2
- up_weight: bfloat16 [1024, 4096], P(None, 'tensor'), may hold values from -0.1875 to 0.1875
- up_bias: float32 [4096], P('tensor'), may hold values from -3 to 3
- down_weight: bfloat16 [4096, 1024], P('tensor'), may hold values from -0.09375 to 0.09375
- down_bias: float32 [1024], replicated, may hold values from -2 to 2
Outputs:
- block_output: bfloat16 [4, 1024, 1024], P('dp', 'ctx')
- input_grad: bfloat16 [4, 1024, 1024], P('dp', 'ctx')
- grad_norm1_gain: float32 [1024], replicated
- grad_norm1_shift: float32 [1024], replicated
- grad_norm2_gain: float32 [1024], replicated
- grad_norm2_shift: float32 [1024], replicated
- grad_qkv: float32 [1024, 3, 1024], P(None, None, 'tensor')
- grad_qkv_bias: float32 [3, 1024], P(None, 'tensor')
- grad_out: float32 [1024, 1024], P('tensor')
- grad_out_bias: float32 [1024], replicated
- grad_up: float32 [1024, 4096], P(None, 'tensor')
- grad_up_bias: float32 [4096], P('tensor')
- grad_down: float32 [4096, 1024], P('tensor')
- grad_down_bias: float32 [1024], replicated
Inputs may be any that keep to these rules, and one draw needn't show every extreme that they name: `segments`: within a sequence the ids never fall; a token's id is the position at which its document begins; the first token of a sequence begins a document. Each sequence is real tokens followed by a padding tail of 1 to 256 tokens, which lies inside the sequence's last document after at least one real token of it.
All inputs are finite; a program needn't handle non-finite values.
Results may differ from a plain program's by a relative error of at most 0.018.
Values may be sent and summed in bfloat16 or wider, within the bound.
No kernel may reach another device: no remote copies, remote signals or barrier semaphores. Data moves between devices by JAX's collectives and lax.ppermute only.
A program may use at most 128 MiB of HBM per device.

v0:
```python
import jax
import jax.numpy as jnp
from jax import lax
from jax.sharding import PartitionSpec as P

HEAD_DIM = 64
ROT = 16
KBLOCK = 512


def layer_norm(values, gain_vec, shift_vec):
    centre = jnp.mean(values, axis=-1, keepdims=True)
    centred = values - centre
    spread = jnp.mean(centred * centred, axis=-1, keepdims=True)
    return centred * lax.rsqrt(spread + 1e-05) * gain_vec + shift_vec


def norm_back(values, gain_vec, shift_vec, upstream):
    outcome, pullback = jax.vjp(layer_norm, values, gain_vec, shift_vec)
    return pullback(upstream)


def gelu_exact(values):
    return jax.nn.gelu(values, approximate=False)


def rotary_tables(positions):
    half_dims = ROT // 2
    freq_index = jnp.arange(half_dims, dtype=jnp.float32)
    inverse = jnp.exp(freq_index * (-2.0 * jnp.log(10000.0) / ROT))
    angles = positions.astype(jnp.float32)[:, None] * inverse[None, :]
    return (jnp.cos(angles)[:, None, :], jnp.sin(angles)[:, None, :])


def rotate(values, cosine_tab, sine_tab):
    half_dims = ROT // 2
    first_half = values[..., :half_dims]
    second_half = values[..., half_dims:ROT]
    return jnp.concatenate(
        [
            first_half * cosine_tab - second_half * sine_tab,
            second_half * cosine_tab + first_half * sine_tab,
            values[..., ROT:],
        ],
        axis=-1,
    )


def score_block(query_block, key_block, query_at, query_doc, key_at, key_doc):
    scores = jnp.einsum(
        "qhd,khd->hqk", query_block, key_block, preferred_element_type=jnp.float32
    ) * HEAD_DIM ** (-0.5)
    visible = (key_at[None, :] <= query_at[:, None]) & (
        (key_doc[None, :] == query_doc[:, None]) | (key_at[None, :] == query_at[:, None])
    )
    return (scores, visible[None])


def grad_scores(
    query_block,
    grad_block,
    query_at,
    query_doc,
    top_block,
    delta_block,
    key_block,
    value_block,
    key_at,
    key_doc,
):
    scores, visible = score_block(query_block, key_block, query_at, query_doc, key_at, key_doc)
    probs_full = jnp.where(
        visible, jnp.exp(jnp.where(visible, scores, -1e30) - top_block[..., None]), 0.0
    )
    probs_grad = jnp.einsum(
        "qhd,khd->hqk", grad_block, value_block, preferred_element_type=jnp.float32
    )
    score_grad = (probs_full * (probs_grad - delta_block[..., None])).astype(jnp.bfloat16)
    return (probs_full.astype(jnp.bfloat16), score_grad)


def on_device(
    tokens,
    segments,
    padding,
    cotangent,
    norm1_gain,
    norm1_shift,
    norm2_gain,
    norm2_shift,
    qkv_weight,
    qkv_bias,
    out_weight,
    out_bias,
    up_weight,
    up_bias,
    down_weight,
    down_bias,
):
    inputs = tokens[0].astype(jnp.float32)
    seg_own = segments[0]
    pad_own = padding[0]
    span_rows = inputs.shape[0]
    local_width = qkv_weight.shape[2]
    heads_loc = local_width // HEAD_DIM
    score_scale = HEAD_DIM ** (-0.5)
    query_pos = lax.axis_index("ctx") * span_rows + jnp.arange(span_rows, dtype=jnp.int32)
    normed1 = layer_norm(inputs, norm1_gain, norm1_shift).astype(jnp.bfloat16)
    normed2 = layer_norm(inputs, norm2_gain, norm2_shift).astype(jnp.bfloat16)
    projected = (
        jnp.einsum("cd,dtf->ctf", normed1, qkv_weight, preferred_element_type=jnp.float32)
        + qkv_bias[None]
    )
    projected = projected.reshape(span_rows, 3, heads_loc, HEAD_DIM)
    cosine_tab, sine_tab = rotary_tables(query_pos)
    queries = rotate(projected[:, 0], cosine_tab, sine_tab).astype(jnp.bfloat16)
    keys_own = rotate(projected[:, 1], cosine_tab, sine_tab).astype(jnp.bfloat16)
    values_own = projected[:, 2].astype(jnp.bfloat16)
    code_own = jnp.where(pad_own == 1, seg_own, -1)
    keys_all, values_all, codes_all = (
        lax.all_gather(keys_own.reshape(span_rows, local_width), "ctx", axis=0, tiled=True),
        lax.all_gather(values_own.reshape(span_rows, local_width), "ctx", axis=0, tiled=True),
        lax.all_gather(code_own, "ctx", axis=0, tiled=True),
    )
    seq_len = keys_all.shape[0]
    block_count = seq_len // KBLOCK
    key_pos = jnp.arange(seq_len, dtype=jnp.int32)
    key_blocks = keys_all.reshape(block_count, KBLOCK, heads_loc, HEAD_DIM)
    value_blocks = values_all.reshape(block_count, KBLOCK, heads_loc, HEAD_DIM)
    code_blocks = codes_all.reshape(block_count, KBLOCK)
    pos_blocks = key_pos.reshape(block_count, KBLOCK)

    def total_step(state_pair, block_data):
        run_top, run_sum = state_pair
        key_block, code_block, pos_block = block_data
        scores, visible = score_block(queries, key_block, query_pos, seg_own, pos_block, code_block)
        masked = jnp.where(visible, scores, -1e30)
        new_top = jnp.maximum(run_top, jnp.max(masked, axis=-1))
        fresh_sum = jnp.sum(jnp.where(visible, jnp.exp(masked - new_top[..., None]), 0.0), axis=-1)
        return ((new_top, run_sum * jnp.exp(run_top - new_top) + fresh_sum), None)

    start_state = (
        jnp.full((heads_loc, span_rows), -1e30, jnp.float32),
        jnp.zeros((heads_loc, span_rows), jnp.float32),
    )
    final_pair, unused = lax.scan(total_step, start_state, (key_blocks, code_blocks, pos_blocks))
    log_total = final_pair[0] + jnp.log(final_pair[1])

    def attend_step(running, block_data):
        key_block, value_block, code_block, pos_block = block_data
        scores, visible = score_block(queries, key_block, query_pos, seg_own, pos_block, code_block)
        weights_low = jnp.where(
            visible, jnp.exp(jnp.where(visible, scores, -1e30) - log_total[..., None]), 0.0
        ).astype(jnp.bfloat16)
        return (
            running
            + jnp.einsum(
                "hqk,khd->qhd", weights_low, value_block, preferred_element_type=jnp.float32
            ),
            None,
        )

    zero_heads = jnp.zeros((span_rows, heads_loc, HEAD_DIM), jnp.float32)
    attended, unused = lax.scan(
        attend_step, zero_heads, (key_blocks, value_blocks, code_blocks, pos_blocks)
    )
    attended_b = attended.reshape(span_rows, local_width).astype(jnp.bfloat16)
    upward = jnp.dot(normed2, up_weight, preferred_element_type=jnp.float32) + up_bias
    activated = gelu_exact(upward).astype(jnp.bfloat16)
    partial_sum = jnp.dot(attended_b, out_weight, preferred_element_type=jnp.float32) + jnp.dot(
        activated, down_weight, preferred_element_type=jnp.float32
    )
    bias_sum = out_bias + down_bias
    summed = lax.psum(partial_sum.astype(jnp.bfloat16), "tensor").astype(jnp.float32)
    block_output = (inputs + summed + bias_sum).astype(jnp.bfloat16)
    grad_in = cotangent[0]
    grad_att_b = jnp.einsum(
        "cd,fd->cf", grad_in, out_weight, preferred_element_type=jnp.float32
    ).astype(jnp.bfloat16)
    grad_act = jnp.einsum("cd,fd->cf", grad_in, down_weight, preferred_element_type=jnp.float32)
    unused, gelu_pull = jax.vjp(gelu_exact, upward)
    grad_up_b = gelu_pull(grad_act)[0].astype(jnp.bfloat16)
    grad_heads = grad_att_b.reshape(span_rows, heads_loc, HEAD_DIM)
    delta_t = jnp.sum(grad_heads.astype(jnp.float32) * attended, axis=-1).T

    def both_step(query_grad, block_data):
        key_block, value_block, code_block, pos_block = block_data
        probs_low, score_grad = grad_scores(
            queries,
            grad_heads,
            query_pos,
            seg_own,
            log_total,
            delta_t,
            key_block,
            value_block,
            pos_block,
            code_block,
        )
        query_grad = query_grad + jnp.einsum(
            "hqk,khd->qhd", score_grad, key_block, preferred_element_type=jnp.float32
        )
        key_grad = jnp.einsum(
            "hqk,qhd->khd", score_grad, queries, preferred_element_type=jnp.float32
        )
        value_grad = jnp.einsum(
            "hqk,qhd->khd", probs_low, grad_heads, preferred_element_type=jnp.float32
        )
        return (query_grad, (key_grad, value_grad))

    query_grad, stacked = lax.scan(
        both_step, zero_heads, (key_blocks, value_blocks, code_blocks, pos_blocks)
    )
    key_grad, value_grad = (
        lax.psum_scatter(
            stacked[0].reshape(seq_len, local_width).astype(jnp.bfloat16),
            "ctx",
            scatter_dimension=0,
            tiled=True,
        ).astype(jnp.float32),
        lax.psum_scatter(
            stacked[1].reshape(seq_len, local_width).astype(jnp.bfloat16),
            "ctx",
            scatter_dimension=0,
            tiled=True,
        ).astype(jnp.float32),
    )
    key_grad = key_grad.reshape(span_rows, heads_loc, HEAD_DIM)
    value_grad = value_grad.reshape(span_rows, heads_loc, HEAD_DIM)
    query_pre = rotate(query_grad * score_scale, cosine_tab, -sine_tab)
    key_pre = rotate(key_grad * score_scale, cosine_tab, -sine_tab)
    grad_proj = (
        jnp.stack([query_pre, key_pre, value_grad], axis=1)
        .reshape(span_rows, 3, local_width)
        .astype(jnp.bfloat16)
    )
    grad_qkv_w = jnp.einsum("cd,ctf->dtf", normed1, grad_proj, preferred_element_type=jnp.float32)
    grad_qkv_b = jnp.sum(grad_proj.astype(jnp.float32), axis=0)
    grad_out_w = jnp.einsum("cf,cd->fd", attended_b, grad_in, preferred_element_type=jnp.float32)
    grad_bias_shared = jnp.sum(grad_in.astype(jnp.float32), axis=0)
    grad_up_w = jnp.einsum("cd,cf->df", normed2, grad_up_b, preferred_element_type=jnp.float32)
    grad_up_bias = jnp.sum(grad_up_b.astype(jnp.float32), axis=0)
    grad_down_w = jnp.einsum("cf,cd->fd", activated, grad_in, preferred_element_type=jnp.float32)
    norm_in1 = jnp.einsum("ctf,dtf->cd", grad_proj, qkv_weight, preferred_element_type=jnp.float32)
    norm_in2 = jnp.einsum("cf,df->cd", grad_up_b, up_weight, preferred_element_type=jnp.float32)
    full_one, full_two = (
        lax.psum(norm_in1.astype(jnp.bfloat16), "tensor").astype(jnp.float32),
        lax.psum(norm_in2.astype(jnp.bfloat16), "tensor").astype(jnp.float32),
    )
    input_one, gain_one, shift_one = norm_back(inputs, norm1_gain, norm1_shift, full_one)
    input_two, gain_two, shift_two = norm_back(inputs, norm2_gain, norm2_shift, full_two)
    input_grad = (grad_in.astype(jnp.float32) + input_one + input_two).astype(jnp.bfloat16)
    summed_grads = lax.psum(
        (
            gain_one,
            shift_one,
            gain_two,
            shift_two,
            grad_qkv_w,
            grad_qkv_b,
            grad_out_w,
            grad_bias_shared,
            grad_up_w,
            grad_up_bias,
            grad_down_w,
        ),
        ("dp", "ctx"),
    )
    return (
        block_output[None],
        input_grad[None],
        summed_grads[0],
        summed_grads[1],
        summed_grads[2],
        summed_grads[3],
        summed_grads[4],
        summed_grads[5],
        summed_grads[6],
        summed_grads[7],
        summed_grads[8],
        summed_grads[9],
        summed_grads[10],
        summed_grads[7],
    )


def solution(mesh):
    return jax.shard_map(
        on_device,
        mesh=mesh,
        in_specs=(
            P("dp", "ctx", None),
            P("dp", "ctx"),
            P("dp", "ctx"),
            P("dp", "ctx", None),
            P(),
            P(),
            P(),
            P(),
            P(None, None, "tensor"),
            P(None, "tensor"),
            P("tensor", None),
            P(),
            P(None, "tensor"),
            P("tensor"),
            P("tensor", None),
            P(),
        ),
        out_specs=(
            P("dp", "ctx", None),
            P("dp", "ctx", None),
            P(),
            P(),
            P(),
            P(),
            P(None, None, "tensor"),
            P(None, "tensor"),
            P("tensor", None),
            P(),
            P(None, "tensor"),
            P("tensor"),
            P("tensor", None),
            P(),
        ),
        check_vma=False,
    )
```

profile of v0, /device:TPU:0, one launch (start us, length us, event | category | flops | bytes accessed | tf_op | source)
XLA Modules:
  0.0 633.0 jit_solution(5543811374188564276)
XLA Ops:
  7.3 1.6 convert_reduce_fusion.3
  8.9 1.6 fusion.74
  10.6 2.6 convolution_add_fusion
  13.3 1.0 slice_bitcast_fusion
  14.4 9.9 %all_gather.9 = bf16[1024,256]{0,1:T(8,128)(2,1)S(1)} all-gather(bf16[512,256]{0,1:T(8,128)(2,1)S(1)} %bitcast.309), channel_id=1, replica_groups=mesh['dp'=4,'ctx'=2,'tensor'=4] {'ctx'}, dimensions={0}, use_global_device_ids=true | all-gather | bytes 786432 | tf_op jit(solution)/shard_map/all_gather | solution.py:122
  25.6 4.3 all-gather
  31.1 1.0 slice.107
  32.1 1.7 slice.106
  35.0 7.2 %all_gather.11 = bf16[1024,256]{0,1:T(8,128)(2,1)S(1)} all-gather(bf16[512,256]{0,1:T(8,128)(2,1)S(1)} %bitcast.310), channel_id=1, replica_groups=mesh['dp'=4,'ctx'=2,'tensor'=4] {'ctx'}, dimensions={0}, use_global_device_ids=true | all-gather | bytes 786432 | tf_op jit(solution)/shard_map/all_gather | solution.py:121
  42.6 1.1 pad_maximum_fusion.2
  43.8 1.1 copy.47
  44.9 13.1 %while.39 = (s32[]{:T(128)}, f32[4,512]{1,0:T(4,128)S(1)}, f32[4,512]{1,0:T(4,128)S(1)}, s32[2,512]{1,0:T(2,128)S(1)}, s32[2,512]{1,0:T(2,128)S(1)}, /*index=5*/...) while((s32[]{:T(128)}, f32[4,512]{1,0:T(4,128)S(1)}, ...), condition=%wide.region_5.6_spmd.clone, body=%wide.region_2.5_spmd.clone.sunk | while | flops 143927808 | bytes 9824396 | solution.py:146
  45.3 2.9 fusion.158
  48.2 3.2 select_reduce_fusion.2
  51.8 2.9 fusion.158
  54.7 3.2 select_reduce_fusion.2
  58.0 16.0 %while.40 = (s32[]{:T(128)}, f32[512,4,64]{0,2,1:T(8,128)}, bf16[2,512,4,64]{1,3,2,0:T(8,128)(2,1)}, s32[2,512]{1,0:T(2,128)S(1)}, s32[2,512]{1,0:T(2,128)S(1)},...) while((s32[]{:T(128)}, f32[512,4,64]{0,2,1:T(8,128)}, ...), condition=%wide.region_7.8_spmd.clone, body=%wide.region_6.7_spmd.clone.sunk | while | flops 275251712 | bytes 3958935 | solution.py:164
  58.0 1.0 or_and_fusion.7
  59.1 1.6 constant_dynamic-slice_fusion.13
  60.7 1.3 copy.79
  61.9 4.0 fusion.163
  66.0 1.0 or_and_fusion.7
  67.0 1.6 constant_dynamic-slice_fusion.13
  68.6 1.3 copy.79
  69.9 4.2 fusion.163
  74.0 3.0 multiply_reduce_fusion
  77.0 22.3 %while.41 = (s32[]{:T(128)}, f32[512,4,64]{0,2,1:T(8,128)S(1)}, bf16[2,512,4,64]{1,3,2,0:T(8,128)(2,1)}, bf16[2,512,4,64]{1,3,2,0:T(8,128)(2,1)}, bf16[2,512,4,6...) while((s32[]{:T(128)}, f32[512,4,64]{0,2,1:T(8,128)S(1)}, ...), condition=%wide.region_11.12_spmd.clone, body=%wide.region_10.11_spmd.clone.sunk | while | flops 685244928 | bytes 69773672 | solution.py:211
  78.2 3.0 fusion.175
  81.2 2.2 fusion.176
  83.5 1.5 fusion.177
  84.9 3.2 fusion.178
  89.3 3.0 fusion.175
  92.3 2.2 fusion.176
  94.6 1.5 fusion.177
  96.1 3.3 fusion.178
  99.3 1.8 copy.50
  102.3 2.3 copy.63
  104.6 2.7 reshape.498
  107.5 5.6 multiply_convert_fusion
  113.1 1.3 fusion.113
  114.6 1.4 add_convert_fusion.1
  116.0 2.0 convert_reduce_fusion.4
  119.7 2.3 convolution_convert_fusion
  122.0 1.0 convert_multiply_fusion.4
  123.9 1.8 pad_maximum_fusion.3
  125.7 1.8 copy.54
  127.5 1.8 copy.53
  129.3 6.4 %reduce-scatter.5.cloned.1.call-done = bf16[512,256]{1,0:T(8,128)(2,1)} async-done(((bf16[1024,256]{1,0:T(8,128)(2,1)}), bf16[512,256]{1,0:T(8,128)(2,1)}) %reduce-scatter.5.cloned.1.call-update) | async-done | bytes 262160 | tf_op jit(solution)/shard_map/reduce_scatter | solution.py:221
  135.7 3.6 bitcast_convert_fusion
  139.7 2.8 fusion.95
  142.5 3.3 fusion.93
  145.8 3.5 fusion.108
  149.3 2.9 fusion.105
  152.9 1.2 convert_reduce_fusion.5
  154.0 54.3 %all-reduce.8.cloned.1.call-done = (bf16[512,1024]{1,0:T(8,128)(2,1)}, bf16[512,1024]{1,0:T(8,128)(2,1)}, bf16[512,1024]{1,0:T(8,128)(2,1)}) async-done(((bf16[512,1024]{1,0:T(8,128)(2,1)}, bf16[512,1024]{1,0:T(8,128)(2,1)}, bf16[512,1024]{1,0:T(8,128)(2,1)}), (bf16[512,1024]{1,0:T(8,128)(2,1)}, bf16[512,1024]{1,0:T(8,128)(2,1)}, bf16[512,1024]{1,0:T(8,128)(2,1)})) %all-reduce.8.cloned.1.call-update) | async-done | bytes 3145744 | tf_op jit(solution)/shard_map/psum | solution.py:174
  208.3 2.7 fusion.75
  211.0 2.2 fusion.83
  213.2 2.9 convert_reduce_fusion.2
  216.2 39.6 %all-reduce = (f32[1024]{0:T(1024)}, f32[1024]{0:T(1024)}, f32[1024]{0:T(1024)}, f32[1024]{0:T(1024)}, f32[3,256]{1,0:T(4,128)}, /*index=5*/f32[1024]{0:T(1024)S(1)}, f32[1024]{0:T(1024)}) all-reduce(f32[1024]{0:T(1024)S(1)} %get-tuple-element.359, ...), channel_id=1, replica_groups=mesh['dp'=4,'ctx'=2,'tensor'=4] {'dp','ctx'}, use_global_device_ids=true, to_apply=%region_21.22 | all-reduce | flops 6912 | bytes 55296 | tf_op jit(solution)/shard_map/psum | solution.py:253
  255.8 359.5 %all-reduce.6.cloned.1.call-done = (f32[1024,3,256]{2,0,1:T(8,128)}, f32[256,1024]{1,0:T(8,128)}, f32[1024,1024]{1,0:T(8,128)}, f32[1024,1024]{1,0:T(8,128)}) async-done(((f32[1024,3,256]{2,0,1:T(8,128)}, f32[256,1024]{1,0:T(8,128)}, f32[1024,1024]{1,0:T(8,128)}, f32[1024,1024]{1,0:T(8,128)}), (f32[1024,3,256]{2,0,1:T(8,128)}, f32[256,1024]{1,0:T(8,128)}, f32[1024,1024]{1,0:T(8,128)}, ...) | async-done | bytes 12582928 | tf_op jit(solution)/shard_map/psum | solution.py:253
  615.9 3.9 copy.118
  620.8 2.1 copy.120
  622.9 1.6 copy-done.16
  624.5 2.0 copy.121
  (167 shorter events, 13.8 us)
Async XLA Ops:
  7.2 100.3 %copy-start = (bf16[1024,1024]{1,0:T(8,128)(2,1)S(1)}, bf16[1024,1024]{1,0:T(8,128)(2,1)}, u32[]{:S(2)}) copy-start(bf16[1024,1024]{1,0:T(8,128)(2,1)} %param.34) | copy-start | bytes 6291460
  7.2 3.4 copy-start.4
  7.2 3.3 copy-start.38
  7.2 3.3 copy-start.41
  7.2 3.3 copy-start.31
  7.2 114.7 %reduce-scatter.3.cloned.1.call-start = ((), (), s32[]{:S(2)}) async-start(), calls=%async_computation.2 | async-start | bytes 786432 | tf_op jit(solution)/shard_map/reduce_scatter | solution.py:215
  13.3 12.3 %copy-start.27 = (s32[1,512]{1,0:T(1,128)S(1)}, s32[1,512]{1,0:T(1,128)}, u32[]{:S(2)}) copy-start(s32[1,512]{1,0:T(1,128)} %param.23) | copy-start | bytes 6148
  13.3 12.3 %copy-start.36 = (s32[1,512]{1,0:T(1,128)S(1)}, s32[1,512]{1,0:T(1,128)}, u32[]{:S(2)}) copy-start(s32[1,512]{1,0:T(1,128)} %param.24) | copy-start | bytes 6148
  42.6 2.3 copy-start.6
  74.0 3.0 copy-start.7
  77.0 1.2 copy-start.28
  77.0 1.2 copy-start.30
  77.8 3.4 copy-start.2
  78.2 3.0 copy-start.15
  81.2 2.3 copy-start.1
  81.2 3.7 copy-start.3
  88.2 1.1 copy-start.28
  88.2 1.1 copy-start.30
  88.9 3.4 copy-start.2
  89.3 3.0 copy-start.15
  92.3 2.3 copy-start.1
  92.3 3.7 copy-start.3
  99.3 2.6 copy-start.8
  102.0 5.5 copy-start.5
  102.0 5.5 copy-start.32
  102.0 5.5 copy-start.39
  102.0 5.5 copy-start.40
  102.0 33.7 %reduce-scatter.5.cloned.1.call-start = ((), (), s32[]{:S(2)}) async-start(), calls=%async_computation.3 | async-start | bytes 786432 | tf_op jit(solution)/shard_map/reduce_scatter | solution.py:221
  107.4 101.0 %all-reduce.8.cloned.1.call-start = ((), (), s32[]{:S(2)}) async-start(), calls=%async_computation.5 | async-start | bytes 6291456 | tf_op jit(solution)/shard_map/psum | solution.py:174
  107.5 5.6 copy-start.37
  113.1 1.3 copy-start.20
  113.1 1.3 copy-start.18
  113.1 1.5 copy-start.19
  114.4 1.6 copy-start.10
  116.0 2.0 copy-start.9
  118.0 1.7 copy-start.42
  118.1 0.9 copy-start.22
  139.4 475.9 %all-reduce.6.cloned.1.call-start = ((), (), s32[]{:S(2)}) async-start(), calls=%async_computation.4 | async-start | bytes 25165824 | tf_op jit(solution)/shard_map/psum | solution.py:253
  139.7 2.8 copy-start.11
  139.7 2.8 copy-start.21
  142.5 3.3 copy-start.43
  145.8 3.5 copy-start.23
  145.8 3.5 copy-start.24
  145.8 3.5 copy-start.29
  152.2 0.7 copy-start.33
  152.2 0.7 copy-start.34
  208.3 2.7 copy-start.13
  208.3 2.7 copy-start.14
  211.0 2.2 copy-start.12
  211.0 2.2 copy-start.26
  255.8 364.0 %copy-start.35 = (f32[1024]{0:T(1024)}, f32[1024]{0:T(1024)S(1)}, u32[]{:S(2)}) copy-start(f32[1024]{0:T(1024)S(1)} %get-tuple-element.855) | copy-start | bytes 12292
  615.9 3.9 copy-start.25
  615.9 4.9 copy-start.17
  620.8 3.7 copy-start.16
Sparse Core Ops, SparseCore 0:
  102.1 16.0 reduce-scatter.2
  121.1 14.5 reduce-scatter.4
  139.5 68.8 all-reduce.7
  214.1 401.1 all-reduce.5
where the time goes:
time: 634 us; the launch traced here: 633 us
  waiting for transfers between devices  420 us (66%)
  matrix products  69.7 us (11%)
  blocking collectives  61.1 us (10%)
  local copies, waits for them, and re-layouts  38 us (6%)
  other arithmetic  28.7 us (5%)
  between operations  14.3 us (2%)
    psum x1, waiting for transfers between devices, on_device(): lax.psum((gain_one, shift_one, gain_two, shift_two, grad_qkv_w, grad_qkv_...  359 us
    psum x1, waiting for transfers between devices, on_device(): lax.psum(partial_sum.astype(jnp.bfloat16), 'tensor').astype(jnp.float32)  54.3 us
    psum x1, blocking collectives, on_device(): lax.psum((gain_one, shift_one, gain_two, shift_two, grad_qkv_w, grad_qkv_...  39.6 us
    unnamed x85, local copies, waits for them, and re-layouts  15.9 us
  transfers between devices with their start and end apart: 4, of which 3 were waited for; matrix products, arithmetic and copies ran while one was open for 7% of the time, Pallas kernels for 0%

commit v1 on v0

--- a/solution.py
+++ b/solution.py
@@ -1,7 +1,11 @@
+import functools
+
 import jax
 import jax.numpy as jnp
 from jax import lax
 from jax.sharding import PartitionSpec as P
+from jax.experimental import pallas as pl
+from jax.experimental.pallas import tpu as pltpu
 
 HEAD_DIM = 64
 ROT = 16
@@ -284,9 +288,770 @@
     )
 
 
+F32 = jnp.float32
+BF16 = jnp.bfloat16
+NEG = -1e30
+MIB = 1 << 20
+CHUNKS = 4
+
+
+def params(mib=40):
+    return pltpu.CompilerParams(vmem_limit_bytes=mib * MIB)
+
+
+def cost(flops, moved):
+    return pl.CostEstimate(flops=int(flops), bytes_accessed=int(moved), transcendentals=0)
+
+
+def dot(a, b):
+    return lax.dot_general(a, b, (((1,), (0,)), ((), ())), preferred_element_type=F32)
+
+
+def dot_nt(a, b):
+    return lax.dot_general(a, b, (((1,), (1,)), ((), ())), preferred_element_type=F32)
+
+
+def dot_tn(a, b):
+    return lax.dot_general(a, b, (((0,), (0,)), ((), ())), preferred_element_type=F32)
+
+
+def whole(shape):
+    return pl.BlockSpec(shape, lambda *_: (0,) * len(shape))
+
+
+def struct(shape, dtype):
+    return jax.ShapeDtypeStruct(shape, dtype)
+
+
+def standard(values):
+    centre = jnp.mean(values, axis=-1, keepdims=True)
+    centred = values - centre
+    spread = jnp.mean(centred * centred, axis=-1, keepdims=True)
+    inverse = lax.rsqrt(spread + 1e-05)
+    return centred * inverse, inverse
+
+
+def ctx_flag():
+    return lax.axis_index("ctx")
+
+
+def inner_flag():
+    z = lax.axis_index("dp")
+    return ((z == 1) | (z == 2)).astype(jnp.int32)
+
+
+def core_flag():
+    return lax.axis_index("tensor") % 2
+
+
+def halves(flag, values):
+    rows = values.shape[0] // 2
+    top, low = values[:rows], values[rows:]
+    return jnp.where(flag == 0, top, low), jnp.where(flag == 0, low, top)
+
+
+def resident():
+    return pl.BlockSpec(memory_space=pltpu.VMEM)
+
+
+def small(kernel, arrays, outs, name, mib=16, flops=0):
+    return pl.pallas_call(
+        kernel,
+        in_specs=[resident()] * len(arrays),
+        out_specs=[resident()] * len(outs),
+        out_shape=list(outs),
+        compiler_params=params(mib),
+        cost_estimate=cost(flops, 1024),
+        name=name,
+    )(*arrays)
+
+
+def fetched(kernel, arrays, outs, name, flops, later=0, scratch=(), mib=48):
+    now = len(arrays) - later
+    return pl.pallas_call(
+        kernel,
+        grid=(1,),
+        in_specs=[whole(a.shape) for a in arrays[:now]] + [pl.BlockSpec(memory_space=pl.ANY)] * later,
+        out_specs=[whole(o.shape) for o in outs],
+        out_shape=list(outs),
+        scratch_shapes=list(scratch),
+        compiler_params=params(mib),
+        cost_estimate=cost(flops, 1024),
+        name=name,
+    )(*arrays)
+
+
+def add_kernel(a_ref, b_ref, o_ref):
+    o_ref[...] = (a_ref[...].astype(F32) + b_ref[...].astype(F32)).astype(o_ref.dtype)
+
+
+def add(a, b):
+    return small(add_kernel, (a, b), [struct(a.shape, a.dtype)], "add")[0]
+
+
+def choose_kernel(a_ref, b_ref, o_ref):
+    o_ref[...] = jnp.where(inner_flag() == 1, a_ref[...], b_ref[...])
+
+
+def choose(a, b):
+    return small(choose_kernel, (a, b), [struct(a.shape, a.dtype)], "choose")[0]
+
+
+def place_halves_kernel(mine_ref, other_ref, *refs):
+    o_ref = refs[-1]
+    rows = o_ref.shape[0]
+    o_ref[...] = jnp.where(ctx_flag() == pl.program_id(0), mine_ref[:rows], other_ref[:rows]).astype(F32)
+
+
+def turn_lanes(table):
+    half, lanes = ROT // 2, 2 * HEAD_DIM
+    row = lax.broadcasted_iota(jnp.int32, (2 * half, lanes), 0)
+    lane = lax.broadcasted_iota(jnp.int32, (2 * half, lanes), 1) % HEAD_DIM
+    turned = (lane < ROT) & (lane % half == row % half)
+    pick_cos = jnp.where(turned & (row < half), 1.0, 0.0)
+    pick_sin = jnp.where(turned & (row >= half), jnp.where(lane < half, -1.0, 1.0), 0.0)
+    exact = functools.partial(
+        lax.dot_general, dimension_numbers=(((0,), (0,)), ((), ())), precision=lax.Precision.HIGHEST,
+        preferred_element_type=F32,
+    )
+    return exact(table, pick_cos) + jnp.where(lane[0:1] < ROT, 0.0, 1.0), exact(table, pick_sin)
+
+
+def partner(values):
+    lane = lax.broadcasted_iota(jnp.int32, values.shape, 1) % HEAD_DIM
+    half = ROT // 2
+    width = values.shape[1]
+    return jnp.where(lane < half, pltpu.roll(values, width - half, 1), pltpu.roll(values, half, 1))
+
+
+def turn(values, cosine, sine):
+    return values * cosine + partner(values) * sine
+
+
+def activation(up):
+    phi = 0.5 * (1.0 + lax.erf(up * 0.7071067811865476))
+    return (up * phi).astype(BF16), phi + up * (0.3989422804014327 * jnp.exp(up * up * -0.5))
+
+
+def own_kernel(x_ref, dy_ref, up_ref, down_ref, pack_ref, n1_ref, n2_ref, act_ref, gu_ref, gub_ref):
+    step = pl.program_id(0)
+
+    @pl.when(step == 0)
+    def _():
+        xhat, _ = standard(x_ref[...].astype(F32))
+        n1_ref[...] = (xhat * pack_ref[0:1] + pack_ref[1:2]).astype(BF16)
+        n2_ref[...] = (xhat * pack_ref[2:3] + pack_ref[3:4]).astype(BF16)
+
+    size = act_ref.shape[1]
+    dy = dy_ref[...]
+    act, slope = activation(dot(n2_ref[...], up_ref[...]) + pack_ref[4:5, pl.ds(pl.multiple_of(step * size, size), size)])
+    grad = (dot_nt(dy, down_ref[...]) * slope).astype(BF16)
+    act_ref[...] = act
+    gu_ref[...] = grad
+    gub_ref[...] = jnp.sum(grad.astype(F32), axis=0, keepdims=True)
+
+
+def own_call(x, dy, up_w, down_w, pack):
+    rows, width = x.shape
+    hidden = up_w.shape[1]
+    size = hidden // CHUNKS
+    cols = pl.BlockSpec((rows, size), lambda i: (0, i))
+    return pl.pallas_call(
+        own_kernel,
+        grid=(CHUNKS,),
+        in_specs=[
+            whole(x.shape), whole(x.shape),
+            pl.BlockSpec((width, size), lambda i: (0, i)), pl.BlockSpec((size, width), lambda i: (i, 0)),
+            whole(pack.shape),
+        ],
+        out_specs=[whole(x.shape)] * 2 + [cols, cols, pl.BlockSpec((1, size), lambda i: (0, i))],
+        out_shape=[struct(x.shape, BF16)] * 2 + [struct((rows, hidden), BF16)] * 2 + [struct((1, hidden), F32)],
+        compiler_params=params(48),
+        cost_estimate=cost(8e9, 1024),
+        name="own",
+    )(x, dy, up_w, down_w, pack)
+
+
+def half_at(flag, size):
+    return pl.ds(pl.multiple_of(flag * size, size), size)
+
+
+def project(n1, span, w_ref, b_ref, table_ref, q_ref, k_ref, v_ref):
+    lanes = q_ref.shape[1]
+    mine = half_at(ctx_flag(), lanes)
+    cosine, sine = turn_lanes(table_ref[:, half_at(span, n1.shape[0])])
+    q_ref[...] = turn(dot(n1, w_ref[0, :, mine]) + b_ref[0:1, mine], cosine, sine).astype(BF16)
+    k_ref[...] = turn(dot(n1, w_ref[1, :, mine]) + b_ref[1:2, mine], cosine, sine).astype(BF16)
+    v_ref[...] = (dot(n1, w_ref[2, :, mine]) + b_ref[2:3, mine]).astype(BF16)
+
+
+def pieces(near_ref, pair_ref, step):
+    core, size = core_flag(), near_ref.shape[0]
+    step(half_at(core, size), near_ref[...])
+    step(half_at(1 - core, size), pair_ref[...])
+
+
+def other_kernel(near_ref, pair_ref, n1_o_ref, pack_ref, w_ref, b_ref, table_ref, up_ref,
+                 n1_ref, n2_ref, q_o_ref, k_o_ref, v_o_ref, q_ref, k_ref, v_ref, act_ref, slope_ref):
+    def norm(at, x):
+        xhat, _ = standard(x.astype(F32))
+        n1_ref[at] = (xhat * pack_ref[0:1] + pack_ref[1:2]).astype(BF16)
+        n2_ref[at] = (xhat * pack_ref[2:3] + pack_ref[3:4]).astype(BF16)
+
+    pieces(near_ref, pair_ref, norm)
+    project(n1_o_ref[...], ctx_flag(), w_ref, b_ref, table_ref, q_o_ref, k_o_ref, v_o_ref)
+    project(n1_ref[...], 1 - ctx_flag(), w_ref, b_ref, table_ref, q_ref, k_ref, v_ref)
+    size = slope_ref.shape[1] // 2
+    for j in range(2):
+        mine = pl.ds(pl.multiple_of(ctx_flag() * 2 * size + j * size, size), size)
+        at = slice(j * size, (j + 1) * size)
+        act_ref[:, at], slope_ref[:, at] = activation(dot(n2_ref[...], up_ref[:, mine]) + pack_ref[4:5, mine])
+
+
+def other_call(near, pair, n1, pack, w3, bias, table, up_w):
+    rows, width = 2 * near.shape[0], near.shape[1]
+    half = up_w.shape[1] // 2
+    head = struct((rows, 2 * HEAD_DIM), BF16)
+    outs = [struct((rows, width), BF16)] * 2 + [head] * 6 + [struct((rows, half), BF16), struct((rows, half), F32)]
+    return fetched(other_kernel, (near, pair, n1, pack, w3, bias, table, up_w), outs, "other", 5e9)
+
+
+EXTRA = 16
+
+
+def unit_struct(rows, cols):
+    return struct((rows + EXTRA, cols), BF16)
+
+
+def fill(ref, *values):
+    rows = ref.shape[0] - EXTRA
+    at = 0
+    for value in values:
+        for first in range(0, value.shape[0], rows):
+            ref[:rows, at : at + value.shape[1]] = value[first : first + rows]
+            at += value.shape[1]
+    ref[rows:] = jnp.zeros((EXTRA, ref.shape[1]), ref.dtype)
+
+
+def unfold(value, lanes, index, count):
+    rows = value.shape[0] - EXTRA
+    folds = [value[:rows, (index * count + i) * lanes : (index * count + i + 1) * lanes] for i in range(count)]
+    return jnp.concatenate(folds, axis=0)
+
+
+def weights_kernel(near_ref, pair_ref, act_o_ref, dy_o_ref, act_ref, slope_ref, down_ref, ow_ref,
+                   dy_ref, gu_ref, ga_ref, *grad_refs):
+    hidden = slope_ref.shape[1]
+
+    def put(at, dy):
+        dy_ref[at] = dy
+
+    pieces(near_ref, pair_ref, put)
+    dy, dy_o = dy_ref[...], dy_o_ref[...]
+    rows, lanes = dy.shape[0], ga_ref.shape[1]
+    act_o, act = act_o_ref[:, half_at(ctx_flag(), hidden)], act_ref[...]
+    for i, ref in enumerate(grad_refs):
+        cols = slice(i * ref.shape[1], (i + 1) * ref.shape[1])
+        fill(ref, (dot_tn(act_o, dy_o[:, cols]) + dot_tn(act, dy[:, cols])).astype(BF16))
+    gu_ref[...] = (dot_nt(dy, down_ref[half_at(ctx_flag(), hidden)]) * slope_ref[...]).astype(BF16)
+    out_w = ow_ref[half_at(ctx_flag(), lanes)]
+    ga_ref[half_at(ctx_flag(), rows)] = dot_nt(dy_o, out_w).astype(BF16)
+    ga_ref[half_at(1 - ctx_flag(), rows)] = dot_nt(dy, out_w).astype(BF16)
+
+
+def weights_call(near, pair, act_o, dy_o, act, slope, down_w, out_w):
+    rows, width = dy_o.shape
+    hidden = slope.shape[1]
+    outs = [struct((rows, width), BF16), struct((rows, hidden), BF16), struct((2 * rows, 2 * HEAD_DIM), BF16)]
+    outs += [unit_struct(hidden, width // 2)] * 2
+    arrays = (near, pair, act_o, dy_o, act, slope, down_w, out_w)
+    return fetched(weights_kernel, arrays, outs, "weights", 4e9)
+
+
+def in_order(own, other, axis=0):
+    first = ctx_flag() == 0
+    return jnp.concatenate([jnp.where(first, own, other), jnp.where(first, other, own)], axis=axis)
+
+
+def attend_kernel(q_o_ref, k_o_ref, v_o_ref, q_x_ref, k_x_ref, v_x_ref, ga_ref, ids_o_ref, ids_x_ref, table_ref,
+                  n1_o_hbm, n1_x_hbm, dy_o_hbm, dy_x_hbm, n2_o_hbm, n2_x_hbm, gu_o_hbm, gu_x_hbm,
+                  keep_ref, send_ref, qk_grad_ref, vo_grad_ref, *refs):
+    up_refs, refs = refs[:2], refs[2:]
+    q_ref, k_ref, v_ref, dk_ref, dv_ref, att_ref, gp_ref, *held, sems = refs
+    n1_o_ref, n1_x_ref, dy_o_ref, dy_x_ref, n2_o_ref, n2_x_ref, gu_o_ref, gu_x_ref = held
+    rows, lanes = q_ref.shape
+    span = rows // 2
+    mine, theirs = half_at(ctx_flag(), span), half_at(1 - ctx_flag(), span)
+    copies = [
+        pltpu.make_async_copy(src, dst, sems.at[i])
+        for i, (src, dst) in enumerate((
+            (n1_o_hbm, n1_o_ref), (n1_x_hbm, n1_x_ref), (dy_o_hbm, dy_o_ref), (dy_x_hbm, dy_x_ref),
+            (n2_o_hbm, n2_o_ref), (n2_x_hbm, n2_x_ref),
+            (gu_o_hbm.at[:, half_at(ctx_flag(), gu_x_ref.shape[1])], gu_o_ref), (gu_x_hbm, gu_x_ref),
+        ))
+    ]
+    for copy in copies:
+        copy.start()
+    cosine, sine = turn_lanes(table_ref[...])
+    step = 256
+    zero = jnp.zeros((), BF16)
+    scale = HEAD_DIM ** (-0.5)
+    q_ref[...] = in_order(q_o_ref[...], q_x_ref[...]) * jnp.asarray(scale, BF16)
+    k_ref[...], v_ref[...] = in_order(k_o_ref[...], k_x_ref[...]), in_order(v_o_ref[...], v_x_ref[...])
+    dk_ref[...] = jnp.zeros(dk_ref.shape, F32)
+    dv_ref[...] = jnp.zeros(dv_ref.shape, F32)
+    ids = in_order(ids_o_ref[...], ids_x_ref[...], axis=1)
+    code = jnp.where(ids[1:2] == 1, ids[0:1], -1).astype(F32)
+    doc = jnp.broadcast_to(ids[0:1].astype(F32), (8, rows)).T[:, 0:1]
+    lane = lax.broadcasted_iota(jnp.int32, (1, lanes), 1)
+    heads = [(lane // HEAD_DIM) == h for h in range(lanes // HEAD_DIM)]
+    for i in range(rows // step):
+        at, upto = slice(i * step, (i + 1) * step), (i + 1) * step
+        k, v = k_ref[:upto], v_ref[:upto]
+        row = lax.broadcasted_iota(jnp.int32, (step, upto), 0) + i * step
+        col = lax.broadcasted_iota(jnp.int32, (step, upto), 1)
+        seen = ((col <= row) & (code[:, :upto] == doc[at])) | (col == row)
+        bias = jnp.where(seen, 0.0, NEG)
+        q, ga = q_ref[at], ga_ref[at]
+        sums = None
+        for head in heads:
+            qh, gh = jnp.where(head, q, zero), jnp.where(head, ga, zero)
+            scores = dot_nt(qh, k) + bias
+            e = jnp.exp(scores - jnp.max(scores, axis=1, keepdims=True))
+            p = e * (1.0 / jnp.sum(e, axis=1, keepdims=True))
+            low = p.astype(BF16)
+            att = jnp.where(head, dot(low, v), 0.0)
+            delta = jnp.sum(att * gh.astype(F32), axis=1, keepdims=True)
+            g = (p * (dot_nt(gh, v) - delta)).astype(BF16)
+            terms = att, jnp.where(head, dot(g, k), 0.0), dot_tn(g, qh), dot_tn(low, gh)
+            sums = terms if sums is None else [a + b for a, b in zip(sums, terms)]
+        att_ref[at] = sums[0].astype(BF16)
+        gp_ref[0, at] = turn(sums[1] * scale, cosine[at], -sine[at]).astype(BF16)
+        dk_ref[:upto] += sums[2]
+        dv_ref[:upto] += sums[3]
+    gp_ref[1] = turn(dk_ref[...], cosine, -sine).astype(BF16)
+    gp_ref[2] = dv_ref[...].astype(BF16)
+    keep_ref[0], send_ref[0] = att_ref[mine], att_ref[theirs]
+    for t in range(3):
+        keep_ref[t + 1], send_ref[t + 1] = gp_ref[t, mine], gp_ref[t, theirs]
+    for copy in copies:
+        copy.wait()
+    q_grad, k_grad, v_grad = [
+        (dot_tn(n1_o_ref[...], keep_ref[t]) + dot_tn(n1_x_ref[...], send_ref[t])).astype(BF16) for t in (1, 2, 3)
+    ]
+    o_grad = (dot_tn(dy_o_ref[...], keep_ref[0]) + dot_tn(dy_x_ref[...], send_ref[0])).astype(BF16)
+    fill(qk_grad_ref, q_grad, k_grad)
+    fill(vo_grad_ref, v_grad, o_grad)
+    gu_o, gu_x = gu_o_ref[...], gu_x_ref[...]
+    for i, ref in enumerate(up_refs):
+        at = slice(i * (ref.shape[0] - EXTRA), (i + 1) * (ref.shape[0] - EXTRA))
+        fill(ref, (dot_tn(n2_o_ref[:, at], gu_o) + dot_tn(n2_x_ref[:, at], gu_x)).astype(BF16))
+
+
+def attend_call(own, other, ga, ids, ids_x, table, *later):
+    arrays = (*own, *other, ga, ids, ids_x, table, *later)
+    rows, lanes = ga.shape
+    span, width = later[0].shape
+    hidden = later[-1].shape[1]
+    outs = [struct((4, span, lanes), BF16)] * 2 + [unit_struct(width // 2, 4 * lanes)] * 2 + [unit_struct(width // 2, hidden)] * 2
+    scratch = [pltpu.VMEM((rows, lanes), BF16)] * 3 + [pltpu.VMEM((rows, lanes), F32)] * 2
+    scratch += [pltpu.VMEM((rows, lanes), BF16), pltpu.VMEM((3, rows, lanes), BF16)]
+    scratch += [pltpu.VMEM((span, width), BF16)] * 6 + [pltpu.VMEM((span, hidden), BF16)] * 2
+    scratch.append(pltpu.SemaphoreType.DMA((len(later),)))
+    return fetched(attend_kernel, arrays, outs, "attend", 1024, len(later), scratch)
+
+
+def sums_kernel(mine_ref, recv_ref, act_ref, gu_ref, dy_ref, x_ref, pack_ref, w_ref, ow_ref, up_ref, down_ref,
+                gub_ref, keep_ref, send_ref, vec_ref, gb_ref):
+    lanes = mine_ref.shape[2]
+    heads = [(mine_ref, half_at(ctx_flag(), lanes)), (recv_ref, half_at(1 - ctx_flag(), lanes))]
+    out = dot(act_ref[...], down_ref[...])
+    two = dot_nt(gu_ref[...], up_ref[...])
+    one = None
+    for ref, at in heads:
+        out = out + dot(ref[0], ow_ref[at])
+        for t in range(3):
+            term = dot_nt(ref[t + 1], w_ref[t, :, at])
+            one = term if one is None else one + term
+            gb_ref[t : t + 1, at] = jnp.sum(ref[t + 1].astype(F32), axis=0, keepdims=True)
+    xhat, _ = standard(x_ref[...].astype(F32))
+    sums = [jnp.sum(v, axis=0, keepdims=True) for v in (one * xhat, one, two * xhat, two)]
+    heads_bias = jnp.concatenate([gb_ref[t : t + 1] for t in range(3)], axis=1)
+    heads_bias = jnp.concatenate([heads_bias, jnp.zeros((1, xhat.shape[1] - heads_bias.shape[1]), F32)], axis=1)
+    sums += [jnp.sum(dy_ref[...].astype(F32), axis=0, keepdims=True), gub_ref[...], heads_bias, jnp.zeros_like(heads_bias)]
+    vec = jnp.concatenate(sums, axis=0)
+    cols = vec_ref.shape[1]
+    vec_ref[...] = jnp.concatenate([vec[:, :cols], vec[:, cols:]], axis=0).astype(BF16)
+    rows = x_ref.shape[0] // 2
+    for at, value in ((0, out), (rows, one * pack_ref[0:1] + two * pack_ref[2:3])):
+        keep_ref[at : at + rows], send_ref[at : at + rows] = halves(core_flag(), value.astype(BF16))
+
+
+def sums_call(mine, recv, act, gu, dy, x, pack, w3, out_w, up_w, down_w, gub):
+    rows, width = x.shape
+    both = struct((rows, width), BF16)
+    outs = [both, both, struct((EXTRA, width // 2), BF16), struct((3, w3.shape[2]), F32)]
+    return small(sums_kernel, (mine, recv, act, gu, dy, x, pack, w3, out_w, up_w, down_w, gub), outs, "sums", 32)
+
+
+def ride_kernel(grad_ref, vec_ref, o_ref):
+    rows = grad_ref.shape[0] - EXTRA
+    o_ref[:rows] = grad_ref[:rows]
+    o_ref[rows:] = vec_ref[...]
+
+
+def ride(grad, vec):
+    return small(ride_kernel, (grad, vec), [struct(grad.shape, BF16)], "ride")[0]
+
+
+def place_ride_kernel(mine_ref, other_ref, *refs):
+    grad_ref, vec_ref = refs[-2:]
+    count, rows, lanes = grad_ref.shape
+    value = jnp.where(ctx_flag() == pl.program_id(0), mine_ref[...], other_ref[...]).astype(F32)
+    folds = rows // (mine_ref.shape[0] - EXTRA)
+    for t in range(count):
+        grad_ref[t] = unfold(value, lanes, t, folds)
+    at = slice(mine_ref.shape[0] - EXTRA, mine_ref.shape[0])
+    vec_ref[...] = mine_ref[at].astype(F32) + other_ref[at].astype(F32)
+
+
+def rows_kernel(a_ref, b_ref, v_ref, *refs):
+    heads_ref = refs[-1]
+    held = jnp.concatenate([v_ref[:8], v_ref[8:]], axis=1)
+    total = jnp.concatenate([a_ref[:8] + b_ref[:8], a_ref[8:] + b_ref[8:]], axis=1)
+    for r, ref in enumerate(refs[:-1]):
+        ref[...] = total[r : r + 1] if r < 4 else held[5:6] if r == 5 else held[4:5]
+    cols = heads_ref.shape[1]
+    for t in range(heads_ref.shape[0]):
+        heads_ref[t : t + 1] = held[6:7, t * cols : (t + 1) * cols]
+
+
+def rows_call(local, a, b, v):
+    row = struct((1, 2 * a.shape[1]), F32)
+    return small(rows_kernel, (a, b, v), [row] * 7 + [struct((3, local), F32)], "rows")
+
+
+def place_pair_kernel(mine_ref, other_ref, *refs):
+    value = jnp.where(ctx_flag() == pl.program_id(0), mine_ref[...], other_ref[...]).astype(F32)
+    heads_ref, out_ref = refs[-2:]
+    lanes = heads_ref.shape[2]
+    folds = heads_ref.shape[1] // (mine_ref.shape[0] - EXTRA)
+    heads_ref[0] = unfold(value, lanes, 0, folds)
+    out_ref[...] = unfold(value, lanes, 1, folds).T
+
+
+def results_kernel(mine_ref, other_ref, x_ref, dy_ref, pack_ref, out_ref, grad_ref):
+    rows = x_ref.shape[0] // 2
+    bias = pack_ref[5:6] + pack_ref[6:7]
+    first = core_flag() == 0
+    for i in range(2):
+        at = slice(i * rows, (i + 1) * rows)
+        here, there = (mine_ref, other_ref) if i == 0 else (other_ref, mine_ref)
+        out, grad = [
+            jnp.where(first, here[part], there[part]).astype(F32) for part in (slice(0, rows), slice(rows, 2 * rows))
+        ]
+        x = x_ref[at].astype(F32)
+        out_ref[at] = (x + out + bias).astype(BF16)
+        xhat, inverse = standard(x)
+        mean = jnp.mean(grad, axis=-1, keepdims=True)
+        along = jnp.mean(grad * xhat, axis=-1, keepdims=True)
+        grad_ref[at] = (dy_ref[at].astype(F32) + inverse * (grad - mean - xhat * along)).astype(BF16)
+
+
+def results_call(mine, other, x, dy, pack):
+    return small(results_kernel, (mine, other, x, dy, pack), [struct(x.shape, BF16)] * 2, "results", 24)
+
+
+INWARD = [(0, 1), (3, 2)]
+MIDDLE = [(1, 2), (2, 1)]
+OUTWARD = [(1, 0), (2, 3)]
+SWAP = [(0, 1), (1, 0)]
+CORES = [(i, i ^ 1) for i in range(4)]
+CHIPS = [(i, i ^ 2) for i in range(4)]
+
+
+class Sequence:
+    def __init__(self):
+        self.last = None
+
+    def tied(self, operands):
+        if self.last is None:
+            return operands
+        return lax.optimization_barrier((operands, self.last))[0]
+
+    def __call__(self, step, *operands):
+        result = step(*self.tied(operands))
+        self.last = jax.tree.leaves(result)[0]
+        return result
+
+    def send(self, value, axis, perm):
+        return lax.ppermute(self.tied(value), axis, perm)
+
+    def arrived(self, value):
+        value = self.tied(value)
+        self.last = value
+        return value
+
+
+def turn_table(positions):
+    half = ROT // 2
+    inverse = jnp.exp(jnp.arange(half, dtype=F32) * (-2.0 * jnp.log(10000.0) / ROT))
+    angles = inverse[:, None] * positions.astype(F32)[None, :]
+    return jnp.concatenate([jnp.cos(angles), jnp.sin(angles)], axis=0)
+
+
+def line_then_ctx(run, x, finish):
+    r = yield "dp", INWARD, run.tied(x)
+    x = run(add, x, r)
+    r = yield "dp", MIDDLE, x
+    x = run(add, x, r)
+    r = yield "dp", OUTWARD, x
+    x = run(choose, x, r)
+    r = yield "ctx", SWAP, x
+    finish(x, r)
+
+
+def over_tensor(run, mine, other, finish):
+    r = yield "tensor", CORES, run.tied(other)
+    mine = run(add, mine, r)
+    r = yield "tensor", CHIPS, mine
+    mine = run(add, mine, r)
+    r = yield "tensor", CORES, mine
+    finish(mine, r)
+
+
+def vectors_over_tensor(run, local, vec, finish):
+    r = yield "tensor", CORES, run.tied(vec)
+    x = run(add, vec, r)
+    r = yield "tensor", CHIPS, x
+    finish(run(functools.partial(rows_call, local), x, r, vec))
+
+
+def gather_span(run, x, finish):
+    half = x.shape[0] // 2
+    near = yield "ctx", SWAP, lax.dynamic_slice_in_dim(run.tied(x), lax.axis_index("tensor") % 2 * half, half, 0)
+    near = run.arrived(near)
+    pair = yield "tensor", CORES, near
+    finish(near, pair)
+
+
+class Unit:
+    def __init__(self, run, steps):
+        self.run, self.steps, self.message = run, steps, None
+
+    def request(self):
+        try:
+            return self.steps.send(self.message)
+        except StopIteration:
+            return None
+
+    def advance(self):
+        request = self.request()
+        if request:
+            axis, perm, value = request
+            self.message = lax.ppermute(value, axis, perm)
+
+    def advance_with(self, other):
+        (_, _, inward), (_, _, outward) = self.request(), other.request()
+        self.message = other.message = lax.ppermute(self.run(choose, outward, inward), "dp", INWARD + OUTWARD)
+
+    def wait(self):
+        self.message = self.run.arrived(self.message)
+
+
+class Held:
+    pass
+
+
+def two_spans(
+    tokens, segments, padding, cotangent, norm1_gain, norm1_shift, norm2_gain, norm2_shift,
+    qkv_weight, qkv_bias, out_weight, out_bias, up_weight, up_bias, down_weight, down_bias,
+):
+    x, dy = tokens[0], cotangent[0]
+    rows, width = x.shape
+    local = qkv_weight.shape[2]
+    hidden = up_weight.shape[1]
+    lanes = 2 * HEAD_DIM
+    row = lambda v: v.reshape(1, -1)
+    w3 = jnp.transpose(qkv_weight, (1, 0, 2))
+    run = Sequence()
+    s, u = Held(), Held()
+    dests = {}
+    shapes = {"down": (hidden, width), "up": (width, hidden), "qkv": (3, width, local), "out": (local, width),
+              "vec": (EXTRA, width // 2)}
+
+    def open_unit(name, steps, *operands):
+        setattr(u, name, Unit(run, steps(run, *operands)))
+
+    def placing(names, kernel, count, blocks, indices):
+        def finish(a, b):
+            held = [n for n in names if n in dests]
+
+            def step(a, b, *old):
+                return pl.pallas_call(
+                    kernel,
+                    grid=(count,),
+                    in_specs=[resident()] * 2 + [pl.BlockSpec(memory_space=pl.ANY)] * len(old),
+                    out_specs=[pl.BlockSpec(block, index) for block, index in zip(blocks, indices)],
+                    out_shape=[struct(shapes[n], F32) for n in names],
+                    input_output_aliases={2 + i: names.index(n) for i, n in enumerate(held)},
+                    compiler_params=params(24),
+                    cost_estimate=cost(0, 0),
+                    name="place",
+                )(a, b, *old)
+
+            dests.update(zip(names, run(step, a, b, *[dests[n] for n in held])))
+
+        return finish
+
+    open_unit("tk", gather_span, x, lambda *p: s.__dict__.update(tokens=p))
+    open_unit("dy", gather_span, dy, lambda *p: s.__dict__.update(dy=p))
+
+    def ids_0():
+        ids = jnp.concatenate([segments, padding], axis=0)
+        s.ids = ids, run.send(ids, "ctx", SWAP)
+
+    def ids_w():
+        s.ids = s.ids[0], run.arrived(s.ids[1])
+
+    def own():
+        s.pack = jnp.stack([norm1_gain, norm1_shift, norm2_gain, norm2_shift, up_bias, out_bias, down_bias])
+        s.n1, s.n2, s.act, s.gu, s.gub = run(own_call, x, dy, up_weight, down_weight, s.pack)
+
+    def other():
+        u.tk.advance()
+        s.n1x, s.n2x, *heads, s.actx, s.slope = run(
+            other_call, *s.tokens, s.n1, s.pack, w3, qkv_bias, s.table, up_weight)
+        s.qkv, s.qkvx = heads[:3], heads[3:]
+
+    def tables():
+        s.table = run(turn_table, jnp.arange(2 * rows, dtype=jnp.int32))
+
+    def weights():
+        u.dy.advance()
+        s.dyx, s.gux, s.ga, *grads = run(
+            weights_call, *s.dy, s.act, dy, s.actx, s.slope, down_weight, out_weight)
+        for j, grad in enumerate(grads):
+            open_unit(f"D{j}", line_then_ctx, grad, placing(
+                ["down"], place_halves_kernel, 2, [(hidden // 2, width // 2)], [lambda i, j=j: (i, j)]))
+
+    def attend():
+        s.mine, s.theirs, s.qk, vo_grad, *ups = run(
+            lambda *a: attend_call(a[:3], a[3:6], *a[6:]),
+            *s.qkv, *s.qkvx, s.ga, *s.ids, s.table,
+            s.n1, s.n1x, dy, s.dyx, s.n2, s.n2x, s.gu, s.gux)
+        open_unit("Q1", line_then_ctx, vo_grad, placing(
+            ["qkv", "out"], place_pair_kernel, 2, [(1, width, lanes), (lanes, width)],
+            [lambda i: (2, 0, i), lambda i: (i, 0)]))
+        for j, grad in enumerate(ups):
+            open_unit(f"U{j}", line_then_ctx, grad, placing(
+                ["up"], place_halves_kernel, 2, [(width // 2, hidden // 2)], [lambda i, j=j: (j, i)]))
+
+    def gpx_0():
+        s.recv = run.send(s.theirs, "ctx", SWAP)
+
+    def gpx_w():
+        s.recv = run.arrived(s.recv)
+
+    def sums():
+        keep, send, s.vec, _ = run(
+            sums_call, s.mine, s.recv, s.act, s.gu, dy, x, s.pack, w3, out_weight, up_weight, down_weight,
+            s.gub)
+
+        def finish(a, b):
+            s.block_output, s.input_grad = run(lambda a, b: results_call(a, b, x, dy, s.pack), a, b)
+
+        open_unit("both", over_tensor, keep, send, finish)
+
+    def join():
+        both = run(ride, s.qk, s.vec)
+        put = placing(
+            ["qkv", "vec"], place_ride_kernel, 2, [(2, width, lanes), s.vec.shape], [lambda i: (0, 0, i), lambda i: (0, 0)])
+
+        def finish(a, b):
+            put(a, b)
+            open_unit("vec", vectors_over_tensor, local, dests["vec"], lambda rows: s.__dict__.update(rows=rows))
+
+        open_unit("Q0", line_then_ctx, both, finish)
+
+    u.tk.advance()
+    own()
+    u.dy.advance()
+    tables()
+    u.tk.advance()
+    ids_0()
+    other()
+    ids_w()
+    u.dy.advance()
+    weights()
+    u.D0.advance()
+    attend()
+    u.D1.advance()
+    u.D0.wait()
+    u.D0.advance()
+    gpx_0()
+    gpx_w()
+    u.D1.wait()
+    u.D0.wait()
+    u.U0.advance_with(u.D0)
+    u.D1.advance()
+    sums()
+    join()
+    u.U0.wait()
+    u.Q0.advance_with(u.D1)
+    u.D0.advance()
+    u.U0.advance()
+    u.both.advance()
+    u.Q0.wait()
+    u.Q1.advance_with(u.U0)
+    u.D1.advance()
+    u.Q0.advance()
+    u.both.advance()
+    u.D0.advance()
+    u.Q1.wait()
+    u.U1.advance_with(u.Q0)
+    u.U0.advance()
+    u.Q1.advance()
+    u.D1.advance()
+    u.U1.advance()
+    u.Q1.advance()
+    u.Q0.advance()
+    u.both.advance()
+    u.U0.advance()
+    u.U1.advance()
+    u.Q1.advance()
+    u.Q0.advance()
+    u.vec.advance()
+    u.both.advance()
+    u.U1.advance()
+    u.Q1.advance()
+    u.vec.advance()
+    u.vec.advance()
+    u.U1.advance()
+    *rows, heads_bias = s.rows
+    gain1, shift1, gain2, shift2, dy_sum, up_sum, dy_same = [r.reshape(-1) for r in rows]
+    return (
+        s.block_output[None],
+        s.input_grad[None],
+        gain1, shift1, gain2, shift2,
+        jnp.transpose(dests["qkv"], (1, 0, 2)),
+        heads_bias,
+        dests["out"],
+        dy_sum,
+        dests["up"],
+        up_sum,
+        dests["down"],
+        dy_same,
+    )
+
+
+def fits(mesh):
+    return dict(mesh.shape) == {"dp": 4, "ctx": 2, "tensor": 4}
+
+
 def solution(mesh):
     return jax.shard_map(
-        on_device,
+        two_spans if fits(mesh) else on_device,
         mesh=mesh,
         in_specs=(
             P("dp", "ctx", None),

time: 634 us -> 182 us (0.29)
  waiting for transfers between devices: 420 us -> 74 us
  matrix products: 69.7 us -> 0 us
  blocking collectives: 61.1 us -> 0 us
  Pallas kernels: 0 us -> 51.3 us
  starting transfers between devices: 0.64 us -> 45.5 us
  local copies, waits for them, and re-layouts: 38 us -> 9.07 us
  other arithmetic: 28.7 us -> 0.23 us
  between operations: 14.3 us -> 1.14 us
    psum x2 -> x0, waiting for transfers between devices: 414 us -> none  [the longest x1 359 us: on_device(): lax.psum((gain_one, shift_one, gain_two, shift_two, grad_qkv_w, grad_qkv_...]
    ppermute x0 -> x31, waiting for transfers between devices: none -> 74 us  [the longest x25 30.4 us: advance(): self.message = lax.ppermute(value, axis, perm)]
    dot_general x26 -> x0, matrix products: 69.7 us -> none  [the longest x2 8.17 us: attend_step(): jnp.einsum('hqk,khd->qhd', weights_low, value_block, preferred_element_ty...]
    pallas_call x0 -> x39, Pallas kernels: none -> 51.3 us  [the longest x3 24 us: fetched(): pl.pallas_call(kernel, grid=(1,), in_specs=[whole(a.shape) for a in array...]
    ppermute x0 -> x31, starting transfers between devices: none -> 45.5 us  [the longest x25 30 us: advance(): self.message = lax.ppermute(value, axis, perm)]
    psum x1 -> x0, blocking collectives: 39.6 us -> none  [on_device(): lax.psum((gain_one, shift_one, gain_two, shift_two, grad_qkv_w, grad_qkv_...]
    all_gather x3 -> x0, blocking collectives: 21.5 us -> none  [the longest x1 9.94 us: on_device(): lax.all_gather(values_own.reshape(span_rows, local_width), 'ctx', axis=0,...]
    reduce_sum x8 -> x0, other arithmetic: 18.6 us -> none  [the longest x2 6.45 us: total_step(): jnp.sum(jnp.where(visible, jnp.exp(masked - new_top[..., None]), 0.0), ax...]
  transfers between devices with their start and end apart: 4 -> 31, of which waited for: 3 -> 13; matrix products, arithmetic and copies ran while one was open for 7% -> 1% of each run, Pallas kernels for 0% -> 25%
where the time goes in v1:
time: 182 us; the launch traced here: 181 us
  waiting for transfers between devices  74 us (41%)
  Pallas kernels  51.3 us (28%)
  starting transfers between devices  45.5 us (25%)
  local copies, waits for them, and re-layouts  9.07 us (5%)
    ppermute x25, waiting for transfers between devices, advance(): self.message = lax.ppermute(value, axis, perm)  30.4 us
    ppermute x25, starting transfers between devices, advance(): self.message = lax.ppermute(value, axis, perm)  30 us
    ppermute x4, waiting for transfers between devices, advance_with(): lax.ppermute(self.run(choose, outward, inward), 'dp', INWARD + OUTWARD)  28.5 us
    pallas_call x3, Pallas kernels, fetched(): pl.pallas_call(kernel, grid=(1,), in_specs=[whole(a.shape) for a in array...  24 us
    ppermute x2, waiting for transfers between devices, send(): return lax.ppermute(self.tied(value), axis, perm)  15.2 us
    ppermute x4, starting transfers between devices, advance_with(): lax.ppermute(self.run(choose, outward, inward), 'dp', INWARD + OUTWARD)  13.5 us
    pallas_call x29, Pallas kernels, small(): pl.pallas_call(kernel, in_specs=[resident()] * len(arrays), out_specs=[re...  11.8 us
    pallas_call x6, Pallas kernels, step(): pl.pallas_call(kernel, grid=(count,), in_specs=[resident()] * 2 + [pl.Blo...  8.45 us
  transfers between devices with their start and end apart: 31, of which 13 were waited for; matrix products, arithmetic and copies ran while one was open for 1% of the time, Pallas kernels for 25%

profile of v1, /device:TPU:0, one launch (start us, length us, event | category | flops | bytes accessed | tf_op | source)
XLA Modules:
  0.0 181.3 jit_solution(4853790971475215829)
XLA Ops:
  0.7 1.1 dynamic-slice_bitcast_fusion
  1.7 3.0 %collective-permute-start = (bf16[256,1024]{1,0:T(8,128)(2,1)S(1)}, bf16[256,1024]{1,0:T(8,128)(2,1)S(1)}, u32[]{:S(2)}, u32[]{:S(2)}) collective-permute-start(bf16[256,1024]{1,0:T(8,128)(2,1)S(1)} %dynamic-slice_bitcast_fusion), channel_id=1, source_target_pairs={{0,4},{4,0},{1,5},{5,1},{2,6},{6,2},{3,7},{7,3},{8,12},{12,8},{9,1... | collective-permute-start | bytes 1572872 | tf_op jit(solution)/shard_map/ppermute | solution.py:852
  4.8 0.8 stack.31.pack_ref
  5.6 1.2 copy-done.2
  6.8 7.0 %own.1 = (bf16[512,1024]{1,0:T(8,128)(2,1)S(1)}, bf16[512,1024]{1,0:T(8,128)(2,1)S(1)}, bf16[512,1024]{1,0:T(8,128)(2,1)S(1)}, bf16[512,1024]{1,0:T(8,128)(2,1)S(1)}, f32[1,1024]{1,0:T(1,128)S(1)}) custom-call(bf16[512,1024]{1,0:T(8,128)(2,1)S(1)} %bitcast.28, bf16[512,1024]{1,0:T(8,128)(2,1)} %bitcast.22, bf16[1024,1024]{1,0:T(8,128)(2,1)} %up_ref.3, ...), custom_call_target="tpu_custom_call" | custom-call | flops 8000000000 | bytes 1024 | tf_op jit(solution)/shard_map/own/pallas_call | solution.py:459
  13.9 1.0 copy-done.9
  14.8 1.0 copy-done.11
  15.8 0.2 multiply_cosine_fusion
  16.1 0.6 collective-permute-done.near_ref
  16.8 1.8 collective-permute-start.2
  18.6 0.4 collective-permute-start.3
  18.9 6.4 %other.1 = (bf16[512,1024]{1,0:T(8,128)(2,1)S(1)}, bf16[512,1024]{1,0:T(8,128)(2,1)S(1)}, bf16[512,128]{1,0:T(8,128)(2,1)S(1)}, bf16[512,128]{1,0:T(8,128)(2,1)S...) custom-call(bf16[256,1024]{1,0:T(8,128)(2,1)S(1)} %collective-permut, ...), custom_call_target="tpu_custom_call" | custom-call | flops 5000000000 | bytes 1024 | tf_op jit(solution)/shard_map/other/pallas_call | solution.py:371
  25.3 1.0 copy-done.12
  26.3 1.0 copy-done.13
  27.3 1.0 copy-done.17
  28.2 3.0 %collective-permute-done.3.ids_x_ref = s32[2,512]{1,0:T(2,128)S(1)} collective-permute-done((s32[2,512]{1,0:T(2,128)S(1)}, s32[2,512]{1,0:T(2,128)S(1)}, u32[]{:S(2)}, u32[]{:S(2)}) %collective-permute-start.3) | collective-permute-done | bytes 4128 | tf_op jit(solution)/shard_map/ppermute | solution.py:788
  31.2 1.9 %collective-permute-done.4.pair_ref = bf16[256,1024]{1,0:T(8,128)(2,1)S(1)} collective-permute-done((bf16[256,1024]{1,0:T(8,128)(2,1)S(1)}, bf16[256,1024]{1,0:T(8,128)(2,1)S(1)}, u32[]{:S(2)}, u32[]{:S(2)}) %collective-permute-start.4) | collective-permute-done | bytes 524320 | tf_op jit(solution)/shard_map/ppermute | solution.py:852
  33.2 4.8 %weights.1 = (bf16[512,1024]{1,0:T(8,128)(2,1)S(1)}, bf16[512,512]{1,0:T(8,128)(2,1)S(1)}, bf16[1024,128]{1,0:T(8,128)(2,1)S(1)}, bf16[528,512]{1,0:T(8,128)(2,1)S(1)}, bf16[528,512]{1,0:T(8,128)(2,1)S(1)}) custom-call(bf16[256,1024]{1,0:T(8,128)(2,1)S(1)} %collective-permute-done.2.near_ref, bf16[256,1024]{1,0:T(8,128)(2,1)S(1)} %collective-permute-done.4.pair_ref, ...), custom_call_target="tpu_custom_call" | custom-call | flops 4000000000 | bytes 1024 | tf_op jit(solution)/shard_map/weights/pallas_call | solution.py:371
  38.0 1.0 copy-done.14
  38.9 3.9 %collective-permute-start.5 = (bf16[528,512]{1,0:T(8,128)(2,1)S(1)}, bf16[528,512]{1,0:T(8,128)(2,1)S(1)}, u32[]{:S(2)}, u32[]{:S(2)}) collective-permute-start(bf16[528,512]{1,0:T(8,128)(2,1)S(1)} %get-tuple-element.259.a_ref), channel_id=1, source_target_pairs={{0,8},{24,16},{1,9},{25,17},{2,10},{26,18},{3,11},{27,19},{4,12},{... | collective-permute-start | bytes 1622024 | tf_op jit(solution)/shard_map/ppermute | solution.py:852
  42.9 12.9 %attend.1 = (bf16[4,512,128]{2,1,0:T(8,128)(2,1)S(1)}, bf16[4,512,128]{2,1,0:T(8,128)(2,1)S(1)}, bf16[528,512]{1,0:T(8,128)(2,1)S(1)}, bf16[528,512]{1,0:T(8,128...) custom-call(bf16[512,128]{1,0:T(8,128)(2,1)S(1)} %get-tuple-element.236.q_o_ref, ...), custom_call_target="tpu_custom_call" | custom-call | flops 1024 | bytes 1024 | tf_op jit(solution)/shard_map/attend/pallas_call | solution.py:371
  55.8 1.7 collective-permute-start.7
  57.7 0.7 collective-permute-start.8
  58.4 1.6 collective-permute-start.6
  59.9 12.2 %collective-permute-done.6.recv_ref = bf16[4,512,128]{2,1,0:T(8,128)(2,1)S(1)} collective-permute-done((bf16[4,512,128]{2,1,0:T(8,128)(2,1)S(1)}, bf16[4,512,128]{2,1,0:T(8,128)(2,1)S(1)}, u32[]{:S(2)}, u32[]{:S(2)}) %collective-permute-start.6) | collective-permute-done | bytes 524320 | tf_op jit(solution)/shard_map/ppermute | solution.py:788
  72.3 2.1 %collective-permute-start.9 = (bf16[528,512]{1,0:T(8,128)(2,1)S(1)}, bf16[528,512]{1,0:T(8,128)(2,1)S(1)}, u32[]{:S(2)}, u32[]{:S(2)}) collective-permute-start(bf16[528,512]{1,0:T(8,128)(2,1)S(1)} %choose.10), channel_id=1, source_target_pairs={{0,8},{24,16},{8,0},{16,24},{1,9},{25,17},{9,1},{17,25},{2,10},{26... | collective-permute-start | bytes 1622024 | tf_op jit(solution)/shard_map/ppermute | solution.py:856
  74.5 0.9 collective-permute-start.10
  75.5 5.9 %sums.1 = (bf16[512,1024]{1,0:T(8,128)(2,1)S(1)}, bf16[512,1024]{1,0:T(8,128)(2,1)S(1)}, bf16[16,512]{1,0:T(8,128)(2,1)S(1)}, f32[3,256]{1,0:T(4,128)}) custom-call(bf16[4,512,128]{2,1,0:T(8,128)(2,1)S(1)} %get-tuple-element.276.mine_ref, bf16[4,512,128]{2,1,0:T(8,128)(2,1)S(1)} %collective-permute-done.6.recv_ref, ...), custom_call_target="tpu_custom_call" | custom-call | bytes 1024 | tf_op jit(solution)/shard_map/sums/pallas_call | solution.py:358
  81.5 4.1 %collective-permute-done.9.b_ref = bf16[528,512]{1,0:T(8,128)(2,1)S(1)} collective-permute-done((bf16[528,512]{1,0:T(8,128)(2,1)S(1)}, bf16[528,512]{1,0:T(8,128)(2,1)S(1)}, u32[]{:S(2)}, u32[]{:S(2)}) %collective-permute-start.9) | collective-permute-done | bytes 540704 | tf_op jit(solution)/shard_map/ppermute | solution.py:856
  86.1 3.8 %collective-permute-start.12 = (bf16[528,512]{1,0:T(8,128)(2,1)S(1)}, bf16[528,512]{1,0:T(8,128)(2,1)S(1)}, u32[]{:S(2)}, u32[]{:S(2)}) collective-permute-start(bf16[528,512]{1,0:T(8,128)(2,1)S(1)} %choose.11), channel_id=1, source_target_pairs={{0,8},{24,16},{8,0},{16,24},{1,9},{25,17},{9,1},{17,25},{2,10},{26... | collective-permute-start | bytes 1622024 | tf_op jit(solution)/shard_map/ppermute | solution.py:856
  89.9 0.7 collective-permute-start.13
  90.6 1.6 collective-permute-start.17
  92.2 10.6 %collective-permute-done.12.b_ref = bf16[528,512]{1,0:T(8,128)(2,1)S(1)} collective-permute-done((bf16[528,512]{1,0:T(8,128)(2,1)S(1)}, bf16[528,512]{1,0:T(8,128)(2,1)S(1)}, u32[]{:S(2)}, u32[]{:S(2)}) %collective-permute-start.12) | collective-permute-done | bytes 540704 | tf_op jit(solution)/shard_map/ppermute | solution.py:856
  103.0 3.7 %collective-permute-start.16 = (bf16[528,512]{1,0:T(8,128)(2,1)S(1)}, bf16[528,512]{1,0:T(8,128)(2,1)S(1)}, u32[]{:S(2)}, u32[]{:S(2)}) collective-permute-start(bf16[528,512]{1,0:T(8,128)(2,1)S(1)} %choose.13), channel_id=1, source_target_pairs={{0,8},{24,16},{8,0},{16,24},{1,9},{25,17},{9,1},{17,25},{2,10},{26... | collective-permute-start | bytes 1622024 | tf_op jit(solution)/shard_map/ppermute | solution.py:856
  106.9 0.7 collective-permute-start.15
  107.6 0.2 add.35.a_ref
  107.9 1.6 collective-permute-start.14
  109.4 1.5 collective-permute-start.20
  111.0 1.4 place.6.refs_0_
  112.3 6.4 %collective-permute-done.16.b_ref = bf16[528,512]{1,0:T(8,128)(2,1)S(1)} collective-permute-done((bf16[528,512]{1,0:T(8,128)(2,1)S(1)}, bf16[528,512]{1,0:T(8,128)(2,1)S(1)}, u32[]{:S(2)}, u32[]{:S(2)}) %collective-permute-start.16) | collective-permute-done | bytes 540704 | tf_op jit(solution)/shard_map/ppermute | solution.py:856
  119.0 3.9 %collective-permute-start.18 = (bf16[528,512]{1,0:T(8,128)(2,1)S(1)}, bf16[528,512]{1,0:T(8,128)(2,1)S(1)}, u32[]{:S(2)}, u32[]{:S(2)}) collective-permute-start(bf16[528,512]{1,0:T(8,128)(2,1)S(1)} %choose.15), channel_id=1, source_target_pairs={{0,8},{24,16},{8,0},{16,24},{1,9},{25,17},{9,1},{17,25},{2,10},{26... | collective-permute-start | bytes 1622024 | tf_op jit(solution)/shard_map/ppermute | solution.py:856
  123.1 0.7 collective-permute-start.19
  123.8 1.6 collective-permute-start.25
  125.4 1.4 place.7
  126.8 7.3 %collective-permute-done.18.b_ref = bf16[528,512]{1,0:T(8,128)(2,1)S(1)} collective-permute-done((bf16[528,512]{1,0:T(8,128)(2,1)S(1)}, bf16[528,512]{1,0:T(8,128)(2,1)S(1)}, u32[]{:S(2)}, u32[]{:S(2)}) %collective-permute-start.18) | collective-permute-done | bytes 540704 | tf_op jit(solution)/shard_map/ppermute | solution.py:856
  134.2 0.7 collective-permute-start.24
  135.1 0.2 add.40.mine_ref
  135.5 1.3 collective-permute-start.23
  136.8 1.6 collective-permute-start.22
  138.4 1.4 place.8.refs_0_
  139.9 1.3 collective-permute-start.28
  141.2 13.1 %collective-permute-done.23.b_ref = bf16[528,512]{1,0:T(8,128)(2,1)S(1)} collective-permute-done((bf16[528,512]{1,0:T(8,128)(2,1)S(1)}, bf16[528,512]{1,0:T(8,128)(2,1)S(1)}, u32[]{:S(2)}, u32[]{:S(2)}) %collective-permute-start.23) | collective-permute-done | bytes 540704 | tf_op jit(solution)/shard_map/ppermute | solution.py:852
  154.4 1.6 collective-permute-start.27
  156.0 1.4 place.9
  157.4 2.6 %results.1 = (bf16[512,1024]{1,0:T(8,128)(2,1)}, bf16[512,1024]{1,0:T(8,128)(2,1)}) custom-call(bf16[512,1024]{1,0:T(8,128)(2,1)S(1)} %add.40.mine_ref, bf16[512,1024]{1,0:T(8,128)(2,1)S(1)} %collective-permute-done.21.other_ref, bf16[512,1024]{1,0:T(8,128)(2,1)S(1)} %bitcast.30, bf16[512,1024]{1,0:T(8,128)(2,1)S(1)} %bitcast.27, f32[7,1024]{1,0:T(8,128)S(1)} %stack.31.pack_ref), custom_call_target="tpu_custom_call" | custom-call | bytes 1024 | tf_op jit(solution)/shard_map/results/pallas_call | solution.py:358
  160.0 5.7 %collective-permute-done.28.b_ref = bf16[528,512]{1,0:T(8,128)(2,1)S(1)} collective-permute-done((bf16[528,512]{1,0:T(8,128)(2,1)S(1)}, bf16[528,512]{1,0:T(8,128)(2,1)S(1)}, u32[]{:S(2)}, u32[]{:S(2)}) %collective-permute-start.28) | collective-permute-done | bytes 540704 | tf_op jit(solution)/shard_map/ppermute | solution.py:852
  165.8 1.6 collective-permute-start.30
  167.3 1.0 collective-permute-done.27.other_ref
  168.3 1.5 place.10
  169.8 1.5 collective-permute-start.29
  171.4 2.4 %collective-permute-done.29.b_ref = f32[16,512]{1,0:T(8,128)S(1)} collective-permute-done((f32[16,512]{1,0:T(8,128)S(1)}, f32[16,512]{1,0:T(8,128)S(1)}, u32[]{:S(2)}, u32[]{:S(2)}) %collective-permute-start.29) | collective-permute-done | bytes 32800 | tf_op jit(solution)/shard_map/ppermute | solution.py:852
  173.8 0.6 rows.1
  174.4 5.5 %collective-permute-done.30.other_ref = bf16[528,512]{1,0:T(8,128)(2,1)S(1)} collective-permute-done((bf16[528,512]{1,0:T(8,128)(2,1)S(1)}, bf16[528,512]{1,0:T(8,128)(2,1)S(1)}, u32[]{:S(2)}, u32[]{:S(2)}) %collective-permute-start.30) | collective-permute-done | bytes 540704 | tf_op jit(solution)/shard_map/ppermute | solution.py:852
  179.9 1.4 place.11
  (86 shorter events, 2.6 us)
Async XLA Ops:
  1.7 15.0 %collective-permute-start = (bf16[256,1024]{1,0:T(8,128)(2,1)S(1)}, bf16[256,1024]{1,0:T(8,128)(2,1)S(1)}, u32[]{:S(2)}, u32[]{:S(2)}) collective-permute-start(bf16[256,1024]{1,0:T(8,128)(2,1)S(1)} %dynamic-slice_bitcast_fusion), channel_id=1, source_target_pairs={{0,4},{4,0},{1,5},{5,1},{2,6},{6,2},{3,7},{7,3},{8,12},{12,8},{9,1... | collective-permute-start | bytes 1572872 | tf_op jit(solution)/shard_map/ppermute | solution.py:852
  5.6 1.2 copy-start.2
  6.8 9.9 %copy-start = (bf16[1,512,1024]{2,1,0:T(8,128)(2,1)S(1)}, bf16[1,512,1024]{2,1,0:T(8,128)(2,1)}, u32[]{:S(2)}) copy-start(bf16[1,512,1024]{2,1,0:T(8,128)(2,1)} %param.19) | copy-start | bytes 3145732
  6.8 11.7 %copy-start.18 = (s32[1,512]{1,0:T(1,128)S(1)}, s32[1,512]{1,0:T(1,128)}, u32[]{:S(2)}) copy-start(s32[1,512]{1,0:T(1,128)} %param.18) | copy-start | bytes 6148
  6.8 11.7 %copy-start.19 = (s32[1,512]{1,0:T(1,128)S(1)}, s32[1,512]{1,0:T(1,128)}, u32[]{:S(2)}) copy-start(s32[1,512]{1,0:T(1,128)} %param.17) | copy-start | bytes 6148
  6.8 12.1 %copy-start.16 = (f32[3,256]{1,0:T(4,128)S(1)}, f32[3,256]{1,0:T(4,128)}, u32[]{:S(2)}) copy-start(f32[3,256]{1,0:T(4,128)} %b_ref) | copy-start | bytes 9220
  13.9 1.0 copy-start.9
  14.8 1.0 copy-start.11
  15.8 1.0 copy-start.4
  16.7 2.2 %collective-permute-start.1 = (bf16[256,1024]{1,0:T(8,128)(2,1)S(1)}, bf16[256,1024]{1,0:T(8,128)(2,1)S(1)}, u32[]{:S(2)}, u32[]{:S(2)}) collective-permute-start(bf16[256,1024]{1,0:T(8,128)(2,1)S(1)} %collective-permute-done.near_ref), channel_id=1, source_target_pairs={{0,1},{1,0},{2,3},{3,2},{4,5},{5,4},{6,7},{7,6},{8,9},{9,8},{10,11... | collective-permute-start | bytes 1572872 | tf_op jit(solution)/shard_map/ppermute | solution.py:852
  16.8 14.5 %collective-permute-start.2 = (bf16[256,1024]{1,0:T(8,128)(2,1)S(1)}, bf16[256,1024]{1,0:T(8,128)(2,1)S(1)}, u32[]{:S(2)}, u32[]{:S(2)}) collective-permute-start(bf16[256,1024]{1,0:T(8,128)(2,1)S(1)} %constant_dynamic-slice_fusion), channel_id=1, source_target_pairs={{0,4},{4,0},{1,5},{5,1},{2,6},{6,2},{3,7},{7,3},{8,12},{12,8},{9,1... | collective-permute-start | bytes 1572872 | tf_op jit(solution)/shard_map/ppermute | solution.py:852
  18.6 12.7 %collective-permute-start.3 = (s32[2,512]{1,0:T(2,128)S(1)}, s32[2,512]{1,0:T(2,128)S(1)}, u32[]{:S(2)}, u32[]{:S(2)}) collective-permute-start(s32[2,512]{1,0:T(2,128)S(1)} %pad_add_fusion.ids_o_ref), channel_id=1, source_target_pairs={{0,4},{4,0},{1,5},{5,1},{2,6},{6,2},{3,7},{7,3},{8,12},{12,8},{9,1... | collective-permute-start | bytes 12296 | tf_op jit(solution)/shard_map/ppermute | solution.py:788
  18.9 14.2 %copy-start.15 = (bf16[256,1024]{1,0:T(8,128)(2,1)S(1)}, bf16[256,1024]{1,0:T(8,128)(2,1)}, u32[]{:S(2)}) copy-start(bf16[256,1024]{1,0:T(8,128)(2,1)} %ow_ref.1) | copy-start | bytes 1572868
  25.3 1.0 copy-start.12
  26.3 1.0 copy-start.13
  27.3 1.0 copy-start.17
  31.2 1.9 %collective-permute-start.4 = (bf16[256,1024]{1,0:T(8,128)(2,1)S(1)}, bf16[256,1024]{1,0:T(8,128)(2,1)S(1)}, u32[]{:S(2)}, u32[]{:S(2)}) collective-permute-start(bf16[256,1024]{1,0:T(8,128)(2,1)S(1)} %collective-permute-done.2.near_ref), channel_id=1, source_target_pairs={{0,1},{1,0},{2,3},{3,2},{4,5},{5,4},{6,7},{7,6},{8,9},{9,8},{10,11... | collective-permute-start | bytes 1572872 | tf_op jit(solution)/shard_map/ppermute | solution.py:852
  33.2 9.7 %copy-start.10 = (bf16[512,1024]{1,0:T(8,128)(2,1)S(1)}, bf16[512,1024]{1,0:T(8,128)(2,1)}, u32[]{:S(2)}) copy-start(bf16[512,1024]{1,0:T(8,128)(2,1)} %copy-done.9) | copy-start | bytes 3145732
  38.0 1.0 copy-start.14
  38.9 18.6 %collective-permute-start.5 = (bf16[528,512]{1,0:T(8,128)(2,1)S(1)}, bf16[528,512]{1,0:T(8,128)(2,1)S(1)}, u32[]{:S(2)}, u32[]{:S(2)}) collective-permute-start(bf16[528,512]{1,0:T(8,128)(2,1)S(1)} %get-tuple-element.259.a_ref), channel_id=1, source_target_pairs={{0,8},{24,16},{1,9},{25,17},{2,10},{26,18},{3,11},{27,19},{4,12},{... | collective-permute-start | bytes 1622024 | tf_op jit(solution)/shard_map/ppermute | solution.py:852
  42.9 32.6 %copy-start.7 = (bf16[1024,1024]{1,0:T(8,128)(2,1)S(1)}, bf16[1024,1024]{1,0:T(8,128)(2,1)}, u32[]{:S(2)}) copy-start(bf16[1024,1024]{1,0:T(8,128)(2,1)} %down_ref.3) | copy-start | bytes 6291460
  42.9 32.6 %copy-start.8 = (bf16[1024,3,256]{2,0,1:T(8,128)(2,1)S(1)}, bf16[1024,3,256]{2,0,1:T(8,128)(2,1)}, u32[]{:S(2)}) copy-start(bf16[1024,3,256]{2,0,1:T(8,128)(2,1)} %param.24) | copy-start | bytes 4718596
  55.8 19.7 %copy-start.1 = (bf16[1,512,1024]{2,1,0:T(8,128)(2,1)S(1)}, bf16[1,512,1024]{2,1,0:T(8,128)(2,1)}, u32[]{:S(2)}) copy-start(bf16[1,512,1024]{2,1,0:T(8,128)(2,1)} %param.19) | copy-start | bytes 3145732
  55.8 19.7 %copy-start.3 = (bf16[1,512,1024]{2,1,0:T(8,128)(2,1)S(1)}, bf16[1,512,1024]{2,1,0:T(8,128)(2,1)}, u32[]{:S(2)}) copy-start(bf16[1,512,1024]{2,1,0:T(8,128)(2,1)} %param.16) | copy-start | bytes 3145732
  55.8 19.7 %copy-start.5 = (bf16[512,1024]{1,0:T(8,128)(2,1)S(1)}, bf16[512,1024]{1,0:T(8,128)(2,1)}, u32[]{:S(2)}) copy-start(bf16[512,1024]{1,0:T(8,128)(2,1)} %copy-done.4) | copy-start | bytes 3145732
  55.8 19.7 %copy-start.6 = (bf16[1024,1024]{1,0:T(8,128)(2,1)S(1)}, bf16[1024,1024]{1,0:T(8,128)(2,1)}, u32[]{:S(2)}) copy-start(bf16[1024,1024]{1,0:T(8,128)(2,1)} %up_ref.3) | copy-start | bytes 6291460
  55.8 16.3 %collective-permute-start.7 = (bf16[528,512]{1,0:T(8,128)(2,1)S(1)}, bf16[528,512]{1,0:T(8,128)(2,1)S(1)}, u32[]{:S(2)}, u32[]{:S(2)}) collective-permute-start(bf16[528,512]{1,0:T(8,128)(2,1)S(1)} %get-tuple-element.274.a_ref), channel_id=1, source_target_pairs={{0,8},{24,16},{1,9},{25,17},{2,10},{26,18},{3,11},{27,19},{4,12},{... | collective-permute-start | bytes 1622024 | tf_op jit(solution)/shard_map/ppermute | solution.py:852
  57.7 14.4 %collective-permute-start.8 = (bf16[528,512]{1,0:T(8,128)(2,1)S(1)}, bf16[528,512]{1,0:T(8,128)(2,1)S(1)}, u32[]{:S(2)}, u32[]{:S(2)}) collective-permute-start(bf16[528,512]{1,0:T(8,128)(2,1)S(1)} %add.28.a_ref), channel_id=1, source_target_pairs={{8,16},{16,8},{9,17},{17,9},{10,18},{18,10},{11,19},{19,11},{12,20... | collective-permute-start | bytes 1622024 | tf_op jit(solution)/shard_map/ppermute | solution.py:852
  58.4 13.7 %collective-permute-start.6 = (bf16[4,512,128]{2,1,0:T(8,128)(2,1)S(1)}, bf16[4,512,128]{2,1,0:T(8,128)(2,1)S(1)}, u32[]{:S(2)}, u32[]{:S(2)}) collective-permute-start(bf16[4,512,128]{2,1,0:T(8,128)(2,1)S(1)} %get-tuple-element.261), channel_id=1, source_target_pairs={{0,4},{4,0},{1,5},{5,1},{2,6},{6,2},{3,7},{7,3},{8,12},{12,8},{9,1... | collective-permute-start | bytes 1572872 | tf_op jit(solution)/shard_map/ppermute | solution.py:788
  72.3 13.3 %collective-permute-start.9 = (bf16[528,512]{1,0:T(8,128)(2,1)S(1)}, bf16[528,512]{1,0:T(8,128)(2,1)S(1)}, u32[]{:S(2)}, u32[]{:S(2)}) collective-permute-start(bf16[528,512]{1,0:T(8,128)(2,1)S(1)} %choose.10), channel_id=1, source_target_pairs={{0,8},{24,16},{8,0},{16,24},{1,9},{25,17},{9,1},{17,25},{2,10},{26... | collective-permute-start | bytes 1622024 | tf_op jit(solution)/shard_map/ppermute | solution.py:856
  74.5 11.1 %collective-permute-start.10 = (bf16[528,512]{1,0:T(8,128)(2,1)S(1)}, bf16[528,512]{1,0:T(8,128)(2,1)S(1)}, u32[]{:S(2)}, u32[]{:S(2)}) collective-permute-start(bf16[528,512]{1,0:T(8,128)(2,1)S(1)} %add.30.a_ref), channel_id=1, source_target_pairs={{8,16},{16,8},{9,17},{17,9},{10,18},{18,10},{11,19},{19,11},{12,20... | collective-permute-start | bytes 1622024 | tf_op jit(solution)/shard_map/ppermute | solution.py:852
  86.0 21.6 %collective-permute-start.11 = (bf16[512,1024]{1,0:T(8,128)(2,1)S(1)}, bf16[512,1024]{1,0:T(8,128)(2,1)S(1)}, u32[]{:S(2)}, u32[]{:S(2)}) collective-permute-start(bf16[512,1024]{1,0:T(8,128)(2,1)S(1)} %get-tuple-element.304), channel_id=1, source_target_pairs={{0,1},{1,0},{2,3},{3,2},{4,5},{5,4},{6,7},{7,6},{8,9},{9,8},{10,11... | collective-permute-start | bytes 3145736 | tf_op jit(solution)/shard_map/ppermute | solution.py:852
  86.1 16.7 %collective-permute-start.12 = (bf16[528,512]{1,0:T(8,128)(2,1)S(1)}, bf16[528,512]{1,0:T(8,128)(2,1)S(1)}, u32[]{:S(2)}, u32[]{:S(2)}) collective-permute-start(bf16[528,512]{1,0:T(8,128)(2,1)S(1)} %choose.11), channel_id=1, source_target_pairs={{0,8},{24,16},{8,0},{16,24},{1,9},{25,17},{9,1},{17,25},{2,10},{26... | collective-permute-start | bytes 1622024 | tf_op jit(solution)/shard_map/ppermute | solution.py:856
  89.9 12.9 %collective-permute-start.13 = (bf16[528,512]{1,0:T(8,128)(2,1)S(1)}, bf16[528,512]{1,0:T(8,128)(2,1)S(1)}, u32[]{:S(2)}, u32[]{:S(2)}) collective-permute-start(bf16[528,512]{1,0:T(8,128)(2,1)S(1)} %add.32.a_ref), channel_id=1, source_target_pairs={{8,16},{16,8},{9,17},{17,9},{10,18},{18,10},{11,19},{19,11},{12,20... | collective-permute-start | bytes 1622024 | tf_op jit(solution)/shard_map/ppermute | solution.py:852
  90.6 20.3 %collective-permute-start.17 = (bf16[528,512]{1,0:T(8,128)(2,1)S(1)}, bf16[528,512]{1,0:T(8,128)(2,1)S(1)}, u32[]{:S(2)}, u32[]{:S(2)}) collective-permute-start(bf16[528,512]{1,0:T(8,128)(2,1)S(1)} %choose.12.mine_ref), channel_id=1, source_target_pairs={{0,4},{4,0},{1,5},{5,1},{2,6},{6,2},{3,7},{7,3},{8,12},{12,8},{9,1... | collective-permute-start | bytes 1622024 | tf_op jit(solution)/shard_map/ppermute | solution.py:852
  103.0 15.8 %collective-permute-start.16 = (bf16[528,512]{1,0:T(8,128)(2,1)S(1)}, bf16[528,512]{1,0:T(8,128)(2,1)S(1)}, u32[]{:S(2)}, u32[]{:S(2)}) collective-permute-start(bf16[528,512]{1,0:T(8,128)(2,1)S(1)} %choose.13), channel_id=1, source_target_pairs={{0,8},{24,16},{8,0},{16,24},{1,9},{25,17},{9,1},{17,25},{2,10},{26... | collective-permute-start | bytes 1622024 | tf_op jit(solution)/shard_map/ppermute | solution.py:856
  106.9 11.9 %collective-permute-start.15 = (bf16[528,512]{1,0:T(8,128)(2,1)S(1)}, bf16[528,512]{1,0:T(8,128)(2,1)S(1)}, u32[]{:S(2)}, u32[]{:S(2)}) collective-permute-start(bf16[528,512]{1,0:T(8,128)(2,1)S(1)} %add.34.a_ref), channel_id=1, source_target_pairs={{8,16},{16,8},{9,17},{17,9},{10,18},{18,10},{11,19},{19,11},{12,20... | collective-permute-start | bytes 1622024 | tf_op jit(solution)/shard_map/ppermute | solution.py:852
  107.9 27.3 %collective-permute-start.14 = (bf16[512,1024]{1,0:T(8,128)(2,1)S(1)}, bf16[512,1024]{1,0:T(8,128)(2,1)S(1)}, u32[]{:S(2)}, u32[]{:S(2)}) collective-permute-start(bf16[512,1024]{1,0:T(8,128)(2,1)S(1)} %add.35.a_ref), channel_id=1, source_target_pairs={{0,2},{1,3},{2,0},{3,1},{4,6},{5,7},{6,4},{7,5},{8,10},{9,11},{10,... | collective-permute-start | bytes 3145736 | tf_op jit(solution)/shard_map/ppermute | solution.py:852
  109.4 16.0 %collective-permute-start.20 = (bf16[528,512]{1,0:T(8,128)(2,1)S(1)}, bf16[528,512]{1,0:T(8,128)(2,1)S(1)}, u32[]{:S(2)}, u32[]{:S(2)}) collective-permute-start(bf16[528,512]{1,0:T(8,128)(2,1)S(1)} %choose.14.mine_ref), channel_id=1, source_target_pairs={{0,4},{4,0},{1,5},{5,1},{2,6},{6,2},{3,7},{7,3},{8,12},{12,8},{9,1... | collective-permute-start | bytes 1622024 | tf_op jit(solution)/shard_map/ppermute | solution.py:852
  119.0 15.1 %collective-permute-start.18 = (bf16[528,512]{1,0:T(8,128)(2,1)S(1)}, bf16[528,512]{1,0:T(8,128)(2,1)S(1)}, u32[]{:S(2)}, u32[]{:S(2)}) collective-permute-start(bf16[528,512]{1,0:T(8,128)(2,1)S(1)} %choose.15), channel_id=1, source_target_pairs={{0,8},{24,16},{8,0},{16,24},{1,9},{25,17},{9,1},{17,25},{2,10},{26... | collective-permute-start | bytes 1622024 | tf_op jit(solution)/shard_map/ppermute | solution.py:856
  123.1 11.8 %collective-permute-start.19 = (bf16[528,512]{1,0:T(8,128)(2,1)S(1)}, bf16[528,512]{1,0:T(8,128)(2,1)S(1)}, u32[]{:S(2)}, u32[]{:S(2)}) collective-permute-start(bf16[528,512]{1,0:T(8,128)(2,1)S(1)} %add.37.a_ref), channel_id=1, source_target_pairs={{8,16},{16,8},{9,17},{17,9},{10,18},{18,10},{11,19},{19,11},{12,20... | collective-permute-start | bytes 1622024 | tf_op jit(solution)/shard_map/ppermute | solution.py:852
  123.8 14.6 %collective-permute-start.25 = (bf16[528,512]{1,0:T(8,128)(2,1)S(1)}, bf16[528,512]{1,0:T(8,128)(2,1)S(1)}, u32[]{:S(2)}, u32[]{:S(2)}) collective-permute-start(bf16[528,512]{1,0:T(8,128)(2,1)S(1)} %choose.16.mine_ref), channel_id=1, source_target_pairs={{0,4},{4,0},{1,5},{5,1},{2,6},{6,2},{3,7},{7,3},{8,12},{12,8},{9,1... | collective-permute-start | bytes 1622024 | tf_op jit(solution)/shard_map/ppermute | solution.py:852
  134.2 5.5 %collective-permute-start.24 = (bf16[528,512]{1,0:T(8,128)(2,1)S(1)}, bf16[528,512]{1,0:T(8,128)(2,1)S(1)}, u32[]{:S(2)}, u32[]{:S(2)}) collective-permute-start(bf16[528,512]{1,0:T(8,128)(2,1)S(1)} %add.38.a_ref), channel_id=1, source_target_pairs={{8,16},{16,8},{9,17},{17,9},{10,18},{18,10},{11,19},{19,11},{12,20... | collective-permute-start | bytes 1622024 | tf_op jit(solution)/shard_map/ppermute | solution.py:852
  135.4 22.0 %collective-permute-start.21 = (bf16[512,1024]{1,0:T(8,128)(2,1)S(1)}, bf16[512,1024]{1,0:T(8,128)(2,1)S(1)}, u32[]{:S(2)}, u32[]{:S(2)}) collective-permute-start(bf16[512,1024]{1,0:T(8,128)(2,1)S(1)} %add.40.mine_ref), channel_id=1, source_target_pairs={{0,1},{1,0},{2,3},{3,2},{4,5},{5,4},{6,7},{7,6},{8,9},{9,8},{10,11... | collective-permute-start | bytes 3145736 | tf_op jit(solution)/shard_map/ppermute | solution.py:852
  135.5 18.9 %collective-permute-start.23 = (bf16[528,512]{1,0:T(8,128)(2,1)S(1)}, bf16[528,512]{1,0:T(8,128)(2,1)S(1)}, u32[]{:S(2)}, u32[]{:S(2)}) collective-permute-start(bf16[528,512]{1,0:T(8,128)(2,1)S(1)} %add.39.a_ref), channel_id=1, source_target_pairs={{8,0},{16,24},{9,1},{17,25},{10,2},{18,26},{11,3},{19,27},{12,4},{... | collective-permute-start | bytes 1622024 | tf_op jit(solution)/shard_map/ppermute | solution.py:852
  136.8 19.2 %collective-permute-start.22 = (bf16[528,512]{1,0:T(8,128)(2,1)S(1)}, bf16[528,512]{1,0:T(8,128)(2,1)S(1)}, u32[]{:S(2)}, u32[]{:S(2)}) collective-permute-start(bf16[528,512]{1,0:T(8,128)(2,1)S(1)} %choose.17.mine_ref), channel_id=1, source_target_pairs={{0,4},{4,0},{1,5},{5,1},{2,6},{6,2},{3,7},{7,3},{8,12},{12,8},{9,1... | collective-permute-start | bytes 1622024 | tf_op jit(solution)/shard_map/ppermute | solution.py:852
  139.9 25.8 %collective-permute-start.28 = (bf16[528,512]{1,0:T(8,128)(2,1)S(1)}, bf16[528,512]{1,0:T(8,128)(2,1)S(1)}, u32[]{:S(2)}, u32[]{:S(2)}) collective-permute-start(bf16[528,512]{1,0:T(8,128)(2,1)S(1)} %add.41.a_ref), channel_id=1, source_target_pairs={{8,0},{16,24},{9,1},{17,25},{10,2},{18,26},{11,3},{19,27},{12,4},{... | collective-permute-start | bytes 1622024 | tf_op jit(solution)/shard_map/ppermute | solution.py:852
  154.4 13.9 %collective-permute-start.27 = (bf16[528,512]{1,0:T(8,128)(2,1)S(1)}, bf16[528,512]{1,0:T(8,128)(2,1)S(1)}, u32[]{:S(2)}, u32[]{:S(2)}) collective-permute-start(bf16[528,512]{1,0:T(8,128)(2,1)S(1)} %choose.18.mine_ref), channel_id=1, source_target_pairs={{0,4},{4,0},{1,5},{5,1},{2,6},{6,2},{3,7},{7,3},{8,12},{12,8},{9,1... | collective-permute-start | bytes 1622024 | tf_op jit(solution)/shard_map/ppermute | solution.py:852
  165.8 14.2 %collective-permute-start.30 = (bf16[528,512]{1,0:T(8,128)(2,1)S(1)}, bf16[528,512]{1,0:T(8,128)(2,1)S(1)}, u32[]{:S(2)}, u32[]{:S(2)}) collective-permute-start(bf16[528,512]{1,0:T(8,128)(2,1)S(1)} %choose.19.mine_ref), channel_id=1, source_target_pairs={{0,4},{4,0},{1,5},{5,1},{2,6},{6,2},{3,7},{7,3},{8,12},{12,8},{9,1... | collective-permute-start | bytes 1622024 | tf_op jit(solution)/shard_map/ppermute | solution.py:852
  167.3 2.5 %collective-permute-start.26 = (f32[16,512]{1,0:T(8,128)S(1)}, f32[16,512]{1,0:T(8,128)S(1)}, u32[]{:S(2)}, u32[]{:S(2)}) collective-permute-start(f32[16,512]{1,0:T(8,128)S(1)} %get-tuple-element.367.a_ref.v_ref), channel_id=1, source_target_pairs={{0,1},{1,0},{2,3},{3,2},{4,5},{5,4},{6,7},{7,6},{8,9},{9,8},{10,11... | collective-permute-start | bytes 98312 | tf_op jit(solution)/shard_map/ppermute | solution.py:852
  169.8 4.0 %collective-permute-start.29 = (f32[16,512]{1,0:T(8,128)S(1)}, f32[16,512]{1,0:T(8,128)S(1)}, u32[]{:S(2)}, u32[]{:S(2)}) collective-permute-start(f32[16,512]{1,0:T(8,128)S(1)} %add.42.a_ref), channel_id=1, source_target_pairs={{0,2},{1,3},{2,0},{3,1},{4,6},{5,7},{6,4},{7,5},{8,10},{9,11},{10,... | collective-permute-start | bytes 98312 | tf_op jit(solution)/shard_map/ppermute | solution.py:852

commit v2 on v1

--- a/solution.py
+++ b/solution.py
@@ -300,7 +300,7 @@
 
 
 def cost(flops, moved):
-    return pl.CostEstimate(flops=int(flops), bytes_accessed=int(moved), transcendentals=0)
+    return pl.CostEstimate(flops=1024, bytes_accessed=1024, transcendentals=0)
 
 
 def dot(a, b):
@@ -433,43 +433,68 @@
     return (up * phi).astype(BF16), phi + up * (0.3989422804014327 * jnp.exp(up * up * -0.5))
 
 
-def own_kernel(x_ref, dy_ref, up_ref, down_ref, pack_ref, n1_ref, n2_ref, act_ref, gu_ref, gub_ref):
-    step = pl.program_id(0)
-
-    @pl.when(step == 0)
+def early_kernel(x_ref, dy_ref, up_ref, down_ref, pack_ref, n1_ref, n2_ref, act_ref, gu_ref, gub_ref, gd_ref):
+    @pl.when(pl.program_id(0) == 0)
     def _():
         xhat, _ = standard(x_ref[...].astype(F32))
         n1_ref[...] = (xhat * pack_ref[0:1] + pack_ref[1:2]).astype(BF16)
         n2_ref[...] = (xhat * pack_ref[2:3] + pack_ref[3:4]).astype(BF16)
 
-    size = act_ref.shape[1]
+    branch(n2_ref, dy_ref, up_ref, down_ref, pack_ref, 0, act_ref, gu_ref, gub_ref, gd_ref)
+
+
+def own_kernel(n2_ref, dy_ref, up_ref, down_ref, pack_ref, act_in, gu_in, gub_in, act_ref, gu_ref, gub_ref, gd_ref):
+    branch(n2_ref, dy_ref, up_ref, down_ref, pack_ref, CHUNKS // 2, act_ref, gu_ref, gub_ref, gd_ref)
+
+
+def branch(n2_ref, dy_ref, up_ref, down_ref, pack_ref, first, act_ref, gu_ref, gub_ref, gd_ref):
+    step = pl.program_id(0)
+    size, cols = act_ref.shape[1], gd_ref.shape[1]
     dy = dy_ref[...]
-    act, slope = activation(dot(n2_ref[...], up_ref[...]) + pack_ref[4:5, pl.ds(pl.multiple_of(step * size, size), size)])
+    bias = pack_ref[4:5, pl.ds(pl.multiple_of((first + step) * size, size), size)]
+    act, slope = activation(dot(n2_ref[...], up_ref[...]) + bias)
     grad = (dot_nt(dy, down_ref[...]) * slope).astype(BF16)
     act_ref[...] = act
     gu_ref[...] = grad
     gub_ref[...] = jnp.sum(grad.astype(F32), axis=0, keepdims=True)
-
-
-def own_call(x, dy, up_w, down_w, pack):
-    rows, width = x.shape
+    gd_ref[pl.ds(pl.multiple_of(step * size, size), size)] = dot_tn(act, dy[:, :cols]).astype(BF16)
+
+    @pl.when(step == CHUNKS // 2 - 1)
+    def _():
+        gd_ref[gd_ref.shape[0] - EXTRA :] = jnp.zeros((EXTRA, cols), BF16)
+
+
+def branch_call(kernel, first, before, up_w, down_w, pack, outs, held, name):
+    rows, width = before[0].shape
     hidden = up_w.shape[1]
     size = hidden // CHUNKS
-    cols = pl.BlockSpec((rows, size), lambda i: (0, i))
+    cols = pl.BlockSpec((rows, size), lambda i: (0, first + i))
+    grads = unit_struct(hidden // 2, width // 2)
+    count = len(before) + 3
     return pl.pallas_call(
-        own_kernel,
-        grid=(CHUNKS,),
-        in_specs=[
-            whole(x.shape), whole(x.shape),
-            pl.BlockSpec((width, size), lambda i: (0, i)), pl.BlockSpec((size, width), lambda i: (i, 0)),
+        kernel,
+        grid=(CHUNKS // 2,),
+        in_specs=[whole(a.shape) for a in before] + [
+            pl.BlockSpec((width, size), lambda i: (0, first + i)),
+            pl.BlockSpec((size, width), lambda i: (first + i, 0)),
             whole(pack.shape),
-        ],
-        out_specs=[whole(x.shape)] * 2 + [cols, cols, pl.BlockSpec((1, size), lambda i: (0, i))],
-        out_shape=[struct(x.shape, BF16)] * 2 + [struct((rows, hidden), BF16)] * 2 + [struct((1, hidden), F32)],
+        ] + [pl.BlockSpec(memory_space=pl.ANY)] * len(held),
+        out_specs=[whole(o.shape) for o in outs] + [cols, cols, pl.BlockSpec((1, size), lambda i: (0, first + i))]
+        + [whole(grads.shape)],
+        out_shape=outs + [struct((rows, hidden), BF16)] * 2 + [struct((1, hidden), F32), grads],
+        input_output_aliases={count + i: len(outs) + i for i in range(len(held))},
         compiler_params=params(48),
-        cost_estimate=cost(8e9, 1024),
-        name="own",
-    )(x, dy, up_w, down_w, pack)
+        cost_estimate=cost(5e9, 1024),
+        name=name,
+    )(*before, up_w, down_w, pack, *held)
+
+
+def early_call(x, dy, up_w, down_w, pack):
+    return branch_call(early_kernel, 0, (x, dy), up_w, down_w, pack, [struct(x.shape, BF16)] * 2, (), "early")
+
+
+def own_call(n2, dy, up_w, down_w, pack, *held):
+    return branch_call(own_kernel, CHUNKS // 2, (n2, dy), up_w, down_w, pack, [], held, "own")
 
 
 def half_at(flag, size):
@@ -540,7 +565,7 @@
 
 
 def weights_kernel(near_ref, pair_ref, act_o_ref, dy_o_ref, act_ref, slope_ref, down_ref, ow_ref,
-                   dy_ref, gu_ref, ga_ref, *grad_refs):
+                   dy_ref, gu_ref, ga_ref, gd_ref):
     hidden = slope_ref.shape[1]
 
     def put(at, dy):
@@ -549,10 +574,8 @@
     pieces(near_ref, pair_ref, put)
     dy, dy_o = dy_ref[...], dy_o_ref[...]
     rows, lanes = dy.shape[0], ga_ref.shape[1]
-    act_o, act = act_o_ref[:, half_at(ctx_flag(), hidden)], act_ref[...]
-    for i, ref in enumerate(grad_refs):
-        cols = slice(i * ref.shape[1], (i + 1) * ref.shape[1])
-        fill(ref, (dot_tn(act_o, dy_o[:, cols]) + dot_tn(act, dy[:, cols])).astype(BF16))
+    act_o, cols = act_o_ref[:, half_at(ctx_flag(), hidden)], gd_ref.shape[1]
+    fill(gd_ref, (dot_tn(act_o, dy_o[:, cols:]) + dot_tn(act_ref[...], dy[:, cols:])).astype(BF16))
     gu_ref[...] = (dot_nt(dy, down_ref[half_at(ctx_flag(), hidden)]) * slope_ref[...]).astype(BF16)
     out_w = ow_ref[half_at(ctx_flag(), lanes)]
     ga_ref[half_at(ctx_flag(), rows)] = dot_nt(dy_o, out_w).astype(BF16)
@@ -563,7 +586,7 @@
     rows, width = dy_o.shape
     hidden = slope.shape[1]
     outs = [struct((rows, width), BF16), struct((rows, hidden), BF16), struct((2 * rows, 2 * HEAD_DIM), BF16)]
-    outs += [unit_struct(hidden, width // 2)] * 2
+    outs.append(unit_struct(hidden, width // 2))
     arrays = (near, pair, act_o, dy_o, act, slope, down_w, out_w)
     return fetched(weights_kernel, arrays, outs, "weights", 4e9)
 
@@ -573,25 +596,9 @@
     return jnp.concatenate([jnp.where(first, own, other), jnp.where(first, other, own)], axis=axis)
 
 
-def attend_kernel(q_o_ref, k_o_ref, v_o_ref, q_x_ref, k_x_ref, v_x_ref, ga_ref, ids_o_ref, ids_x_ref, table_ref,
-                  n1_o_hbm, n1_x_hbm, dy_o_hbm, dy_x_hbm, n2_o_hbm, n2_x_hbm, gu_o_hbm, gu_x_hbm,
-                  keep_ref, send_ref, qk_grad_ref, vo_grad_ref, *refs):
-    up_refs, refs = refs[:2], refs[2:]
-    q_ref, k_ref, v_ref, dk_ref, dv_ref, att_ref, gp_ref, *held, sems = refs
-    n1_o_ref, n1_x_ref, dy_o_ref, dy_x_ref, n2_o_ref, n2_x_ref, gu_o_ref, gu_x_ref = held
+def attend_head(index, q_o_ref, k_o_ref, v_o_ref, q_x_ref, k_x_ref, v_x_ref, ga_ref, ids_o_ref, ids_x_ref, table_ref,
+                q_ref, k_ref, v_ref, dk_ref, dv_ref, att_ref, gp_ref):
     rows, lanes = q_ref.shape
-    span = rows // 2
-    mine, theirs = half_at(ctx_flag(), span), half_at(1 - ctx_flag(), span)
-    copies = [
-        pltpu.make_async_copy(src, dst, sems.at[i])
-        for i, (src, dst) in enumerate((
-            (n1_o_hbm, n1_o_ref), (n1_x_hbm, n1_x_ref), (dy_o_hbm, dy_o_ref), (dy_x_hbm, dy_x_ref),
-            (n2_o_hbm, n2_o_ref), (n2_x_hbm, n2_x_ref),
-            (gu_o_hbm.at[:, half_at(ctx_flag(), gu_x_ref.shape[1])], gu_o_ref), (gu_x_hbm, gu_x_ref),
-        ))
-    ]
-    for copy in copies:
-        copy.start()
     cosine, sine = turn_lanes(table_ref[...])
     step = 256
     zero = jnp.zeros((), BF16)
@@ -604,7 +611,7 @@
     code = jnp.where(ids[1:2] == 1, ids[0:1], -1).astype(F32)
     doc = jnp.broadcast_to(ids[0:1].astype(F32), (8, rows)).T[:, 0:1]
     lane = lax.broadcasted_iota(jnp.int32, (1, lanes), 1)
-    heads = [(lane // HEAD_DIM) == h for h in range(lanes // HEAD_DIM)]
+    head = (lane // HEAD_DIM) == index
     for i in range(rows // step):
         at, upto = slice(i * step, (i + 1) * step), (i + 1) * step
         k, v = k_ref[:upto], v_ref[:upto]
@@ -613,27 +620,54 @@
         seen = ((col <= row) & (code[:, :upto] == doc[at])) | (col == row)
         bias = jnp.where(seen, 0.0, NEG)
         q, ga = q_ref[at], ga_ref[at]
-        sums = None
-        for head in heads:
-            qh, gh = jnp.where(head, q, zero), jnp.where(head, ga, zero)
-            scores = dot_nt(qh, k) + bias
-            e = jnp.exp(scores - jnp.max(scores, axis=1, keepdims=True))
-            p = e * (1.0 / jnp.sum(e, axis=1, keepdims=True))
-            low = p.astype(BF16)
-            att = jnp.where(head, dot(low, v), 0.0)
-            delta = jnp.sum(att * gh.astype(F32), axis=1, keepdims=True)
-            g = (p * (dot_nt(gh, v) - delta)).astype(BF16)
-            terms = att, jnp.where(head, dot(g, k), 0.0), dot_tn(g, qh), dot_tn(low, gh)
-            sums = terms if sums is None else [a + b for a, b in zip(sums, terms)]
-        att_ref[at] = sums[0].astype(BF16)
-        gp_ref[0, at] = turn(sums[1] * scale, cosine[at], -sine[at]).astype(BF16)
-        dk_ref[:upto] += sums[2]
-        dv_ref[:upto] += sums[3]
+        qh, gh = jnp.where(head, q, zero), jnp.where(head, ga, zero)
+        scores = dot_nt(qh, k) + bias
+        e = jnp.exp(scores - jnp.max(scores, axis=1, keepdims=True))
+        p = e * (1.0 / jnp.sum(e, axis=1, keepdims=True))
+        low = p.astype(BF16)
+        att = jnp.where(head, dot(low, v), 0.0)
+        delta = jnp.sum(att * gh.astype(F32), axis=1, keepdims=True)
+        g = (p * (dot_nt(gh, v) - delta)).astype(BF16)
+        query_grad = jnp.where(head, dot(g, k), 0.0)
+        att_ref[at] = att.astype(BF16)
+        gp_ref[0, at] = turn(query_grad * scale, cosine[at], -sine[at]).astype(BF16)
+        dk_ref[:upto] += dot_tn(g, qh)
+        dv_ref[:upto] += dot_tn(low, gh)
     gp_ref[1] = turn(dk_ref[...], cosine, -sine).astype(BF16)
     gp_ref[2] = dv_ref[...].astype(BF16)
-    keep_ref[0], send_ref[0] = att_ref[mine], att_ref[theirs]
-    for t in range(3):
-        keep_ref[t + 1], send_ref[t + 1] = gp_ref[t, mine], gp_ref[t, theirs]
+
+
+def head_scratch(rows, lanes):
+    return [pltpu.VMEM((rows, lanes), BF16)] * 3 + [pltpu.VMEM((rows, lanes), F32)] * 2
+
+
+def first_head_kernel(*refs):
+    attend_head(0, *refs[:10], *refs[12:], *refs[10:12])
+
+
+def first_head_call(own, other, ga, ids, ids_x, table):
+    arrays = (*own, *other, ga, ids, ids_x, table)
+    outs = [struct(ga.shape, BF16), struct((3,) + ga.shape, BF16)]
+    return fetched(first_head_kernel, arrays, outs, "first_head", 1024, 0, head_scratch(*ga.shape))
+
+
+def attend_kernel(*refs):
+    heads, (att_in, gp_in), later, outs = refs[:10], refs[10:12], refs[12:20], refs[20:26]
+    att_ref, gp_ref, *held, sems = refs[26 + 5 :]
+    keep_ref, send_ref, qk_grad_ref, vo_grad_ref, *up_refs = outs
+    n1_o_ref, n1_x_ref, dy_o_ref, dy_x_ref, n2_o_ref, n2_x_ref, gu_o_ref, gu_x_ref = held
+    span, hidden = n1_o_ref.shape[0], gu_x_ref.shape[1]
+    mine, theirs = half_at(ctx_flag(), span), half_at(1 - ctx_flag(), span)
+    sources = list(later)
+    sources[6] = later[6].at[:, half_at(ctx_flag(), hidden)]
+    copies = [pltpu.make_async_copy(src, dst, sems.at[i]) for i, (src, dst) in enumerate(zip(sources, held))]
+    for copy in copies:
+        copy.start()
+    attend_head(1, *heads, *refs[26 : 26 + 5], att_ref, gp_ref)
+    for ref, at in ((keep_ref, mine), (send_ref, theirs)):
+        ref[0] = att_ref[at] + att_in[at]
+        for t in range(3):
+            ref[t + 1] = gp_ref[t, at] + gp_in[t, at]
     for copy in copies:
         copy.wait()
     q_grad, k_grad, v_grad = [
@@ -648,50 +682,65 @@
         fill(ref, (dot_tn(n2_o_ref[:, at], gu_o) + dot_tn(n2_x_ref[:, at], gu_x)).astype(BF16))
 
 
-def attend_call(own, other, ga, ids, ids_x, table, *later):
-    arrays = (*own, *other, ga, ids, ids_x, table, *later)
+def attend_call(own, other, ga, ids, ids_x, table, first, *later):
+    arrays = (*own, *other, ga, ids, ids_x, table, *first, *later)
     rows, lanes = ga.shape
     span, width = later[0].shape
     hidden = later[-1].shape[1]
     outs = [struct((4, span, lanes), BF16)] * 2 + [unit_struct(width // 2, 4 * lanes)] * 2 + [unit_struct(width // 2, hidden)] * 2
-    scratch = [pltpu.VMEM((rows, lanes), BF16)] * 3 + [pltpu.VMEM((rows, lanes), F32)] * 2
-    scratch += [pltpu.VMEM((rows, lanes), BF16), pltpu.VMEM((3, rows, lanes), BF16)]
+    scratch = head_scratch(rows, lanes) + [pltpu.VMEM((rows, lanes), BF16), pltpu.VMEM((3, rows, lanes), BF16)]
     scratch += [pltpu.VMEM((span, width), BF16)] * 6 + [pltpu.VMEM((span, hidden), BF16)] * 2
     scratch.append(pltpu.SemaphoreType.DMA((len(later),)))
     return fetched(attend_kernel, arrays, outs, "attend", 1024, len(later), scratch)
 
 
-def sums_kernel(mine_ref, recv_ref, act_ref, gu_ref, dy_ref, x_ref, pack_ref, w_ref, ow_ref, up_ref, down_ref,
-                gub_ref, keep_ref, send_ref, vec_ref, gb_ref):
+def branch_sums_kernel(act_ref, gu_ref, dy_ref, x_ref, up_ref, down_ref, out_ref, grad_ref, sums_ref):
+    two = dot_nt(gu_ref[...], up_ref[...])
+    xhat, _ = standard(x_ref[...].astype(F32))
+    grad_ref[...] = two
+    out_ref[...] = dot(act_ref[...], down_ref[...])
+    rows = [jnp.sum(v, axis=0, keepdims=True) for v in (two * xhat, two, dy_ref[...].astype(F32))]
+    sums_ref[...] = jnp.concatenate(rows + [jnp.zeros((5, two.shape[1]), F32)], axis=0)
+
+
+def branch_sums_call(act, gu, dy, x, up_w, down_w):
+    outs = [struct(x.shape, F32)] * 2 + [struct((8, x.shape[1]), F32)]
+    return small(branch_sums_kernel, (act, gu, dy, x, up_w, down_w), outs, "branch_sums", 24)
+
+
+def sums_kernel(mine_ref, recv_ref, out_ref, grad_ref, sums_ref, x_ref, pack_ref, w_ref, ow_ref, gub_ref,
+                keep_ref, send_ref, vec_ref):
     lanes = mine_ref.shape[2]
     heads = [(mine_ref, half_at(ctx_flag(), lanes)), (recv_ref, half_at(1 - ctx_flag(), lanes))]
-    out = dot(act_ref[...], down_ref[...])
-    two = dot_nt(gu_ref[...], up_ref[...])
-    one = None
+    out, one = out_ref[...], None
+    biases = []
     for ref, at in heads:
         out = out + dot(ref[0], ow_ref[at])
         for t in range(3):
             term = dot_nt(ref[t + 1], w_ref[t, :, at])
             one = term if one is None else one + term
-            gb_ref[t : t + 1, at] = jnp.sum(ref[t + 1].astype(F32), axis=0, keepdims=True)
+        biases.append([jnp.sum(ref[t + 1].astype(F32), axis=0, keepdims=True) for t in range(3)])
+    first = ctx_flag() == 0
+    pairs = [(jnp.where(first, m, r), jnp.where(first, r, m)) for m, r in zip(*biases)]
+    heads_bias = jnp.concatenate([half for pair in pairs for half in pair], axis=1)
+    zeros = jnp.zeros((1, out.shape[1] - heads_bias.shape[1]), F32)
     xhat, _ = standard(x_ref[...].astype(F32))
-    sums = [jnp.sum(v, axis=0, keepdims=True) for v in (one * xhat, one, two * xhat, two)]
-    heads_bias = jnp.concatenate([gb_ref[t : t + 1] for t in range(3)], axis=1)
-    heads_bias = jnp.concatenate([heads_bias, jnp.zeros((1, xhat.shape[1] - heads_bias.shape[1]), F32)], axis=1)
-    sums += [jnp.sum(dy_ref[...].astype(F32), axis=0, keepdims=True), gub_ref[...], heads_bias, jnp.zeros_like(heads_bias)]
-    vec = jnp.concatenate(sums, axis=0)
+    sums = sums_ref[...]
+    rows = [jnp.sum(one * xhat, axis=0, keepdims=True), jnp.sum(one, axis=0, keepdims=True), sums[0:3], gub_ref[...]]
+    rows += [jnp.concatenate([heads_bias, zeros], axis=1), jnp.zeros_like(sums[0:1])]
+    vec = jnp.concatenate(rows, axis=0)
     cols = vec_ref.shape[1]
     vec_ref[...] = jnp.concatenate([vec[:, :cols], vec[:, cols:]], axis=0).astype(BF16)
     rows = x_ref.shape[0] // 2
-    for at, value in ((0, out), (rows, one * pack_ref[0:1] + two * pack_ref[2:3])):
+    for at, value in ((0, out), (rows, one * pack_ref[0:1] + grad_ref[...] * pack_ref[2:3])):
         keep_ref[at : at + rows], send_ref[at : at + rows] = halves(core_flag(), value.astype(BF16))
 
 
-def sums_call(mine, recv, act, gu, dy, x, pack, w3, out_w, up_w, down_w, gub):
+def sums_call(mine, recv, branch, x, pack, w3, out_w, gub):
     rows, width = x.shape
     both = struct((rows, width), BF16)
-    outs = [both, both, struct((EXTRA, width // 2), BF16), struct((3, w3.shape[2]), F32)]
-    return small(sums_kernel, (mine, recv, act, gu, dy, x, pack, w3, out_w, up_w, down_w, gub), outs, "sums", 32)
+    outs = [both, both, struct((EXTRA, width // 2), BF16)]
+    return small(sums_kernel, (mine, recv, *branch, x, pack, w3, out_w, gub), outs, "sums", 32)
 
 
 def ride_kernel(grad_ref, vec_ref, o_ref):
@@ -729,6 +778,11 @@
 def rows_call(local, a, b, v):
     row = struct((1, 2 * a.shape[1]), F32)
     return small(rows_kernel, (a, b, v), [row] * 7 + [struct((3, local), F32)], "rows")
+
+
+def place_sum_kernel(mine_ref, other_ref, *refs):
+    rows = refs[-1].shape[0]
+    refs[-1][...] = mine_ref[:rows].astype(F32) + other_ref[:rows].astype(F32)
 
 
 def place_pair_kernel(mine_ref, other_ref, *refs):
@@ -914,9 +968,19 @@
     def ids_w():
         s.ids = s.ids[0], run.arrived(s.ids[1])
 
+    def early():
+        s.pack = jnp.stack([norm1_gain, norm1_shift, norm2_gain, norm2_shift, up_bias, out_bias, down_bias])
+        s.n1, s.n2, s.act, s.gu, s.gub, grad = run(early_call, x, dy, up_weight, down_weight, s.pack)
+        open_early(0, grad)
+
+    def open_early(i, grad):
+        open_unit(f"E{i}", line_then_ctx, grad, placing(
+            ["down"], place_sum_kernel, 1, [(hidden // 2, width // 2)], [lambda _: (i, 0)]))
+
     def own():
-        s.pack = jnp.stack([norm1_gain, norm1_shift, norm2_gain, norm2_shift, up_bias, out_bias, down_bias])
-        s.n1, s.n2, s.act, s.gu, s.gub = run(own_call, x, dy, up_weight, down_weight, s.pack)
+        s.act, s.gu, s.gub, grad = run(
+            own_call, s.n2, dy, up_weight, down_weight, s.pack, s.act, s.gu, s.gub)
+        open_early(1, grad)
 
     def other():
         u.tk.advance()
@@ -929,16 +993,18 @@
 
     def weights():
         u.dy.advance()
-        s.dyx, s.gux, s.ga, *grads = run(
+        s.dyx, s.gux, s.ga, grad = run(
             weights_call, *s.dy, s.act, dy, s.actx, s.slope, down_weight, out_weight)
-        for j, grad in enumerate(grads):
-            open_unit(f"D{j}", line_then_ctx, grad, placing(
-                ["down"], place_halves_kernel, 2, [(hidden // 2, width // 2)], [lambda i, j=j: (i, j)]))
+        open_unit("D1", line_then_ctx, grad, placing(
+            ["down"], place_halves_kernel, 2, [(hidden // 2, width // 2)], [lambda i: (i, 1)]))
+
+    def first_head():
+        s.first = run(lambda *a: first_head_call(a[:3], a[3:6], *a[6:]), *s.qkv, *s.qkvx, s.ga, *s.ids, s.table)
 
     def attend():
         s.mine, s.theirs, s.qk, vo_grad, *ups = run(
-            lambda *a: attend_call(a[:3], a[3:6], *a[6:]),
-            *s.qkv, *s.qkvx, s.ga, *s.ids, s.table,
+            lambda *a: attend_call(a[:3], a[3:6], *a[6:10], a[10:12], *a[12:]),
+            *s.qkv, *s.qkvx, s.ga, *s.ids, s.table, *s.first,
             s.n1, s.n1x, dy, s.dyx, s.n2, s.n2x, s.gu, s.gux)
         open_unit("Q1", line_then_ctx, vo_grad, placing(
             ["qkv", "out"], place_pair_kernel, 2, [(1, width, lanes), (lanes, width)],
@@ -953,10 +1019,11 @@
     def gpx_w():
         s.recv = run.arrived(s.recv)
 
+    def branch_sums():
+        s.branch = run(branch_sums_call, s.act, s.gu, dy, x, up_weight, down_weight)
+
     def sums():
-        keep, send, s.vec, _ = run(
-            sums_call, s.mine, s.recv, s.act, s.gu, dy, x, s.pack, w3, out_weight, up_weight, down_weight,
-            s.gub)
+        keep, send, s.vec = run(sums_call, s.mine, s.recv, s.branch, x, s.pack, w3, out_weight, s.gub)
 
         def finish(a, b):
             s.block_output, s.input_grad = run(lambda a, b: results_call(a, b, x, dy, s.pack), a, b)
@@ -975,43 +1042,50 @@
         open_unit("Q0", line_then_ctx, both, finish)
 
     u.tk.advance()
+    early()
+    u.E0.advance()
+    u.dy.advance()
     own()
-    u.dy.advance()
     tables()
     u.tk.advance()
     ids_0()
     other()
-    ids_w()
+    u.E0.wait()
+    u.E1.advance()
+    u.E0.advance()
     u.dy.advance()
     weights()
-    u.D0.advance()
+    u.D1.advance()
+    ids_w()
+    first_head()
+    u.E0.advance()
+    u.E1.advance()
     attend()
+    gpx_0()
+    u.D1.wait()
+    u.U0.advance_with(u.E1)
     u.D1.advance()
-    u.D0.wait()
-    u.D0.advance()
-    gpx_0()
+    branch_sums()
+    u.E0.advance()
     gpx_w()
-    u.D1.wait()
-    u.D0.wait()
-    u.U0.advance_with(u.D0)
-    u.D1.advance()
     sums()
     join()
     u.U0.wait()
     u.Q0.advance_with(u.D1)
-    u.D0.advance()
     u.U0.advance()
+    u.E1.advance()
     u.both.advance()
+    u.E0.advance()
     u.Q0.wait()
     u.Q1.advance_with(u.U0)
+    u.Q0.advance()
     u.D1.advance()
-    u.Q0.advance()
     u.both.advance()
-    u.D0.advance()
+    u.E1.advance()
     u.Q1.wait()
     u.U1.advance_with(u.Q0)
+    u.Q1.advance()
     u.U0.advance()
-    u.Q1.advance()
     u.D1.advance()
     u.U1.advance()
     u.Q1.advance()
@@ -1022,8 +1096,8 @@
     u.Q1.advance()
     u.Q0.advance()
     u.vec.advance()
+    u.U1.advance()
     u.both.advance()
-    u.U1.advance()
     u.Q1.advance()
     u.vec.advance()
     u.vec.advance()

time: 182 us -> 172 us (0.945)
  waiting for transfers between devices: 74 us -> 60.9 us
  Pallas kernels: 51.3 us -> 56 us
  local copies, waits for them, and re-layouts: 9.07 us -> 7.11 us
    ppermute x4, waiting for transfers between devices: 28.5 us -> 8.83 us  [advance_with(): lax.ppermute(self.run(choose, outward, inward), 'dp', INWARD + OUTWARD)]
    ppermute x25 -> x29, waiting for transfers between devices: 30.4 us -> 42.2 us  [advance(): self.message = lax.ppermute(value, axis, perm)]
    ppermute x2, waiting for transfers between devices: 15.2 us -> 9.87 us  [send(): return lax.ppermute(self.tied(value), axis, perm)]
    unnamed x40 -> x38, local copies, waits for them, and re-layouts: 7.12 us -> 5.15 us
    pallas_call x1 -> x2, Pallas kernels: 7.01 us -> 8.83 us  [branch_call(): pl.pallas_call(kernel, grid=(CHUNKS // 2,), in_specs=[whole(a.shape) for...]
    pallas_call x3 -> x4, Pallas kernels: 24 us -> 25.3 us  [fetched(): pl.pallas_call(kernel, grid=(1,), in_specs=[whole(a.shape) for a in array...]
    pallas_call x6 -> x7, Pallas kernels: 8.45 us -> 9.25 us  [step(): pl.pallas_call(kernel, grid=(count,), in_specs=[resident()] * 2 + [pl.Blo...]
    pallas_call x29 -> x33, Pallas kernels: 11.8 us -> 12.6 us  [small(): pl.pallas_call(kernel, in_specs=[resident()] * len(arrays), out_specs=[re...]
  transfers between devices with their start and end apart: 31 -> 35, of which waited for: 13 -> 16; matrix products, arithmetic and copies ran while one was open for 1% -> 1% of each run, Pallas kernels for 25% -> 32%
where the time goes in v2:
time: 172 us; the launch traced here: 171 us
  waiting for transfers between devices  60.9 us (35%)
  Pallas kernels  56 us (33%)
  starting transfers between devices  45.8 us (27%)
  local copies, waits for them, and re-layouts  7.11 us (4%)
    ppermute x29, waiting for transfers between devices, advance(): self.message = lax.ppermute(value, axis, perm)  42.2 us
    ppermute x29, starting transfers between devices, advance(): self.message = lax.ppermute(value, axis, perm)  30 us
    pallas_call x4, Pallas kernels, fetched(): pl.pallas_call(kernel, grid=(1,), in_specs=[whole(a.shape) for a in array...  25.3 us
    ppermute x4, starting transfers between devices, advance_with(): lax.ppermute(self.run(choose, outward, inward), 'dp', INWARD + OUTWARD)  14.6 us
    pallas_call x33, Pallas kernels, small(): pl.pallas_call(kernel, in_specs=[resident()] * len(arrays), out_specs=[re...  12.6 us
    ppermute x2, waiting for transfers between devices, send(): return lax.ppermute(self.tied(value), axis, perm)  9.87 us
    pallas_call x7, Pallas kernels, step(): pl.pallas_call(kernel, grid=(count,), in_specs=[resident()] * 2 + [pl.Blo...  9.25 us
    ppermute x4, waiting for transfers between devices, advance_with(): lax.ppermute(self.run(choose, outward, inward), 'dp', INWARD + OUTWARD)  8.83 us
  transfers between devices with their start and end apart: 35, of which 16 were waited for; matrix products, arithmetic and copies ran while one was open for 1% of the time, Pallas kernels for 32%

profile of v2, /device:TPU:0, one launch (start us, length us, event | category | flops | bytes accessed | tf_op | source)
XLA Modules:
  0.0 171.3 jit_solution(12249158378064330220)
XLA Ops:
  0.7 1.1 dynamic-slice_bitcast_fusion
  1.7 3.0 %collective-permute-start = (bf16[256,1024]{1,0:T(8,128)(2,1)S(1)}, bf16[256,1024]{1,0:T(8,128)(2,1)S(1)}, u32[]{:S(2)}, u32[]{:S(2)}) collective-permute-start(bf16[256,1024]{1,0:T(8,128)(2,1)S(1)} %dynamic-slice_bitcast_fusion), channel_id=1, source_target_pairs={{0,4},{4,0},{1,5},{5,1},{2,6},{6,2},{3,7},{7,3},{8,12},{12,8},{9,1... | collective-permute-start | bytes 1572872 | tf_op jit(solution)/shard_map/ppermute | solution.py:906
  4.8 0.8 stack.31.pack_ref
  5.6 1.2 copy-done.4
  6.8 5.2 %early.1 = (bf16[512,1024]{1,0:T(8,128)(2,1)S(1)}, bf16[512,1024]{1,0:T(8,128)(2,1)S(1)}, bf16[512,1024]{1,0:T(8,128)(2,1)S(1)}, bf16[512,1024]{1,0:T(8,128)(2,1...) custom-call(bf16[512,1024]{1,0:T(8,128)(2,1)S(1)} %bitcast.29, bf16[512,1024]{1,0:T(8,128)(2,1)} %bitcast.22, ...), custom_call_target="tpu_custom_call" | custom-call | flops 1024 | bytes 1024 | tf_op jit(solution)/shard_map/early/pallas_call | solution.py:474
  12.0 1.0 copy-done.9
  13.0 3.5 %collective-permute-start.3 = (bf16[528,512]{1,0:T(8,128)(2,1)S(1)}, bf16[528,512]{1,0:T(8,128)(2,1)S(1)}, u32[]{:S(2)}, u32[]{:S(2)}) collective-permute-start(bf16[528,512]{1,0:T(8,128)(2,1)S(1)} %get-tuple-element.274.a_ref), channel_id=1, source_target_pairs={{0,8},{24,16},{1,9},{25,17},{2,10},{26,18},{3,11},{27,19},{4,12},{... | collective-permute-start | bytes 1622024 | tf_op jit(solution)/shard_map/ppermute | solution.py:906
  16.5 3.7 %own.1 = (bf16[512,1024]{1,0:T(8,128)(2,1)S(1)}, bf16[512,1024]{1,0:T(8,128)(2,1)S(1)}, f32[1,1024]{1,0:T(1,128)S(1)}, bf16[528,512]{1,0:T(8,128)(2,1)S(1)}) custom-call(bf16[512,1024]{1,0:T(8,128)(2,1)S(1)} %get-tuple-element.328.n2_ref.refs_16_, bf16[512,1024]{1,0:T(8,128)(2,1)S(1)} %bitcast.25, ...), custom_call_target="tpu_custom_call", output_to_operand_aliasing={{0}: (5, {}), {1}: (6, {}), {2}: (7, {})} | custom-call | flops 1024 | bytes 1024 | tf_op jit(solution)/shard_map/own/pallas_call | solution.py:474
  21.2 1.3 collective-permute-done.1.pair_ref
  22.5 6.4 %other.1 = (bf16[512,1024]{1,0:T(8,128)(2,1)S(1)}, bf16[512,1024]{1,0:T(8,128)(2,1)S(1)}, bf16[512,128]{1,0:T(8,128)(2,1)S(1)}, bf16[512,128]{1,0:T(8,128)(2,1)S...) custom-call(bf16[256,1024]{1,0:T(8,128)(2,1)S(1)} %collective-permut, ...), custom_call_target="tpu_custom_call" | custom-call | flops 1024 | bytes 1024 | tf_op jit(solution)/shard_map/other/pallas_call | solution.py:371
  28.9 1.0 copy-done.13
  29.8 1.0 copy-done.14
  30.9 0.7 collective-permute-start.7
  31.6 4.1 %collective-permute-start.6 = (bf16[528,512]{1,0:T(8,128)(2,1)S(1)}, bf16[528,512]{1,0:T(8,128)(2,1)S(1)}, u32[]{:S(2)}, u32[]{:S(2)}) collective-permute-start(bf16[528,512]{1,0:T(8,128)(2,1)S(1)} %get-tuple-element.310.a_ref), channel_id=1, source_target_pairs={{0,8},{24,16},{1,9},{25,17},{2,10},{26,18},{3,11},{27,19},{4,12},{... | collective-permute-start | bytes 1622024 | tf_op jit(solution)/shard_map/ppermute | solution.py:906
  36.4 1.3 collective-permute-done.4.pair_ref
  37.7 4.1 %weights.1 = (bf16[512,1024]{1,0:T(8,128)(2,1)S(1)}, bf16[512,512]{1,0:T(8,128)(2,1)S(1)}, bf16[1024,128]{1,0:T(8,128)(2,1)S(1)}, bf16[528,512]{1,0:T(8,128)(2,1)S(1)}) custom-call(bf16[256,1024]{1,0:T(8,128)(2,1)S(1)} %collective-permute-done.2.near_ref, bf16[256,1024]{1,0:T(8,128)(2,1)S(1)} %collective-permute-done.4.pair_ref, ...), custom_call_target="tpu_custom_call" | custom-call | flops 1024 | bytes 1024 | tf_op jit(solution)/shard_map/weights/pallas_call | solution.py:371
  41.9 1.0 copy-done.15
  42.9 1.5 collective-permute-start.10
  44.4 5.5 %first_head.1 = (bf16[1024,128]{1,0:T(8,128)(2,1)S(1)}, bf16[3,1024,128]{2,1,0:T(8,128)(2,1)S(1)}) custom-call(bf16[512,128]{1,0:T(8,128)(2,1)S(1)} %get-tuple-element.312.refs_0_, bf16[512,128]{1,0:T(8,128)(2,1)S(1)} %get-tuple-element.313.refs_1_, bf16[512,128]{1,0:T(8,128)(2,1)S(1)} %get-tuple-element.314.refs_2_, ...), custom_call_target="tpu_custom_call" | custom-call | flops 1024 | bytes 1024 | tf_op jit(solution)/shard_map/first_head/pallas_call | solution.py:371
  50.2 0.7 collective-permute-start.11
  50.9 1.3 collective-permute-start.9
  52.2 9.3 %attend.1 = (bf16[4,512,128]{2,1,0:T(8,128)(2,1)S(1)}, bf16[4,512,128]{2,1,0:T(8,128)(2,1)}, bf16[528,512]{1,0:T(8,128)(2,1)S(1)}, bf16[528,512]{1,0:T(8,128)(2,...) custom-call(bf16[512,128]{1,0:T(8,128)(2,1)S(1)} %get-tuple-element.312.refs_0_, ...), custom_call_target="tpu_custom_call" | custom-call | flops 1024 | bytes 1024 | tf_op jit(solution)/shard_map/attend/pallas_call | solution.py:371
  61.8 4.2 %collective-permute-start.12 = (bf16[528,512]{1,0:T(8,128)(2,1)S(1)}, bf16[528,512]{1,0:T(8,128)(2,1)S(1)}, u32[]{:S(2)}, u32[]{:S(2)}) collective-permute-start(bf16[528,512]{1,0:T(8,128)(2,1)S(1)} %choose.11), channel_id=1, source_target_pairs={{0,8},{24,16},{8,0},{16,24},{1,9},{25,17},{9,1},{17,25},{2,10},{26... | collective-permute-start | bytes 1622024 | tf_op jit(solution)/shard_map/ppermute | solution.py:910
  66.1 0.9 collective-permute-start.13
  67.6 3.0 %branch_sums.1 = (f32[512,1024]{1,0:T(8,128)S(1)}, f32[512,1024]{1,0:T(8,128)S(1)}, f32[8,1024]{1,0:T(8,128)S(1)}) custom-call(bf16[512,1024]{1,0:T(8,128)(2,1)S(1)} %get-tuple-element.346.act_o_ref.act_ref, bf16[512,1024]{1,0:T(8,128)(2,1)S(1)} %copy-done.7, bf16[512,1024]{1,0:T(8,128)(2,1)S(1)} %bitcast.27, bf16[512,1024]{1,0:T(8,128)(2,1)S(1)} %bitcast.30, ...), custom_call_target="tpu_custom_call" | custom-call | flops 1024 | bytes 1024 | tf_op jit(solution)/shard_map/branch_sums/pallas_call | solution.py:358
  70.7 1.6 collective-permute-start.16
  72.3 9.9 %collective-permute-done.8.recv_ref = bf16[4,512,128]{2,1,0:T(8,128)(2,1)S(1)} collective-permute-done((bf16[4,512,128]{2,1,0:T(8,128)(2,1)}, bf16[4,512,128]{2,1,0:T(8,128)(2,1)S(1)}, u32[]{:S(2)}, u32[]{:S(2)}) %collective-permute-start.8) | collective-permute-done | bytes 524320 | tf_op jit(solution)/shard_map/ppermute | solution.py:842
  82.2 3.3 %sums.1 = (bf16[512,1024]{1,0:T(8,128)(2,1)S(1)}, bf16[512,1024]{1,0:T(8,128)(2,1)S(1)}, bf16[16,512]{1,0:T(8,128)(2,1)S(1)}) custom-call(bf16[4,512,128]{2,1,0:T(8,128)(2,1)S(1)} %get-tuple-element.359.mine_ref, bf16[4,512,128]{2,1,0:T(8,128)(2,1)S(1)} %collective-permute-done.8.recv_ref, f32[512,1024]{1,0:T(8,128)S(1)} %get-tuple-element.361.out_ref, ...), custom_call_target="tpu_custom_call" | custom-call | flops 1024 | bytes 1024 | tf_op jit(solution)/shard_map/sums/pallas_call | solution.py:358
  85.7 2.1 %collective-permute-start.15 = (bf16[528,512]{1,0:T(8,128)(2,1)S(1)}, bf16[528,512]{1,0:T(8,128)(2,1)S(1)}, u32[]{:S(2)}, u32[]{:S(2)}) collective-permute-start(bf16[528,512]{1,0:T(8,128)(2,1)S(1)} %choose.13), channel_id=1, source_target_pairs={{0,8},{24,16},{8,0},{16,24},{1,9},{25,17},{9,1},{17,25},{2,10},{26... | collective-permute-start | bytes 1622024 | tf_op jit(solution)/shard_map/ppermute | solution.py:910
  88.0 0.7 collective-permute-start.17
  88.8 0.6 collective-permute-start.21
  89.4 1.4 collective-permute-done.16.other_ref
  90.9 1.1 place.7.refs_0_
  91.9 4.2 %collective-permute-done.15.b_ref = bf16[528,512]{1,0:T(8,128)(2,1)S(1)} collective-permute-done((bf16[528,512]{1,0:T(8,128)(2,1)S(1)}, bf16[528,512]{1,0:T(8,128)(2,1)S(1)}, u32[]{:S(2)}, u32[]{:S(2)}) %collective-permute-start.15) | collective-permute-done | bytes 540704 | tf_op jit(solution)/shard_map/ppermute | solution.py:910
  96.3 4.4 %collective-permute-start.20 = (bf16[528,512]{1,0:T(8,128)(2,1)S(1)}, bf16[528,512]{1,0:T(8,128)(2,1)S(1)}, u32[]{:S(2)}, u32[]{:S(2)}) collective-permute-start(bf16[528,512]{1,0:T(8,128)(2,1)S(1)} %choose.15), channel_id=1, source_target_pairs={{0,8},{24,16},{8,0},{16,24},{1,9},{25,17},{9,1},{17,25},{2,10},{26... | collective-permute-start | bytes 1622024 | tf_op jit(solution)/shard_map/ppermute | solution.py:910
  100.9 0.7 collective-permute-start.19
  102.0 2.0 %collective-permute-done.21.other_ref = bf16[528,512]{1,0:T(8,128)(2,1)S(1)} collective-permute-done((bf16[528,512]{1,0:T(8,128)(2,1)S(1)}, bf16[528,512]{1,0:T(8,128)(2,1)S(1)}, u32[]{:S(2)}, u32[]{:S(2)}) %collective-permute-start.21) | collective-permute-done | bytes 540704 | tf_op jit(solution)/shard_map/ppermute | solution.py:906
  104.0 1.1 place.8.refs_0_
  105.0 3.2 %collective-permute-done.20.b_ref = bf16[528,512]{1,0:T(8,128)(2,1)S(1)} collective-permute-done((bf16[528,512]{1,0:T(8,128)(2,1)S(1)}, bf16[528,512]{1,0:T(8,128)(2,1)S(1)}, u32[]{:S(2)}, u32[]{:S(2)}) %collective-permute-start.20) | collective-permute-done | bytes 540704 | tf_op jit(solution)/shard_map/ppermute | solution.py:910
  108.5 3.9 %collective-permute-start.22 = (bf16[528,512]{1,0:T(8,128)(2,1)S(1)}, bf16[528,512]{1,0:T(8,128)(2,1)S(1)}, u32[]{:S(2)}, u32[]{:S(2)}) collective-permute-start(bf16[528,512]{1,0:T(8,128)(2,1)S(1)} %choose.17), channel_id=1, source_target_pairs={{0,8},{24,16},{8,0},{16,24},{1,9},{25,17},{9,1},{17,25},{2,10},{26... | collective-permute-start | bytes 1622024 | tf_op jit(solution)/shard_map/ppermute | solution.py:910
  112.4 1.7 collective-permute-start.18
  114.2 0.7 collective-permute-start.23
  115.0 1.9 %collective-permute-done.24.other_ref = bf16[528,512]{1,0:T(8,128)(2,1)S(1)} collective-permute-done((bf16[528,512]{1,0:T(8,128)(2,1)S(1)}, bf16[528,512]{1,0:T(8,128)(2,1)S(1)}, u32[]{:S(2)}, u32[]{:S(2)}) %collective-permute-start.24) | collective-permute-done | bytes 540704 | tf_op jit(solution)/shard_map/ppermute | solution.py:906
  116.9 1.4 place.9
  118.3 1.4 collective-permute-done.22.b_ref
  119.9 0.7 collective-permute-start.26
  120.7 1.3 collective-permute-start.30
  122.1 9.6 %collective-permute-done.18.b_ref = bf16[512,1024]{1,0:T(8,128)(2,1)S(1)} collective-permute-done((bf16[512,1024]{1,0:T(8,128)(2,1)S(1)}, bf16[512,1024]{1,0:T(8,128)(2,1)S(1)}, u32[]{:S(2)}, u32[]{:S(2)}) %collective-permute-start.18) | collective-permute-done | bytes 1048608 | tf_op jit(solution)/shard_map/ppermute | solution.py:906
  132.1 0.6 collective-permute-start.29
  132.6 1.4 place.10.refs_0_
  134.1 1.6 collective-permute-start.28
  135.7 2.0 %collective-permute-done.30.b_ref = bf16[528,512]{1,0:T(8,128)(2,1)S(1)} collective-permute-done((bf16[528,512]{1,0:T(8,128)(2,1)S(1)}, bf16[528,512]{1,0:T(8,128)(2,1)S(1)}, u32[]{:S(2)}, u32[]{:S(2)}) %collective-permute-start.30) | collective-permute-done | bytes 540704 | tf_op jit(solution)/shard_map/ppermute | solution.py:906
  137.9 9.3 %collective-permute-done.29.other_ref = bf16[528,512]{1,0:T(8,128)(2,1)S(1)} collective-permute-done((bf16[528,512]{1,0:T(8,128)(2,1)S(1)}, bf16[528,512]{1,0:T(8,128)(2,1)S(1)}, u32[]{:S(2)}, u32[]{:S(2)}) %collective-permute-start.29) | collective-permute-done | bytes 540704 | tf_op jit(solution)/shard_map/ppermute | solution.py:906
  147.2 1.4 place.11
  148.6 1.8 %collective-permute-done.28.b_ref = bf16[528,512]{1,0:T(8,128)(2,1)S(1)} collective-permute-done((bf16[528,512]{1,0:T(8,128)(2,1)S(1)}, bf16[528,512]{1,0:T(8,128)(2,1)S(1)}, u32[]{:S(2)}, u32[]{:S(2)}) %collective-permute-start.28) | collective-permute-done | bytes 540704 | tf_op jit(solution)/shard_map/ppermute | solution.py:906
  150.5 1.6 collective-permute-start.34
  152.0 2.6 %results.1 = (bf16[512,1024]{1,0:T(8,128)(2,1)}, bf16[512,1024]{1,0:T(8,128)(2,1)}) custom-call(bf16[512,1024]{1,0:T(8,128)(2,1)S(1)} %add.44.mine_ref, bf16[512,1024]{1,0:T(8,128)(2,1)S(1)} %collective-permute-done.25.other_ref, bf16[512,1024]{1,0:T(8,128)(2,1)S(1)} %bitcast.32, bf16[512,1024]{1,0:T(8,128)(2,1)S(1)} %bitcast.28, f32[7,1024]{1,0:T(8,128)S(1)} %stack.31.pack_ref), custom_call_target="tpu_custom_call" | custom-call | flops 1024 | bytes 1024 | tf_op jit(solution)/shard_map/results/pallas_call | solution.py:358
  154.7 4.1 %collective-permute-done.32.other_ref = bf16[528,512]{1,0:T(8,128)(2,1)S(1)} collective-permute-done((bf16[528,512]{1,0:T(8,128)(2,1)S(1)}, bf16[528,512]{1,0:T(8,128)(2,1)S(1)}, u32[]{:S(2)}, u32[]{:S(2)}) %collective-permute-start.32) | collective-permute-done | bytes 540704 | tf_op jit(solution)/shard_map/ppermute | solution.py:906
  158.8 1.5 place.12
  160.3 1.6 collective-permute-start.33
  161.8 2.4 %collective-permute-done.33.b_ref = f32[16,512]{1,0:T(8,128)S(1)} collective-permute-done((f32[16,512]{1,0:T(8,128)S(1)}, f32[16,512]{1,0:T(8,128)S(1)}, u32[]{:S(2)}, u32[]{:S(2)}) %collective-permute-start.33) | collective-permute-done | bytes 32800 | tf_op jit(solution)/shard_map/ppermute | solution.py:906
  164.3 0.6 rows.1
  164.9 5.0 %collective-permute-done.34.other_ref = bf16[528,512]{1,0:T(8,128)(2,1)S(1)} collective-permute-done((bf16[528,512]{1,0:T(8,128)(2,1)S(1)}, bf16[528,512]{1,0:T(8,128)(2,1)S(1)}, u32[]{:S(2)}, u32[]{:S(2)}) %collective-permute-start.34) | collective-permute-done | bytes 540704 | tf_op jit(solution)/shard_map/ppermute | solution.py:906
  169.9 1.4 place.13
  (99 shorter events, 5.6 us)
Async XLA Ops:
  1.7 18.7 %collective-permute-start = (bf16[256,1024]{1,0:T(8,128)(2,1)S(1)}, bf16[256,1024]{1,0:T(8,128)(2,1)S(1)}, u32[]{:S(2)}, u32[]{:S(2)}) collective-permute-start(bf16[256,1024]{1,0:T(8,128)(2,1)S(1)} %dynamic-slice_bitcast_fusion), channel_id=1, source_target_pairs={{0,4},{4,0},{1,5},{5,1},{2,6},{6,2},{3,7},{7,3},{8,12},{12,8},{9,1... | collective-permute-start | bytes 1572872 | tf_op jit(solution)/shard_map/ppermute | solution.py:906
  5.6 1.2 copy-start.4
  6.8 9.7 %copy-start = (bf16[1,512,1024]{2,1,0:T(8,128)(2,1)S(1)}, bf16[1,512,1024]{2,1,0:T(8,128)(2,1)}, u32[]{:S(2)}) copy-start(bf16[1,512,1024]{2,1,0:T(8,128)(2,1)} %param.19) | copy-start | bytes 3145732
  12.0 1.0 copy-start.9
  13.0 7.2 %copy-start.10 = (bf16[512,1024]{1,0:T(8,128)(2,1)}, bf16[512,1024]{1,0:T(8,128)(2,1)S(1)}, u32[]{:S(2)}) copy-start(bf16[512,1024]{1,0:T(8,128)(2,1)S(1)} %get-tuple-element.328.n2_ref.refs_16_) | copy-start | bytes 3145732
  13.0 17.8 %collective-permute-start.3 = (bf16[528,512]{1,0:T(8,128)(2,1)S(1)}, bf16[528,512]{1,0:T(8,128)(2,1)S(1)}, u32[]{:S(2)}, u32[]{:S(2)}) collective-permute-start(bf16[528,512]{1,0:T(8,128)(2,1)S(1)} %get-tuple-element.274.a_ref), channel_id=1, source_target_pairs={{0,8},{24,16},{1,9},{25,17},{2,10},{26,18},{3,11},{27,19},{4,12},{... | collective-permute-start | bytes 1622024 | tf_op jit(solution)/shard_map/ppermute | solution.py:906
  16.5 5.9 %copy-start.16 = (f32[3,256]{1,0:T(4,128)S(1)}, f32[3,256]{1,0:T(4,128)}, u32[]{:S(2)}) copy-start(f32[3,256]{1,0:T(4,128)} %b_ref) | copy-start | bytes 9220
  20.2 8.6 %copy-start.6 = (bf16[512,1024]{1,0:T(8,128)(2,1)}, bf16[512,1024]{1,0:T(8,128)(2,1)S(1)}, u32[]{:S(2)}) copy-start(bf16[512,1024]{1,0:T(8,128)(2,1)S(1)} %get-tuple-element.347.refs_18_.gu_ref) | copy-start | bytes 3145732
  20.5 2.0 %collective-permute-start.1 = (bf16[256,1024]{1,0:T(8,128)(2,1)S(1)}, bf16[256,1024]{1,0:T(8,128)(2,1)S(1)}, u32[]{:S(2)}, u32[]{:S(2)}) collective-permute-start(bf16[256,1024]{1,0:T(8,128)(2,1)S(1)} %collective-permute-done.near_ref), channel_id=1, source_target_pairs={{0,1},{1,0},{2,3},{3,2},{4,5},{5,4},{6,7},{7,6},{8,9},{9,8},{10,11... | collective-permute-start | bytes 1572872 | tf_op jit(solution)/shard_map/ppermute | solution.py:906
  20.6 15.2 %collective-permute-start.2 = (bf16[256,1024]{1,0:T(8,128)(2,1)S(1)}, bf16[256,1024]{1,0:T(8,128)(2,1)S(1)}, u32[]{:S(2)}, u32[]{:S(2)}) collective-permute-start(bf16[256,1024]{1,0:T(8,128)(2,1)S(1)} %constant_dynamic-slice_fusion), channel_id=1, source_target_pairs={{0,4},{4,0},{1,5},{5,1},{2,6},{6,2},{3,7},{7,3},{8,12},{12,8},{9,1... | collective-permute-start | bytes 1572872 | tf_op jit(solution)/shard_map/ppermute | solution.py:906
  22.5 13.4 %copy-start.17 = (s32[1,512]{1,0:T(1,128)S(1)}, s32[1,512]{1,0:T(1,128)}, u32[]{:S(2)}) copy-start(s32[1,512]{1,0:T(1,128)} %param.18) | copy-start | bytes 6148
  22.5 13.4 %copy-start.18 = (s32[1,512]{1,0:T(1,128)S(1)}, s32[1,512]{1,0:T(1,128)}, u32[]{:S(2)}) copy-start(s32[1,512]{1,0:T(1,128)} %param.17) | copy-start | bytes 6148
  22.5 15.3 %copy-start.11 = (bf16[256,1024]{1,0:T(8,128)(2,1)S(1)}, bf16[256,1024]{1,0:T(8,128)(2,1)}, u32[]{:S(2)}) copy-start(bf16[256,1024]{1,0:T(8,128)(2,1)} %ow_ref.1) | copy-start | bytes 1572868
  28.8 1.0 copy-start.13
  29.8 1.0 copy-start.14
  30.8 7.0 %copy-start.12 = (f32[512,512]{1,0:T(8,128)}, f32[512,512]{1,0:T(8,128)S(1)}, u32[]{:S(2)}) copy-start(f32[512,512]{1,0:T(8,128)S(1)} %get-tuple-element.284.slope_ref) | copy-start | bytes 3145732
  30.9 19.0 %collective-permute-start.7 = (bf16[528,512]{1,0:T(8,128)(2,1)S(1)}, bf16[528,512]{1,0:T(8,128)(2,1)S(1)}, u32[]{:S(2)}, u32[]{:S(2)}) collective-permute-start(bf16[528,512]{1,0:T(8,128)(2,1)S(1)} %add.30.a_ref), channel_id=1, source_target_pairs={{8,16},{16,8},{9,17},{17,9},{10,18},{18,10},{11,19},{19,11},{12,20... | collective-permute-start | bytes 1622024 | tf_op jit(solution)/shard_map/ppermute | solution.py:906
  31.6 18.4 %collective-permute-start.6 = (bf16[528,512]{1,0:T(8,128)(2,1)S(1)}, bf16[528,512]{1,0:T(8,128)(2,1)S(1)}, u32[]{:S(2)}, u32[]{:S(2)}) collective-permute-start(bf16[528,512]{1,0:T(8,128)(2,1)S(1)} %get-tuple-element.310.a_ref), channel_id=1, source_target_pairs={{0,8},{24,16},{1,9},{25,17},{2,10},{26,18},{3,11},{27,19},{4,12},{... | collective-permute-start | bytes 1622024 | tf_op jit(solution)/shard_map/ppermute | solution.py:906
  35.8 2.0 %collective-permute-start.4 = (bf16[256,1024]{1,0:T(8,128)(2,1)S(1)}, bf16[256,1024]{1,0:T(8,128)(2,1)S(1)}, u32[]{:S(2)}, u32[]{:S(2)}) collective-permute-start(bf16[256,1024]{1,0:T(8,128)(2,1)S(1)} %collective-permute-done.2.near_ref), channel_id=1, source_target_pairs={{0,1},{1,0},{2,3},{3,2},{4,5},{5,4},{6,7},{7,6},{8,9},{9,8},{10,11... | collective-permute-start | bytes 1572872 | tf_op jit(solution)/shard_map/ppermute | solution.py:906
  35.9 7.0 %collective-permute-start.5 = (s32[2,512]{1,0:T(2,128)S(1)}, s32[2,512]{1,0:T(2,128)S(1)}, u32[]{:S(2)}, u32[]{:S(2)}) collective-permute-start(s32[2,512]{1,0:T(2,128)S(1)} %pad_add_fusion.refs_7_), channel_id=1, source_target_pairs={{0,4},{4,0},{1,5},{5,1},{2,6},{6,2},{3,7},{7,3},{8,12},{12,8},{9,1... | collective-permute-start | bytes 12296 | tf_op jit(solution)/shard_map/ppermute | solution.py:842
  41.9 1.0 copy-start.15
  42.9 18.7 %collective-permute-start.10 = (bf16[528,512]{1,0:T(8,128)(2,1)S(1)}, bf16[528,512]{1,0:T(8,128)(2,1)S(1)}, u32[]{:S(2)}, u32[]{:S(2)}) collective-permute-start(bf16[528,512]{1,0:T(8,128)(2,1)S(1)} %get-tuple-element.344.a_ref), channel_id=1, source_target_pairs={{0,8},{24,16},{1,9},{25,17},{2,10},{26,18},{3,11},{27,19},{4,12},{... | collective-permute-start | bytes 1622024 | tf_op jit(solution)/shard_map/ppermute | solution.py:906
  50.2 11.4 %collective-permute-start.11 = (bf16[528,512]{1,0:T(8,128)(2,1)S(1)}, bf16[528,512]{1,0:T(8,128)(2,1)S(1)}, u32[]{:S(2)}, u32[]{:S(2)}) collective-permute-start(bf16[528,512]{1,0:T(8,128)(2,1)S(1)} %add.32.a_ref), channel_id=1, source_target_pairs={{8,16},{16,8},{9,17},{17,9},{10,18},{18,10},{11,19},{19,11},{12,20... | collective-permute-start | bytes 1622024 | tf_op jit(solution)/shard_map/ppermute | solution.py:906
  50.9 19.8 %collective-permute-start.9 = (bf16[528,512]{1,0:T(8,128)(2,1)S(1)}, bf16[528,512]{1,0:T(8,128)(2,1)S(1)}, u32[]{:S(2)}, u32[]{:S(2)}) collective-permute-start(bf16[528,512]{1,0:T(8,128)(2,1)S(1)} %add.31.a_ref), channel_id=1, source_target_pairs={{8,0},{16,24},{9,1},{17,25},{10,2},{18,26},{11,3},{19,27},{12,4},{... | collective-permute-start | bytes 1622024 | tf_op jit(solution)/shard_map/ppermute | solution.py:906
  52.2 15.4 %copy-start.3 = (bf16[1024,1024]{1,0:T(8,128)(2,1)S(1)}, bf16[1024,1024]{1,0:T(8,128)(2,1)}, u32[]{:S(2)}) copy-start(bf16[1024,1024]{1,0:T(8,128)(2,1)} %down_ref.4) | copy-start | bytes 6291460
  52.2 15.4 %copy-start.7 = (bf16[512,1024]{1,0:T(8,128)(2,1)S(1)}, bf16[512,1024]{1,0:T(8,128)(2,1)}, u32[]{:S(2)}) copy-start(bf16[512,1024]{1,0:T(8,128)(2,1)} %copy-done.6) | copy-start | bytes 3145732
  61.5 6.1 %copy-start.1 = (bf16[1,512,1024]{2,1,0:T(8,128)(2,1)S(1)}, bf16[1,512,1024]{2,1,0:T(8,128)(2,1)}, u32[]{:S(2)}) copy-start(bf16[1,512,1024]{2,1,0:T(8,128)(2,1)} %param.19) | copy-start | bytes 3145732
  61.5 6.1 %copy-start.2 = (bf16[1024,1024]{1,0:T(8,128)(2,1)S(1)}, bf16[1024,1024]{1,0:T(8,128)(2,1)}, u32[]{:S(2)}) copy-start(bf16[1024,1024]{1,0:T(8,128)(2,1)} %up_ref.4) | copy-start | bytes 6291460
  61.6 6.1 %copy-start.5 = (bf16[1,512,1024]{2,1,0:T(8,128)(2,1)S(1)}, bf16[1,512,1024]{2,1,0:T(8,128)(2,1)}, u32[]{:S(2)}) copy-start(bf16[1,512,1024]{2,1,0:T(8,128)(2,1)} %param.16) | copy-start | bytes 3145732
  61.8 23.7 %collective-permute-start.12 = (bf16[528,512]{1,0:T(8,128)(2,1)S(1)}, bf16[528,512]{1,0:T(8,128)(2,1)S(1)}, u32[]{:S(2)}, u32[]{:S(2)}) collective-permute-start(bf16[528,512]{1,0:T(8,128)(2,1)S(1)} %choose.11), channel_id=1, source_target_pairs={{0,8},{24,16},{8,0},{16,24},{1,9},{25,17},{9,1},{17,25},{2,10},{26... | collective-permute-start | bytes 1622024 | tf_op jit(solution)/shard_map/ppermute | solution.py:910
  66.1 19.4 %collective-permute-start.13 = (bf16[528,512]{1,0:T(8,128)(2,1)S(1)}, bf16[528,512]{1,0:T(8,128)(2,1)S(1)}, u32[]{:S(2)}, u32[]{:S(2)}) collective-permute-start(bf16[528,512]{1,0:T(8,128)(2,1)S(1)} %add.34.a_ref), channel_id=1, source_target_pairs={{8,16},{16,8},{9,17},{17,9},{10,18},{18,10},{11,19},{19,11},{12,20... | collective-permute-start | bytes 1622024 | tf_op jit(solution)/shard_map/ppermute | solution.py:906
  67.0 15.2 %copy-start.8 = (bf16[1024,3,256]{2,0,1:T(8,128)(2,1)S(1)}, bf16[1024,3,256]{2,0,1:T(8,128)(2,1)}, u32[]{:S(2)}) copy-start(bf16[1024,3,256]{2,0,1:T(8,128)(2,1)} %param.24) | copy-start | bytes 4718596
  67.0 15.1 %collective-permute-start.8 = (bf16[4,512,128]{2,1,0:T(8,128)(2,1)}, bf16[4,512,128]{2,1,0:T(8,128)(2,1)S(1)}, u32[]{:S(2)}, u32[]{:S(2)}) collective-permute-start(bf16[4,512,128]{2,1,0:T(8,128)(2,1)} %get-tuple-element.334), channel_id=1, source_target_pairs={{0,4},{4,0},{1,5},{5,1},{2,6},{6,2},{3,7},{7,3},{8,12},{12,8},{9,1... | collective-permute-start | bytes 1572872 | tf_op jit(solution)/shard_map/ppermute | solution.py:842
  70.7 20.1 %collective-permute-start.16 = (bf16[528,512]{1,0:T(8,128)(2,1)S(1)}, bf16[528,512]{1,0:T(8,128)(2,1)S(1)}, u32[]{:S(2)}, u32[]{:S(2)}) collective-permute-start(bf16[528,512]{1,0:T(8,128)(2,1)S(1)} %choose.12.mine_ref), channel_id=1, source_target_pairs={{0,4},{4,0},{1,5},{5,1},{2,6},{6,2},{3,7},{7,3},{8,12},{12,8},{9,1... | collective-permute-start | bytes 1622024 | tf_op jit(solution)/shard_map/ppermute | solution.py:906
  85.7 10.4 %collective-permute-start.15 = (bf16[528,512]{1,0:T(8,128)(2,1)S(1)}, bf16[528,512]{1,0:T(8,128)(2,1)S(1)}, u32[]{:S(2)}, u32[]{:S(2)}) collective-permute-start(bf16[528,512]{1,0:T(8,128)(2,1)S(1)} %choose.13), channel_id=1, source_target_pairs={{0,8},{24,16},{8,0},{16,24},{1,9},{25,17},{9,1},{17,25},{2,10},{26... | collective-permute-start | bytes 1622024 | tf_op jit(solution)/shard_map/ppermute | solution.py:910
  88.0 8.1 %collective-permute-start.17 = (bf16[528,512]{1,0:T(8,128)(2,1)S(1)}, bf16[528,512]{1,0:T(8,128)(2,1)S(1)}, u32[]{:S(2)}, u32[]{:S(2)}) collective-permute-start(bf16[528,512]{1,0:T(8,128)(2,1)S(1)} %add.36.a_ref), channel_id=1, source_target_pairs={{8,16},{16,8},{9,17},{17,9},{10,18},{18,10},{11,19},{19,11},{12,20... | collective-permute-start | bytes 1622024 | tf_op jit(solution)/shard_map/ppermute | solution.py:906
  88.8 13.0 %collective-permute-start.14 = (bf16[512,1024]{1,0:T(8,128)(2,1)S(1)}, bf16[512,1024]{1,0:T(8,128)(2,1)S(1)}, u32[]{:S(2)}, u32[]{:S(2)}) collective-permute-start(bf16[512,1024]{1,0:T(8,128)(2,1)S(1)} %get-tuple-element.385), channel_id=1, source_target_pairs={{0,1},{1,0},{2,3},{3,2},{4,5},{5,4},{6,7},{7,6},{8,9},{9,8},{10,11... | collective-permute-start | bytes 3145736 | tf_op jit(solution)/shard_map/ppermute | solution.py:906
  88.8 15.1 %collective-permute-start.21 = (bf16[528,512]{1,0:T(8,128)(2,1)S(1)}, bf16[528,512]{1,0:T(8,128)(2,1)S(1)}, u32[]{:S(2)}, u32[]{:S(2)}) collective-permute-start(bf16[528,512]{1,0:T(8,128)(2,1)S(1)} %choose.14.mine_ref), channel_id=1, source_target_pairs={{0,4},{4,0},{1,5},{5,1},{2,6},{6,2},{3,7},{7,3},{8,12},{12,8},{9,1... | collective-permute-start | bytes 1622024 | tf_op jit(solution)/shard_map/ppermute | solution.py:906
  96.3 11.9 %collective-permute-start.20 = (bf16[528,512]{1,0:T(8,128)(2,1)S(1)}, bf16[528,512]{1,0:T(8,128)(2,1)S(1)}, u32[]{:S(2)}, u32[]{:S(2)}) collective-permute-start(bf16[528,512]{1,0:T(8,128)(2,1)S(1)} %choose.15), channel_id=1, source_target_pairs={{0,8},{24,16},{8,0},{16,24},{1,9},{25,17},{9,1},{17,25},{2,10},{26... | collective-permute-start | bytes 1622024 | tf_op jit(solution)/shard_map/ppermute | solution.py:910
  100.9 7.4 %collective-permute-start.19 = (bf16[528,512]{1,0:T(8,128)(2,1)S(1)}, bf16[528,512]{1,0:T(8,128)(2,1)S(1)}, u32[]{:S(2)}, u32[]{:S(2)}) collective-permute-start(bf16[528,512]{1,0:T(8,128)(2,1)S(1)} %add.38.a_ref), channel_id=1, source_target_pairs={{8,16},{16,8},{9,17},{17,9},{10,18},{18,10},{11,19},{19,11},{12,20... | collective-permute-start | bytes 1622024 | tf_op jit(solution)/shard_map/ppermute | solution.py:906
  101.6 15.3 %collective-permute-start.24 = (bf16[528,512]{1,0:T(8,128)(2,1)S(1)}, bf16[528,512]{1,0:T(8,128)(2,1)S(1)}, u32[]{:S(2)}, u32[]{:S(2)}) collective-permute-start(bf16[528,512]{1,0:T(8,128)(2,1)S(1)} %choose.16.mine_ref), channel_id=1, source_target_pairs={{0,4},{4,0},{1,5},{5,1},{2,6},{6,2},{3,7},{7,3},{8,12},{12,8},{9,1... | collective-permute-start | bytes 1622024 | tf_op jit(solution)/shard_map/ppermute | solution.py:906
  108.5 11.3 %collective-permute-start.22 = (bf16[528,512]{1,0:T(8,128)(2,1)S(1)}, bf16[528,512]{1,0:T(8,128)(2,1)S(1)}, u32[]{:S(2)}, u32[]{:S(2)}) collective-permute-start(bf16[528,512]{1,0:T(8,128)(2,1)S(1)} %choose.17), channel_id=1, source_target_pairs={{0,8},{24,16},{8,0},{16,24},{1,9},{25,17},{9,1},{17,25},{2,10},{26... | collective-permute-start | bytes 1622024 | tf_op jit(solution)/shard_map/ppermute | solution.py:910
  112.4 19.3 %collective-permute-start.18 = (bf16[512,1024]{1,0:T(8,128)(2,1)S(1)}, bf16[512,1024]{1,0:T(8,128)(2,1)S(1)}, u32[]{:S(2)}, u32[]{:S(2)}) collective-permute-start(bf16[512,1024]{1,0:T(8,128)(2,1)S(1)} %add.39.a_ref), channel_id=1, source_target_pairs={{0,2},{1,3},{2,0},{3,1},{4,6},{5,7},{6,4},{7,5},{8,10},{9,11},{10,... | collective-permute-start | bytes 3145736 | tf_op jit(solution)/shard_map/ppermute | solution.py:906
  114.2 6.4 %collective-permute-start.23 = (bf16[528,512]{1,0:T(8,128)(2,1)S(1)}, bf16[528,512]{1,0:T(8,128)(2,1)S(1)}, u32[]{:S(2)}, u32[]{:S(2)}) collective-permute-start(bf16[528,512]{1,0:T(8,128)(2,1)S(1)} %add.41.a_ref), channel_id=1, source_target_pairs={{8,16},{16,8},{9,17},{17,9},{10,18},{18,10},{11,19},{19,11},{12,20... | collective-permute-start | bytes 1622024 | tf_op jit(solution)/shard_map/ppermute | solution.py:906
  115.0 17.7 %collective-permute-start.27 = (bf16[528,512]{1,0:T(8,128)(2,1)S(1)}, bf16[528,512]{1,0:T(8,128)(2,1)S(1)}, u32[]{:S(2)}, u32[]{:S(2)}) collective-permute-start(bf16[528,512]{1,0:T(8,128)(2,1)S(1)} %choose.18.mine_ref), channel_id=1, source_target_pairs={{0,4},{4,0},{1,5},{5,1},{2,6},{6,2},{3,7},{7,3},{8,12},{12,8},{9,1... | collective-permute-start | bytes 1622024 | tf_op jit(solution)/shard_map/ppermute | solution.py:906
  119.9 14.2 %collective-permute-start.26 = (bf16[528,512]{1,0:T(8,128)(2,1)S(1)}, bf16[528,512]{1,0:T(8,128)(2,1)S(1)}, u32[]{:S(2)}, u32[]{:S(2)}) collective-permute-start(bf16[528,512]{1,0:T(8,128)(2,1)S(1)} %add.42.a_ref), channel_id=1, source_target_pairs={{8,16},{16,8},{9,17},{17,9},{10,18},{18,10},{11,19},{19,11},{12,20... | collective-permute-start | bytes 1622024 | tf_op jit(solution)/shard_map/ppermute | solution.py:906
  120.7 17.0 %collective-permute-start.30 = (bf16[528,512]{1,0:T(8,128)(2,1)S(1)}, bf16[528,512]{1,0:T(8,128)(2,1)S(1)}, u32[]{:S(2)}, u32[]{:S(2)}) collective-permute-start(bf16[528,512]{1,0:T(8,128)(2,1)S(1)} %add.43.a_ref), channel_id=1, source_target_pairs={{8,0},{16,24},{9,1},{17,25},{10,2},{18,26},{11,3},{19,27},{12,4},{... | collective-permute-start | bytes 1622024 | tf_op jit(solution)/shard_map/ppermute | solution.py:906
  132.0 20.1 %collective-permute-start.25 = (bf16[512,1024]{1,0:T(8,128)(2,1)S(1)}, bf16[512,1024]{1,0:T(8,128)(2,1)S(1)}, u32[]{:S(2)}, u32[]{:S(2)}) collective-permute-start(bf16[512,1024]{1,0:T(8,128)(2,1)S(1)} %add.44.mine_ref), channel_id=1, source_target_pairs={{0,1},{1,0},{2,3},{3,2},{4,5},{5,4},{6,7},{7,6},{8,9},{9,8},{10,11... | collective-permute-start | bytes 3145736 | tf_op jit(solution)/shard_map/ppermute | solution.py:906
  132.1 15.1 %collective-permute-start.29 = (bf16[528,512]{1,0:T(8,128)(2,1)S(1)}, bf16[528,512]{1,0:T(8,128)(2,1)S(1)}, u32[]{:S(2)}, u32[]{:S(2)}) collective-permute-start(bf16[528,512]{1,0:T(8,128)(2,1)S(1)} %choose.19.mine_ref), channel_id=1, source_target_pairs={{0,4},{4,0},{1,5},{5,1},{2,6},{6,2},{3,7},{7,3},{8,12},{12,8},{9,1... | collective-permute-start | bytes 1622024 | tf_op jit(solution)/shard_map/ppermute | solution.py:906
  134.1 16.2 %collective-permute-start.28 = (bf16[528,512]{1,0:T(8,128)(2,1)S(1)}, bf16[528,512]{1,0:T(8,128)(2,1)S(1)}, u32[]{:S(2)}, u32[]{:S(2)}) collective-permute-start(bf16[528,512]{1,0:T(8,128)(2,1)S(1)} %add.45.a_ref), channel_id=1, source_target_pairs={{8,0},{16,24},{9,1},{17,25},{10,2},{18,26},{11,3},{19,27},{12,4},{... | collective-permute-start | bytes 1622024 | tf_op jit(solution)/shard_map/ppermute | solution.py:906
  137.8 21.0 %collective-permute-start.32 = (bf16[528,512]{1,0:T(8,128)(2,1)S(1)}, bf16[528,512]{1,0:T(8,128)(2,1)S(1)}, u32[]{:S(2)}, u32[]{:S(2)}) collective-permute-start(bf16[528,512]{1,0:T(8,128)(2,1)S(1)} %choose.20.mine_ref), channel_id=1, source_target_pairs={{0,4},{4,0},{1,5},{5,1},{2,6},{6,2},{3,7},{7,3},{8,12},{12,8},{9,1... | collective-permute-start | bytes 1622024 | tf_op jit(solution)/shard_map/ppermute | solution.py:906
  150.5 19.5 %collective-permute-start.34 = (bf16[528,512]{1,0:T(8,128)(2,1)S(1)}, bf16[528,512]{1,0:T(8,128)(2,1)S(1)}, u32[]{:S(2)}, u32[]{:S(2)}) collective-permute-start(bf16[528,512]{1,0:T(8,128)(2,1)S(1)} %choose.21.mine_ref), channel_id=1, source_target_pairs={{0,4},{4,0},{1,5},{5,1},{2,6},{6,2},{3,7},{7,3},{8,12},{12,8},{9,1... | collective-permute-start | bytes 1622024 | tf_op jit(solution)/shard_map/ppermute | solution.py:906
  152.0 8.2 %collective-permute-start.31 = (f32[16,512]{1,0:T(8,128)S(1)}, f32[16,512]{1,0:T(8,128)S(1)}, u32[]{:S(2)}, u32[]{:S(2)}) collective-permute-start(f32[16,512]{1,0:T(8,128)S(1)} %get-tuple-element.451.a_ref.v_ref), channel_id=1, source_target_pairs={{0,1},{1,0},{2,3},{3,2},{4,5},{5,4},{6,7},{7,6},{8,9},{9,8},{10,11... | collective-permute-start | bytes 98312 | tf_op jit(solution)/shard_map/ppermute | solution.py:906
  160.3 4.0 %collective-permute-start.33 = (f32[16,512]{1,0:T(8,128)S(1)}, f32[16,512]{1,0:T(8,128)S(1)}, u32[]{:S(2)}, u32[]{:S(2)}) collective-permute-start(f32[16,512]{1,0:T(8,128)S(1)} %add.46.a_ref), channel_id=1, source_target_pairs={{0,2},{1,3},{2,0},{3,1},{4,6},{5,7},{6,4},{7,5},{8,10},{9,11},{10,... | collective-permute-start | bytes 98312 | tf_op jit(solution)/shard_map/ppermute | solution.py:906

commit v3 on v2

--- a/solution.py
+++ b/solution.py
@@ -1056,8 +1056,8 @@
     u.dy.advance()
     weights()
     u.D1.advance()
+    first_head()
     ids_w()
-    first_head()
     u.E0.advance()
     u.E1.advance()
     attend()
@@ -1066,6 +1066,7 @@
     u.U0.advance_with(u.E1)
     u.D1.advance()
     branch_sums()
+    u.E0.wait()
     u.E0.advance()
     gpx_w()
     sums()
@@ -1087,14 +1088,15 @@
     u.Q1.advance()
     u.U0.advance()
     u.D1.advance()
+    u.U1.wait()
     u.U1.advance()
     u.Q1.advance()
     u.Q0.advance()
     u.both.advance()
     u.U0.advance()
+    u.Q0.advance()
     u.U1.advance()
     u.Q1.advance()
-    u.Q0.advance()
     u.vec.advance()
     u.U1.advance()
     u.both.advance()

time: 172 us -> 166 us (0.965)
  waiting for transfers between devices: 60.9 us -> 54.4 us
    ppermute x29, waiting for transfers between devices: 42.2 us -> 35.2 us  [advance(): self.message = lax.ppermute(value, axis, perm)]
  transfers between devices with their start and end apart: 35 -> 35, of which waited for: 16 -> 14; matrix products, arithmetic and copies ran while one was open for 1% -> 1% of each run, Pallas kernels for 32% -> 33%
where the time goes in v3:
time: 166 us; the launch traced here: 165 us
  Pallas kernels  56 us (34%)
  waiting for transfers between devices  54.4 us (33%)
  starting transfers between devices  46.3 us (28%)
  local copies, waits for them, and re-layouts  7.11 us (4%)
    ppermute x29, waiting for transfers between devices, advance(): self.message = lax.ppermute(value, axis, perm)  35.2 us
    ppermute x29, starting transfers between devices, advance(): self.message = lax.ppermute(value, axis, perm)  30 us
    pallas_call x4, Pallas kernels, fetched(): pl.pallas_call(kernel, grid=(1,), in_specs=[whole(a.shape) for a in array...  25.3 us
    ppermute x4, starting transfers between devices, advance_with(): lax.ppermute(self.run(choose, outward, inward), 'dp', INWARD + OUTWARD)  15.1 us
    pallas_call x33, Pallas kernels, small(): pl.pallas_call(kernel, in_specs=[resident()] * len(arrays), out_specs=[re...  12.6 us
    ppermute x2, waiting for transfers between devices, send(): return lax.ppermute(self.tied(value), axis, perm)  9.87 us
    ppermute x4, waiting for transfers between devices, advance_with(): lax.ppermute(self.run(choose, outward, inward), 'dp', INWARD + OUTWARD)  9.31 us
    pallas_call x7, Pallas kernels, step(): pl.pallas_call(kernel, grid=(count,), in_specs=[resident()] * 2 + [pl.Blo...  9.23 us
  transfers between devices with their start and end apart: 35, of which 14 were waited for; matrix products, arithmetic and copies ran while one was open for 1% of the time, Pallas kernels for 33%

profile of v3, /device:TPU:0, one launch (start us, length us, event | category | flops | bytes accessed | tf_op | source)
XLA Modules:
  0.0 165.3 jit_solution(1687127778440210262)
XLA Ops:
  0.7 1.1 dynamic-slice_bitcast_fusion
  1.7 3.0 %collective-permute-start = (bf16[256,1024]{1,0:T(8,128)(2,1)S(1)}, bf16[256,1024]{1,0:T(8,128)(2,1)S(1)}, u32[]{:S(2)}, u32[]{:S(2)}) collective-permute-start(bf16[256,1024]{1,0:T(8,128)(2,1)S(1)} %dynamic-slice_bitcast_fusion), channel_id=1, source_target_pairs={{0,4},{4,0},{1,5},{5,1},{2,6},{6,2},{3,7},{7,3},{8,12},{12,8},{9,1... | collective-permute-start | bytes 1572872 | tf_op jit(solution)/shard_map/ppermute | solution.py:906
  4.8 0.8 stack.31.pack_ref
  5.6 1.2 copy-done.4
  6.8 5.2 %early.1 = (bf16[512,1024]{1,0:T(8,128)(2,1)S(1)}, bf16[512,1024]{1,0:T(8,128)(2,1)S(1)}, bf16[512,1024]{1,0:T(8,128)(2,1)S(1)}, bf16[512,1024]{1,0:T(8,128)(2,1...) custom-call(bf16[512,1024]{1,0:T(8,128)(2,1)S(1)} %bitcast.29, bf16[512,1024]{1,0:T(8,128)(2,1)} %bitcast.22, ...), custom_call_target="tpu_custom_call" | custom-call | flops 1024 | bytes 1024 | tf_op jit(solution)/shard_map/early/pallas_call | solution.py:474
  12.0 1.0 copy-done.9
  13.0 3.5 %collective-permute-start.3 = (bf16[528,512]{1,0:T(8,128)(2,1)S(1)}, bf16[528,512]{1,0:T(8,128)(2,1)S(1)}, u32[]{:S(2)}, u32[]{:S(2)}) collective-permute-start(bf16[528,512]{1,0:T(8,128)(2,1)S(1)} %get-tuple-element.276.a_ref), channel_id=1, source_target_pairs={{0,8},{24,16},{1,9},{25,17},{2,10},{26,18},{3,11},{27,19},{4,12},{... | collective-permute-start | bytes 1622024 | tf_op jit(solution)/shard_map/ppermute | solution.py:906
  16.5 3.7 %own.1 = (bf16[512,1024]{1,0:T(8,128)(2,1)S(1)}, bf16[512,1024]{1,0:T(8,128)(2,1)S(1)}, f32[1,1024]{1,0:T(1,128)S(1)}, bf16[528,512]{1,0:T(8,128)(2,1)S(1)}) custom-call(bf16[512,1024]{1,0:T(8,128)(2,1)S(1)} %get-tuple-element.330.n2_ref.refs_16_, bf16[512,1024]{1,0:T(8,128)(2,1)S(1)} %bitcast.25, ...), custom_call_target="tpu_custom_call", output_to_operand_aliasing={{0}: (5, {}), {1}: (6, {}), {2}: (7, {})} | custom-call | flops 1024 | bytes 1024 | tf_op jit(solution)/shard_map/own/pallas_call | solution.py:474
  20.6 0.6 collective-permute-start.2
  21.2 1.3 collective-permute-done.1.pair_ref
  22.5 6.4 %other.1 = (bf16[512,1024]{1,0:T(8,128)(2,1)S(1)}, bf16[512,1024]{1,0:T(8,128)(2,1)S(1)}, bf16[512,128]{1,0:T(8,128)(2,1)S(1)}, bf16[512,128]{1,0:T(8,128)(2,1)S...) custom-call(bf16[256,1024]{1,0:T(8,128)(2,1)S(1)} %collective-permut, ...), custom_call_target="tpu_custom_call" | custom-call | flops 1024 | bytes 1024 | tf_op jit(solution)/shard_map/other/pallas_call | solution.py:371
  28.9 1.0 copy-done.13
  29.8 1.0 copy-done.14
  30.9 0.7 collective-permute-start.7
  31.6 4.1 %collective-permute-start.6 = (bf16[528,512]{1,0:T(8,128)(2,1)S(1)}, bf16[528,512]{1,0:T(8,128)(2,1)S(1)}, u32[]{:S(2)}, u32[]{:S(2)}) collective-permute-start(bf16[528,512]{1,0:T(8,128)(2,1)S(1)} %get-tuple-element.312.a_ref), channel_id=1, source_target_pairs={{0,8},{24,16},{1,9},{25,17},{2,10},{26,18},{3,11},{27,19},{4,12},{... | collective-permute-start | bytes 1622024 | tf_op jit(solution)/shard_map/ppermute | solution.py:906
  35.9 0.6 collective-permute-start.5
  36.4 1.3 collective-permute-done.4.pair_ref
  37.7 4.1 %weights.1 = (bf16[512,1024]{1,0:T(8,128)(2,1)S(1)}, bf16[512,512]{1,0:T(8,128)(2,1)S(1)}, bf16[1024,128]{1,0:T(8,128)(2,1)S(1)}, bf16[528,512]{1,0:T(8,128)(2,1)S(1)}) custom-call(bf16[256,1024]{1,0:T(8,128)(2,1)S(1)} %collective-permute-done.2.near_ref, bf16[256,1024]{1,0:T(8,128)(2,1)S(1)} %collective-permute-done.4.pair_ref, ...), custom_call_target="tpu_custom_call" | custom-call | flops 1024 | bytes 1024 | tf_op jit(solution)/shard_map/weights/pallas_call | solution.py:371
  41.9 1.0 copy-done.15
  42.9 1.5 collective-permute-start.10
  44.4 5.5 %first_head.1 = (bf16[1024,128]{1,0:T(8,128)(2,1)S(1)}, bf16[3,1024,128]{2,1,0:T(8,128)(2,1)S(1)}) custom-call(bf16[512,128]{1,0:T(8,128)(2,1)S(1)} %get-tuple-element.314.refs_0_, bf16[512,128]{1,0:T(8,128)(2,1)S(1)} %get-tuple-element.315.refs_1_, bf16[512,128]{1,0:T(8,128)(2,1)S(1)} %get-tuple-element.316.refs_2_, ...), custom_call_target="tpu_custom_call" | custom-call | flops 1024 | bytes 1024 | tf_op jit(solution)/shard_map/first_head/pallas_call | solution.py:371
  50.2 0.7 collective-permute-start.11
  50.9 1.3 collective-permute-start.9
  52.2 9.3 %attend.1 = (bf16[4,512,128]{2,1,0:T(8,128)(2,1)S(1)}, bf16[4,512,128]{2,1,0:T(8,128)(2,1)}, bf16[528,512]{1,0:T(8,128)(2,1)S(1)}, bf16[528,512]{1,0:T(8,128)(2,...) custom-call(bf16[512,128]{1,0:T(8,128)(2,1)S(1)} %get-tuple-element.314.refs_0_, ...), custom_call_target="tpu_custom_call" | custom-call | flops 1024 | bytes 1024 | tf_op jit(solution)/shard_map/attend/pallas_call | solution.py:371
  61.8 4.2 %collective-permute-start.12 = (bf16[528,512]{1,0:T(8,128)(2,1)S(1)}, bf16[528,512]{1,0:T(8,128)(2,1)S(1)}, u32[]{:S(2)}, u32[]{:S(2)}) collective-permute-start(bf16[528,512]{1,0:T(8,128)(2,1)S(1)} %choose.11), channel_id=1, source_target_pairs={{0,8},{24,16},{8,0},{16,24},{1,9},{25,17},{9,1},{17,25},{2,10},{26... | collective-permute-start | bytes 1622024 | tf_op jit(solution)/shard_map/ppermute | solution.py:910
  66.1 0.9 collective-permute-start.13
  67.6 3.0 %branch_sums.1 = (f32[512,1024]{1,0:T(8,128)S(1)}, f32[512,1024]{1,0:T(8,128)S(1)}, f32[8,1024]{1,0:T(8,128)S(1)}) custom-call(bf16[512,1024]{1,0:T(8,128)(2,1)S(1)} %get-tuple-element.348.act_o_ref.act_ref, bf16[512,1024]{1,0:T(8,128)(2,1)S(1)} %copy-done.7, bf16[512,1024]{1,0:T(8,128)(2,1)S(1)} %bitcast.27, bf16[512,1024]{1,0:T(8,128)(2,1)S(1)} %bitcast.30, ...), custom_call_target="tpu_custom_call" | custom-call | flops 1024 | bytes 1024 | tf_op jit(solution)/shard_map/branch_sums/pallas_call | solution.py:358
  70.7 1.6 collective-permute-start.16
  72.3 9.9 %collective-permute-done.8.recv_ref = bf16[4,512,128]{2,1,0:T(8,128)(2,1)S(1)} collective-permute-done((bf16[4,512,128]{2,1,0:T(8,128)(2,1)}, bf16[4,512,128]{2,1,0:T(8,128)(2,1)S(1)}, u32[]{:S(2)}, u32[]{:S(2)}) %collective-permute-start.8) | collective-permute-done | bytes 524320 | tf_op jit(solution)/shard_map/ppermute | solution.py:842
  82.2 3.3 %sums.1 = (bf16[512,1024]{1,0:T(8,128)(2,1)S(1)}, bf16[512,1024]{1,0:T(8,128)(2,1)S(1)}, bf16[16,512]{1,0:T(8,128)(2,1)S(1)}) custom-call(bf16[4,512,128]{2,1,0:T(8,128)(2,1)S(1)} %get-tuple-element.362.mine_ref, bf16[4,512,128]{2,1,0:T(8,128)(2,1)S(1)} %collective-permute-done.8.recv_ref, f32[512,1024]{1,0:T(8,128)S(1)} %get-tuple-element.364.out_ref, ...), custom_call_target="tpu_custom_call" | custom-call | flops 1024 | bytes 1024 | tf_op jit(solution)/shard_map/sums/pallas_call | solution.py:358
  85.7 2.1 %collective-permute-start.15 = (bf16[528,512]{1,0:T(8,128)(2,1)S(1)}, bf16[528,512]{1,0:T(8,128)(2,1)S(1)}, u32[]{:S(2)}, u32[]{:S(2)}) collective-permute-start(bf16[528,512]{1,0:T(8,128)(2,1)S(1)} %choose.13), channel_id=1, source_target_pairs={{0,8},{24,16},{8,0},{16,24},{1,9},{25,17},{9,1},{17,25},{2,10},{26... | collective-permute-start | bytes 1622024 | tf_op jit(solution)/shard_map/ppermute | solution.py:910
  88.0 0.7 collective-permute-start.17
  88.8 0.6 collective-permute-start.21
  89.4 1.4 collective-permute-done.16.other_ref
  90.9 1.1 place.7.refs_0_
  91.9 4.2 %collective-permute-done.15.b_ref = bf16[528,512]{1,0:T(8,128)(2,1)S(1)} collective-permute-done((bf16[528,512]{1,0:T(8,128)(2,1)S(1)}, bf16[528,512]{1,0:T(8,128)(2,1)S(1)}, u32[]{:S(2)}, u32[]{:S(2)}) %collective-permute-start.15) | collective-permute-done | bytes 540704 | tf_op jit(solution)/shard_map/ppermute | solution.py:910
  96.3 4.4 %collective-permute-start.20 = (bf16[528,512]{1,0:T(8,128)(2,1)S(1)}, bf16[528,512]{1,0:T(8,128)(2,1)S(1)}, u32[]{:S(2)}, u32[]{:S(2)}) collective-permute-start(bf16[528,512]{1,0:T(8,128)(2,1)S(1)} %choose.15), channel_id=1, source_target_pairs={{0,8},{24,16},{8,0},{16,24},{1,9},{25,17},{9,1},{17,25},{2,10},{26... | collective-permute-start | bytes 1622024 | tf_op jit(solution)/shard_map/ppermute | solution.py:910
  100.9 0.7 collective-permute-start.19
  102.0 2.0 %collective-permute-done.21.other_ref = bf16[528,512]{1,0:T(8,128)(2,1)S(1)} collective-permute-done((bf16[528,512]{1,0:T(8,128)(2,1)S(1)}, bf16[528,512]{1,0:T(8,128)(2,1)S(1)}, u32[]{:S(2)}, u32[]{:S(2)}) %collective-permute-start.21) | collective-permute-done | bytes 540704 | tf_op jit(solution)/shard_map/ppermute | solution.py:906
  104.0 1.1 place.8.refs_0_
  105.0 3.2 %collective-permute-done.20.b_ref = bf16[528,512]{1,0:T(8,128)(2,1)S(1)} collective-permute-done((bf16[528,512]{1,0:T(8,128)(2,1)S(1)}, bf16[528,512]{1,0:T(8,128)(2,1)S(1)}, u32[]{:S(2)}, u32[]{:S(2)}) %collective-permute-start.20) | collective-permute-done | bytes 540704 | tf_op jit(solution)/shard_map/ppermute | solution.py:910
  108.5 4.4 %collective-permute-start.22 = (bf16[528,512]{1,0:T(8,128)(2,1)S(1)}, bf16[528,512]{1,0:T(8,128)(2,1)S(1)}, u32[]{:S(2)}, u32[]{:S(2)}) collective-permute-start(bf16[528,512]{1,0:T(8,128)(2,1)S(1)} %choose.17), channel_id=1, source_target_pairs={{0,8},{24,16},{8,0},{16,24},{1,9},{25,17},{9,1},{17,25},{2,10},{26... | collective-permute-start | bytes 1622024 | tf_op jit(solution)/shard_map/ppermute | solution.py:910
  113.0 0.7 collective-permute-start.23
  113.7 1.6 collective-permute-start.18
  115.4 1.5 collective-permute-done.24.other_ref
  116.9 1.4 place.9
  118.3 1.9 %collective-permute-done.22.b_ref = bf16[528,512]{1,0:T(8,128)(2,1)S(1)} collective-permute-done((bf16[528,512]{1,0:T(8,128)(2,1)S(1)}, bf16[528,512]{1,0:T(8,128)(2,1)S(1)}, u32[]{:S(2)}, u32[]{:S(2)}) %collective-permute-start.22) | collective-permute-done | bytes 540704 | tf_op jit(solution)/shard_map/ppermute | solution.py:910
  120.6 0.7 collective-permute-start.26
  121.3 1.3 collective-permute-start.30
  122.6 10.0 %collective-permute-done.18.b_ref = bf16[512,1024]{1,0:T(8,128)(2,1)S(1)} collective-permute-done((bf16[512,1024]{1,0:T(8,128)(2,1)S(1)}, bf16[512,1024]{1,0:T(8,128)(2,1)S(1)}, u32[]{:S(2)}, u32[]{:S(2)}) %collective-permute-start.18) | collective-permute-done | bytes 1048608 | tf_op jit(solution)/shard_map/ppermute | solution.py:906
  133.0 1.4 place.10.refs_0_
  134.4 3.9 %collective-permute-done.27.other_ref = bf16[528,512]{1,0:T(8,128)(2,1)S(1)} collective-permute-done((bf16[528,512]{1,0:T(8,128)(2,1)S(1)}, bf16[528,512]{1,0:T(8,128)(2,1)S(1)}, u32[]{:S(2)}, u32[]{:S(2)}) %collective-permute-start.27) | collective-permute-done | bytes 540704 | tf_op jit(solution)/shard_map/ppermute | solution.py:906
  138.3 1.4 place.11
  139.8 1.6 collective-permute-start.29
  141.5 0.6 collective-permute-start.32
  142.1 10.4 %collective-permute-done.29.b_ref = bf16[528,512]{1,0:T(8,128)(2,1)S(1)} collective-permute-done((bf16[528,512]{1,0:T(8,128)(2,1)S(1)}, bf16[528,512]{1,0:T(8,128)(2,1)S(1)}, u32[]{:S(2)}, u32[]{:S(2)}) %collective-permute-start.29) | collective-permute-done | bytes 540704 | tf_op jit(solution)/shard_map/ppermute | solution.py:906
  152.5 0.7 collective-permute-start.34
  153.3 2.6 %results.1 = (bf16[512,1024]{1,0:T(8,128)(2,1)}, bf16[512,1024]{1,0:T(8,128)(2,1)}) custom-call(bf16[512,1024]{1,0:T(8,128)(2,1)S(1)} %add.44.mine_ref, bf16[512,1024]{1,0:T(8,128)(2,1)S(1)} %collective-permute-done.25.other_ref, bf16[512,1024]{1,0:T(8,128)(2,1)S(1)} %bitcast.32, bf16[512,1024]{1,0:T(8,128)(2,1)S(1)} %bitcast.28, f32[7,1024]{1,0:T(8,128)S(1)} %stack.31.pack_ref), custom_call_target="tpu_custom_call" | custom-call | flops 1024 | bytes 1024 | tf_op jit(solution)/shard_map/results/pallas_call | solution.py:358
  155.9 1.5 place.12
  157.4 2.5 %collective-permute-start.33 = (f32[16,512]{1,0:T(8,128)S(1)}, f32[16,512]{1,0:T(8,128)S(1)}, u32[]{:S(2)}, u32[]{:S(2)}) collective-permute-start(f32[16,512]{1,0:T(8,128)S(1)} %add.46.a_ref), channel_id=1, source_target_pairs={{0,2},{1,3},{2,0},{3,1},{4,6},{5,7},{6,4},{7,5},{8,10},{9,11},{10,... | collective-permute-start | bytes 98312 | tf_op jit(solution)/shard_map/ppermute | solution.py:906
  159.9 2.1 %collective-permute-done.33.b_ref = f32[16,512]{1,0:T(8,128)S(1)} collective-permute-done((f32[16,512]{1,0:T(8,128)S(1)}, f32[16,512]{1,0:T(8,128)S(1)}, u32[]{:S(2)}, u32[]{:S(2)}) %collective-permute-start.33) | collective-permute-done | bytes 32800 | tf_op jit(solution)/shard_map/ppermute | solution.py:906
  162.0 0.6 rows.1
  162.6 1.3 collective-permute-done.34.other_ref
  163.9 1.4 place.13
  (99 shorter events, 4.5 us)
Async XLA Ops:
  1.7 18.7 %collective-permute-start = (bf16[256,1024]{1,0:T(8,128)(2,1)S(1)}, bf16[256,1024]{1,0:T(8,128)(2,1)S(1)}, u32[]{:S(2)}, u32[]{:S(2)}) collective-permute-start(bf16[256,1024]{1,0:T(8,128)(2,1)S(1)} %dynamic-slice_bitcast_fusion), channel_id=1, source_target_pairs={{0,4},{4,0},{1,5},{5,1},{2,6},{6,2},{3,7},{7,3},{8,12},{12,8},{9,1... | collective-permute-start | bytes 1572872 | tf_op jit(solution)/shard_map/ppermute | solution.py:906
  5.6 1.2 copy-start.4
  6.8 9.7 %copy-start = (bf16[1,512,1024]{2,1,0:T(8,128)(2,1)S(1)}, bf16[1,512,1024]{2,1,0:T(8,128)(2,1)}, u32[]{:S(2)}) copy-start(bf16[1,512,1024]{2,1,0:T(8,128)(2,1)} %param.19) | copy-start | bytes 3145732
  12.0 1.0 copy-start.9
  13.0 7.2 %copy-start.10 = (bf16[512,1024]{1,0:T(8,128)(2,1)}, bf16[512,1024]{1,0:T(8,128)(2,1)S(1)}, u32[]{:S(2)}) copy-start(bf16[512,1024]{1,0:T(8,128)(2,1)S(1)} %get-tuple-element.330.n2_ref.refs_16_) | copy-start | bytes 3145732
  13.0 17.8 %collective-permute-start.3 = (bf16[528,512]{1,0:T(8,128)(2,1)S(1)}, bf16[528,512]{1,0:T(8,128)(2,1)S(1)}, u32[]{:S(2)}, u32[]{:S(2)}) collective-permute-start(bf16[528,512]{1,0:T(8,128)(2,1)S(1)} %get-tuple-element.276.a_ref), channel_id=1, source_target_pairs={{0,8},{24,16},{1,9},{25,17},{2,10},{26,18},{3,11},{27,19},{4,12},{... | collective-permute-start | bytes 1622024 | tf_op jit(solution)/shard_map/ppermute | solution.py:906
  16.5 5.9 %copy-start.16 = (f32[3,256]{1,0:T(4,128)S(1)}, f32[3,256]{1,0:T(4,128)}, u32[]{:S(2)}) copy-start(f32[3,256]{1,0:T(4,128)} %b_ref) | copy-start | bytes 9220
  20.2 8.6 %copy-start.6 = (bf16[512,1024]{1,0:T(8,128)(2,1)}, bf16[512,1024]{1,0:T(8,128)(2,1)S(1)}, u32[]{:S(2)}) copy-start(bf16[512,1024]{1,0:T(8,128)(2,1)S(1)} %get-tuple-element.349.refs_18_.gu_ref) | copy-start | bytes 3145732
  20.5 2.0 %collective-permute-start.1 = (bf16[256,1024]{1,0:T(8,128)(2,1)S(1)}, bf16[256,1024]{1,0:T(8,128)(2,1)S(1)}, u32[]{:S(2)}, u32[]{:S(2)}) collective-permute-start(bf16[256,1024]{1,0:T(8,128)(2,1)S(1)} %collective-permute-done.near_ref), channel_id=1, source_target_pairs={{0,1},{1,0},{2,3},{3,2},{4,5},{5,4},{6,7},{7,6},{8,9},{9,8},{10,11... | collective-permute-start | bytes 1572872 | tf_op jit(solution)/shard_map/ppermute | solution.py:906
  20.6 15.2 %collective-permute-start.2 = (bf16[256,1024]{1,0:T(8,128)(2,1)S(1)}, bf16[256,1024]{1,0:T(8,128)(2,1)S(1)}, u32[]{:S(2)}, u32[]{:S(2)}) collective-permute-start(bf16[256,1024]{1,0:T(8,128)(2,1)S(1)} %constant_dynamic-slice_fusion), channel_id=1, source_target_pairs={{0,4},{4,0},{1,5},{5,1},{2,6},{6,2},{3,7},{7,3},{8,12},{12,8},{9,1... | collective-permute-start | bytes 1572872 | tf_op jit(solution)/shard_map/ppermute | solution.py:906
  22.5 13.4 %copy-start.17 = (s32[1,512]{1,0:T(1,128)S(1)}, s32[1,512]{1,0:T(1,128)}, u32[]{:S(2)}) copy-start(s32[1,512]{1,0:T(1,128)} %param.18) | copy-start | bytes 6148
  22.5 13.4 %copy-start.18 = (s32[1,512]{1,0:T(1,128)S(1)}, s32[1,512]{1,0:T(1,128)}, u32[]{:S(2)}) copy-start(s32[1,512]{1,0:T(1,128)} %param.17) | copy-start | bytes 6148
  22.5 15.3 %copy-start.11 = (bf16[256,1024]{1,0:T(8,128)(2,1)S(1)}, bf16[256,1024]{1,0:T(8,128)(2,1)}, u32[]{:S(2)}) copy-start(bf16[256,1024]{1,0:T(8,128)(2,1)} %ow_ref.1) | copy-start | bytes 1572868
  28.8 1.0 copy-start.13
  29.8 1.0 copy-start.14
  30.8 7.0 %copy-start.12 = (f32[512,512]{1,0:T(8,128)}, f32[512,512]{1,0:T(8,128)S(1)}, u32[]{:S(2)}) copy-start(f32[512,512]{1,0:T(8,128)S(1)} %get-tuple-element.286.slope_ref) | copy-start | bytes 3145732
  30.9 19.0 %collective-permute-start.7 = (bf16[528,512]{1,0:T(8,128)(2,1)S(1)}, bf16[528,512]{1,0:T(8,128)(2,1)S(1)}, u32[]{:S(2)}, u32[]{:S(2)}) collective-permute-start(bf16[528,512]{1,0:T(8,128)(2,1)S(1)} %add.30.a_ref), channel_id=1, source_target_pairs={{8,16},{16,8},{9,17},{17,9},{10,18},{18,10},{11,19},{19,11},{12,20... | collective-permute-start | bytes 1622024 | tf_op jit(solution)/shard_map/ppermute | solution.py:906
  31.6 18.4 %collective-permute-start.6 = (bf16[528,512]{1,0:T(8,128)(2,1)S(1)}, bf16[528,512]{1,0:T(8,128)(2,1)S(1)}, u32[]{:S(2)}, u32[]{:S(2)}) collective-permute-start(bf16[528,512]{1,0:T(8,128)(2,1)S(1)} %get-tuple-element.312.a_ref), channel_id=1, source_target_pairs={{0,8},{24,16},{1,9},{25,17},{2,10},{26,18},{3,11},{27,19},{4,12},{... | collective-permute-start | bytes 1622024 | tf_op jit(solution)/shard_map/ppermute | solution.py:906
  35.8 2.0 %collective-permute-start.4 = (bf16[256,1024]{1,0:T(8,128)(2,1)S(1)}, bf16[256,1024]{1,0:T(8,128)(2,1)S(1)}, u32[]{:S(2)}, u32[]{:S(2)}) collective-permute-start(bf16[256,1024]{1,0:T(8,128)(2,1)S(1)} %collective-permute-done.2.near_ref), channel_id=1, source_target_pairs={{0,1},{1,0},{2,3},{3,2},{4,5},{5,4},{6,7},{7,6},{8,9},{9,8},{10,11... | collective-permute-start | bytes 1572872 | tf_op jit(solution)/shard_map/ppermute | solution.py:906
  35.9 7.0 %collective-permute-start.5 = (s32[2,512]{1,0:T(2,128)S(1)}, s32[2,512]{1,0:T(2,128)S(1)}, u32[]{:S(2)}, u32[]{:S(2)}) collective-permute-start(s32[2,512]{1,0:T(2,128)S(1)} %pad_add_fusion.refs_7_), channel_id=1, source_target_pairs={{0,4},{4,0},{1,5},{5,1},{2,6},{6,2},{3,7},{7,3},{8,12},{12,8},{9,1... | collective-permute-start | bytes 12296 | tf_op jit(solution)/shard_map/ppermute | solution.py:842
  41.9 1.0 copy-start.15
  42.9 18.7 %collective-permute-start.10 = (bf16[528,512]{1,0:T(8,128)(2,1)S(1)}, bf16[528,512]{1,0:T(8,128)(2,1)S(1)}, u32[]{:S(2)}, u32[]{:S(2)}) collective-permute-start(bf16[528,512]{1,0:T(8,128)(2,1)S(1)} %get-tuple-element.346.a_ref), channel_id=1, source_target_pairs={{0,8},{24,16},{1,9},{25,17},{2,10},{26,18},{3,11},{27,19},{4,12},{... | collective-permute-start | bytes 1622024 | tf_op jit(solution)/shard_map/ppermute | solution.py:906
  50.2 11.4 %collective-permute-start.11 = (bf16[528,512]{1,0:T(8,128)(2,1)S(1)}, bf16[528,512]{1,0:T(8,128)(2,1)S(1)}, u32[]{:S(2)}, u32[]{:S(2)}) collective-permute-start(bf16[528,512]{1,0:T(8,128)(2,1)S(1)} %add.32.a_ref), channel_id=1, source_target_pairs={{8,16},{16,8},{9,17},{17,9},{10,18},{18,10},{11,19},{19,11},{12,20... | collective-permute-start | bytes 1622024 | tf_op jit(solution)/shard_map/ppermute | solution.py:906
  50.9 19.8 %collective-permute-start.9 = (bf16[528,512]{1,0:T(8,128)(2,1)S(1)}, bf16[528,512]{1,0:T(8,128)(2,1)S(1)}, u32[]{:S(2)}, u32[]{:S(2)}) collective-permute-start(bf16[528,512]{1,0:T(8,128)(2,1)S(1)} %add.31.a_ref), channel_id=1, source_target_pairs={{8,0},{16,24},{9,1},{17,25},{10,2},{18,26},{11,3},{19,27},{12,4},{... | collective-permute-start | bytes 1622024 | tf_op jit(solution)/shard_map/ppermute | solution.py:906
  52.2 15.4 %copy-start.3 = (bf16[1024,1024]{1,0:T(8,128)(2,1)S(1)}, bf16[1024,1024]{1,0:T(8,128)(2,1)}, u32[]{:S(2)}) copy-start(bf16[1024,1024]{1,0:T(8,128)(2,1)} %down_ref.4) | copy-start | bytes 6291460
  52.2 15.4 %copy-start.7 = (bf16[512,1024]{1,0:T(8,128)(2,1)S(1)}, bf16[512,1024]{1,0:T(8,128)(2,1)}, u32[]{:S(2)}) copy-start(bf16[512,1024]{1,0:T(8,128)(2,1)} %copy-done.6) | copy-start | bytes 3145732
  61.5 6.1 %copy-start.1 = (bf16[1,512,1024]{2,1,0:T(8,128)(2,1)S(1)}, bf16[1,512,1024]{2,1,0:T(8,128)(2,1)}, u32[]{:S(2)}) copy-start(bf16[1,512,1024]{2,1,0:T(8,128)(2,1)} %param.19) | copy-start | bytes 3145732
  61.5 6.1 %copy-start.2 = (bf16[1024,1024]{1,0:T(8,128)(2,1)S(1)}, bf16[1024,1024]{1,0:T(8,128)(2,1)}, u32[]{:S(2)}) copy-start(bf16[1024,1024]{1,0:T(8,128)(2,1)} %up_ref.4) | copy-start | bytes 6291460
  61.6 6.1 %copy-start.5 = (bf16[1,512,1024]{2,1,0:T(8,128)(2,1)S(1)}, bf16[1,512,1024]{2,1,0:T(8,128)(2,1)}, u32[]{:S(2)}) copy-start(bf16[1,512,1024]{2,1,0:T(8,128)(2,1)} %param.16) | copy-start | bytes 3145732
  61.8 23.7 %collective-permute-start.12 = (bf16[528,512]{1,0:T(8,128)(2,1)S(1)}, bf16[528,512]{1,0:T(8,128)(2,1)S(1)}, u32[]{:S(2)}, u32[]{:S(2)}) collective-permute-start(bf16[528,512]{1,0:T(8,128)(2,1)S(1)} %choose.11), channel_id=1, source_target_pairs={{0,8},{24,16},{8,0},{16,24},{1,9},{25,17},{9,1},{17,25},{2,10},{26... | collective-permute-start | bytes 1622024 | tf_op jit(solution)/shard_map/ppermute | solution.py:910
  66.1 19.4 %collective-permute-start.13 = (bf16[528,512]{1,0:T(8,128)(2,1)S(1)}, bf16[528,512]{1,0:T(8,128)(2,1)S(1)}, u32[]{:S(2)}, u32[]{:S(2)}) collective-permute-start(bf16[528,512]{1,0:T(8,128)(2,1)S(1)} %add.34.a_ref), channel_id=1, source_target_pairs={{8,16},{16,8},{9,17},{17,9},{10,18},{18,10},{11,19},{19,11},{12,20... | collective-permute-start | bytes 1622024 | tf_op jit(solution)/shard_map/ppermute | solution.py:906
  67.0 15.2 %copy-start.8 = (bf16[1024,3,256]{2,0,1:T(8,128)(2,1)S(1)}, bf16[1024,3,256]{2,0,1:T(8,128)(2,1)}, u32[]{:S(2)}) copy-start(bf16[1024,3,256]{2,0,1:T(8,128)(2,1)} %param.24) | copy-start | bytes 4718596
  67.0 15.1 %collective-permute-start.8 = (bf16[4,512,128]{2,1,0:T(8,128)(2,1)}, bf16[4,512,128]{2,1,0:T(8,128)(2,1)S(1)}, u32[]{:S(2)}, u32[]{:S(2)}) collective-permute-start(bf16[4,512,128]{2,1,0:T(8,128)(2,1)} %get-tuple-element.336), channel_id=1, source_target_pairs={{0,4},{4,0},{1,5},{5,1},{2,6},{6,2},{3,7},{7,3},{8,12},{12,8},{9,1... | collective-permute-start | bytes 1572872 | tf_op jit(solution)/shard_map/ppermute | solution.py:842
  70.7 20.1 %collective-permute-start.16 = (bf16[528,512]{1,0:T(8,128)(2,1)S(1)}, bf16[528,512]{1,0:T(8,128)(2,1)S(1)}, u32[]{:S(2)}, u32[]{:S(2)}) collective-permute-start(bf16[528,512]{1,0:T(8,128)(2,1)S(1)} %choose.12.mine_ref), channel_id=1, source_target_pairs={{0,4},{4,0},{1,5},{5,1},{2,6},{6,2},{3,7},{7,3},{8,12},{12,8},{9,1... | collective-permute-start | bytes 1622024 | tf_op jit(solution)/shard_map/ppermute | solution.py:906
  85.7 10.4 %collective-permute-start.15 = (bf16[528,512]{1,0:T(8,128)(2,1)S(1)}, bf16[528,512]{1,0:T(8,128)(2,1)S(1)}, u32[]{:S(2)}, u32[]{:S(2)}) collective-permute-start(bf16[528,512]{1,0:T(8,128)(2,1)S(1)} %choose.13), channel_id=1, source_target_pairs={{0,8},{24,16},{8,0},{16,24},{1,9},{25,17},{9,1},{17,25},{2,10},{26... | collective-permute-start | bytes 1622024 | tf_op jit(solution)/shard_map/ppermute | solution.py:910
  88.0 8.1 %collective-permute-start.17 = (bf16[528,512]{1,0:T(8,128)(2,1)S(1)}, bf16[528,512]{1,0:T(8,128)(2,1)S(1)}, u32[]{:S(2)}, u32[]{:S(2)}) collective-permute-start(bf16[528,512]{1,0:T(8,128)(2,1)S(1)} %add.36.a_ref), channel_id=1, source_target_pairs={{8,16},{16,8},{9,17},{17,9},{10,18},{18,10},{11,19},{19,11},{12,20... | collective-permute-start | bytes 1622024 | tf_op jit(solution)/shard_map/ppermute | solution.py:906
  88.8 13.0 %collective-permute-start.14 = (bf16[512,1024]{1,0:T(8,128)(2,1)S(1)}, bf16[512,1024]{1,0:T(8,128)(2,1)S(1)}, u32[]{:S(2)}, u32[]{:S(2)}) collective-permute-start(bf16[512,1024]{1,0:T(8,128)(2,1)S(1)} %get-tuple-element.388), channel_id=1, source_target_pairs={{0,1},{1,0},{2,3},{3,2},{4,5},{5,4},{6,7},{7,6},{8,9},{9,8},{10,11... | collective-permute-start | bytes 3145736 | tf_op jit(solution)/shard_map/ppermute | solution.py:906
  88.8 15.1 %collective-permute-start.21 = (bf16[528,512]{1,0:T(8,128)(2,1)S(1)}, bf16[528,512]{1,0:T(8,128)(2,1)S(1)}, u32[]{:S(2)}, u32[]{:S(2)}) collective-permute-start(bf16[528,512]{1,0:T(8,128)(2,1)S(1)} %choose.14.mine_ref), channel_id=1, source_target_pairs={{0,4},{4,0},{1,5},{5,1},{2,6},{6,2},{3,7},{7,3},{8,12},{12,8},{9,1... | collective-permute-start | bytes 1622024 | tf_op jit(solution)/shard_map/ppermute | solution.py:906
  96.3 11.9 %collective-permute-start.20 = (bf16[528,512]{1,0:T(8,128)(2,1)S(1)}, bf16[528,512]{1,0:T(8,128)(2,1)S(1)}, u32[]{:S(2)}, u32[]{:S(2)}) collective-permute-start(bf16[528,512]{1,0:T(8,128)(2,1)S(1)} %choose.15), channel_id=1, source_target_pairs={{0,8},{24,16},{8,0},{16,24},{1,9},{25,17},{9,1},{17,25},{2,10},{26... | collective-permute-start | bytes 1622024 | tf_op jit(solution)/shard_map/ppermute | solution.py:910
  100.9 7.4 %collective-permute-start.19 = (bf16[528,512]{1,0:T(8,128)(2,1)S(1)}, bf16[528,512]{1,0:T(8,128)(2,1)S(1)}, u32[]{:S(2)}, u32[]{:S(2)}) collective-permute-start(bf16[528,512]{1,0:T(8,128)(2,1)S(1)} %add.38.a_ref), channel_id=1, source_target_pairs={{8,16},{16,8},{9,17},{17,9},{10,18},{18,10},{11,19},{19,11},{12,20... | collective-permute-start | bytes 1622024 | tf_op jit(solution)/shard_map/ppermute | solution.py:906
  101.6 15.3 %collective-permute-start.24 = (bf16[528,512]{1,0:T(8,128)(2,1)S(1)}, bf16[528,512]{1,0:T(8,128)(2,1)S(1)}, u32[]{:S(2)}, u32[]{:S(2)}) collective-permute-start(bf16[528,512]{1,0:T(8,128)(2,1)S(1)} %choose.16.mine_ref), channel_id=1, source_target_pairs={{0,4},{4,0},{1,5},{5,1},{2,6},{6,2},{3,7},{7,3},{8,12},{12,8},{9,1... | collective-permute-start | bytes 1622024 | tf_op jit(solution)/shard_map/ppermute | solution.py:906
  108.5 11.7 %collective-permute-start.22 = (bf16[528,512]{1,0:T(8,128)(2,1)S(1)}, bf16[528,512]{1,0:T(8,128)(2,1)S(1)}, u32[]{:S(2)}, u32[]{:S(2)}) collective-permute-start(bf16[528,512]{1,0:T(8,128)(2,1)S(1)} %choose.17), channel_id=1, source_target_pairs={{0,8},{24,16},{8,0},{16,24},{1,9},{25,17},{9,1},{17,25},{2,10},{26... | collective-permute-start | bytes 1622024 | tf_op jit(solution)/shard_map/ppermute | solution.py:910
  113.0 7.3 %collective-permute-start.23 = (bf16[528,512]{1,0:T(8,128)(2,1)S(1)}, bf16[528,512]{1,0:T(8,128)(2,1)S(1)}, u32[]{:S(2)}, u32[]{:S(2)}) collective-permute-start(bf16[528,512]{1,0:T(8,128)(2,1)S(1)} %add.41.a_ref), channel_id=1, source_target_pairs={{8,16},{16,8},{9,17},{17,9},{10,18},{18,10},{11,19},{19,11},{12,20... | collective-permute-start | bytes 1622024 | tf_op jit(solution)/shard_map/ppermute | solution.py:906
  113.7 18.9 %collective-permute-start.18 = (bf16[512,1024]{1,0:T(8,128)(2,1)S(1)}, bf16[512,1024]{1,0:T(8,128)(2,1)S(1)}, u32[]{:S(2)}, u32[]{:S(2)}) collective-permute-start(bf16[512,1024]{1,0:T(8,128)(2,1)S(1)} %add.39.a_ref), channel_id=1, source_target_pairs={{0,2},{1,3},{2,0},{3,1},{4,6},{5,7},{6,4},{7,5},{8,10},{9,11},{10,... | collective-permute-start | bytes 3145736 | tf_op jit(solution)/shard_map/ppermute | solution.py:906
  115.3 17.6 %collective-permute-start.28 = (bf16[528,512]{1,0:T(8,128)(2,1)S(1)}, bf16[528,512]{1,0:T(8,128)(2,1)S(1)}, u32[]{:S(2)}, u32[]{:S(2)}) collective-permute-start(bf16[528,512]{1,0:T(8,128)(2,1)S(1)} %choose.18.mine_ref), channel_id=1, source_target_pairs={{0,4},{4,0},{1,5},{5,1},{2,6},{6,2},{3,7},{7,3},{8,12},{12,8},{9,1... | collective-permute-start | bytes 1622024 | tf_op jit(solution)/shard_map/ppermute | solution.py:906
  120.6 17.7 %collective-permute-start.27 = (bf16[528,512]{1,0:T(8,128)(2,1)S(1)}, bf16[528,512]{1,0:T(8,128)(2,1)S(1)}, u32[]{:S(2)}, u32[]{:S(2)}) collective-permute-start(bf16[528,512]{1,0:T(8,128)(2,1)S(1)} %choose.19.mine_ref), channel_id=1, source_target_pairs={{0,4},{4,0},{1,5},{5,1},{2,6},{6,2},{3,7},{7,3},{8,12},{12,8},{9,1... | collective-permute-start | bytes 1622024 | tf_op jit(solution)/shard_map/ppermute | solution.py:906
  120.6 19.1 %collective-permute-start.26 = (bf16[528,512]{1,0:T(8,128)(2,1)S(1)}, bf16[528,512]{1,0:T(8,128)(2,1)S(1)}, u32[]{:S(2)}, u32[]{:S(2)}) collective-permute-start(bf16[528,512]{1,0:T(8,128)(2,1)S(1)} %add.42.a_ref), channel_id=1, source_target_pairs={{8,16},{16,8},{9,17},{17,9},{10,18},{18,10},{11,19},{19,11},{12,20... | collective-permute-start | bytes 1622024 | tf_op jit(solution)/shard_map/ppermute | solution.py:906
  121.3 20.1 %collective-permute-start.30 = (bf16[528,512]{1,0:T(8,128)(2,1)S(1)}, bf16[528,512]{1,0:T(8,128)(2,1)S(1)}, u32[]{:S(2)}, u32[]{:S(2)}) collective-permute-start(bf16[528,512]{1,0:T(8,128)(2,1)S(1)} %add.43.a_ref), channel_id=1, source_target_pairs={{8,0},{16,24},{9,1},{17,25},{10,2},{18,26},{11,3},{19,27},{12,4},{... | collective-permute-start | bytes 1622024 | tf_op jit(solution)/shard_map/ppermute | solution.py:906
  132.9 20.4 %collective-permute-start.25 = (bf16[512,1024]{1,0:T(8,128)(2,1)S(1)}, bf16[512,1024]{1,0:T(8,128)(2,1)S(1)}, u32[]{:S(2)}, u32[]{:S(2)}) collective-permute-start(bf16[512,1024]{1,0:T(8,128)(2,1)S(1)} %add.44.mine_ref), channel_id=1, source_target_pairs={{0,1},{1,0},{2,3},{3,2},{4,5},{5,4},{6,7},{7,6},{8,9},{9,8},{10,11... | collective-permute-start | bytes 3145736 | tf_op jit(solution)/shard_map/ppermute | solution.py:906
  139.8 12.6 %collective-permute-start.29 = (bf16[528,512]{1,0:T(8,128)(2,1)S(1)}, bf16[528,512]{1,0:T(8,128)(2,1)S(1)}, u32[]{:S(2)}, u32[]{:S(2)}) collective-permute-start(bf16[528,512]{1,0:T(8,128)(2,1)S(1)} %add.45.a_ref), channel_id=1, source_target_pairs={{8,0},{16,24},{9,1},{17,25},{10,2},{18,26},{11,3},{19,27},{12,4},{... | collective-permute-start | bytes 1622024 | tf_op jit(solution)/shard_map/ppermute | solution.py:906
  141.5 14.4 %collective-permute-start.32 = (bf16[528,512]{1,0:T(8,128)(2,1)S(1)}, bf16[528,512]{1,0:T(8,128)(2,1)S(1)}, u32[]{:S(2)}, u32[]{:S(2)}) collective-permute-start(bf16[528,512]{1,0:T(8,128)(2,1)S(1)} %choose.20.mine_ref), channel_id=1, source_target_pairs={{0,4},{4,0},{1,5},{5,1},{2,6},{6,2},{3,7},{7,3},{8,12},{12,8},{9,1... | collective-permute-start | bytes 1622024 | tf_op jit(solution)/shard_map/ppermute | solution.py:906
  152.5 11.3 %collective-permute-start.34 = (bf16[528,512]{1,0:T(8,128)(2,1)S(1)}, bf16[528,512]{1,0:T(8,128)(2,1)S(1)}, u32[]{:S(2)}, u32[]{:S(2)}) collective-permute-start(bf16[528,512]{1,0:T(8,128)(2,1)S(1)} %choose.21.mine_ref), channel_id=1, source_target_pairs={{0,4},{4,0},{1,5},{5,1},{2,6},{6,2},{3,7},{7,3},{8,12},{12,8},{9,1... | collective-permute-start | bytes 1622024 | tf_op jit(solution)/shard_map/ppermute | solution.py:906
  153.3 4.1 %collective-permute-start.31 = (f32[16,512]{1,0:T(8,128)S(1)}, f32[16,512]{1,0:T(8,128)S(1)}, u32[]{:S(2)}, u32[]{:S(2)}) collective-permute-start(f32[16,512]{1,0:T(8,128)S(1)} %get-tuple-element.455.a_ref.v_ref), channel_id=1, source_target_pairs={{0,1},{1,0},{2,3},{3,2},{4,5},{5,4},{6,7},{7,6},{8,9},{9,8},{10,11... | collective-permute-start | bytes 98312 | tf_op jit(solution)/shard_map/ppermute | solution.py:906
  157.4 4.5 %collective-permute-start.33 = (f32[16,512]{1,0:T(8,128)S(1)}, f32[16,512]{1,0:T(8,128)S(1)}, u32[]{:S(2)}, u32[]{:S(2)}) collective-permute-start(f32[16,512]{1,0:T(8,128)S(1)} %add.46.a_ref), channel_id=1, source_target_pairs={{0,2},{1,3},{2,0},{3,1},{4,6},{5,7},{6,4},{7,5},{8,10},{9,11},{10,... | collective-permute-start | bytes 98312 | tf_op jit(solution)/shard_map/ppermute | solution.py:906

commit v4 on v3

--- a/solution.py
+++ b/solution.py
@@ -544,28 +544,33 @@
 EXTRA = 16
 
 
-def unit_struct(rows, cols):
-    return struct((rows + EXTRA, cols), BF16)
+def unit_struct(rows, cols, extra=EXTRA):
+    return struct((rows + extra, cols), BF16)
+
+
+def own_rows(message):
+    return message.shape[0] - message.shape[0] % (2 * EXTRA)
 
 
 def fill(ref, *values):
-    rows = ref.shape[0] - EXTRA
+    rows = own_rows(ref)
     at = 0
     for value in values:
         for first in range(0, value.shape[0], rows):
             ref[:rows, at : at + value.shape[1]] = value[first : first + rows]
             at += value.shape[1]
-    ref[rows:] = jnp.zeros((EXTRA, ref.shape[1]), ref.dtype)
+    if rows < ref.shape[0]:
+        ref[rows:] = jnp.zeros((EXTRA, ref.shape[1]), ref.dtype)
 
 
 def unfold(value, lanes, index, count):
-    rows = value.shape[0] - EXTRA
+    rows = own_rows(value)
     folds = [value[:rows, (index * count + i) * lanes : (index * count + i + 1) * lanes] for i in range(count)]
     return jnp.concatenate(folds, axis=0)
 
 
 def weights_kernel(near_ref, pair_ref, act_o_ref, dy_o_ref, act_ref, slope_ref, down_ref, ow_ref,
-                   dy_ref, gu_ref, ga_ref, gd_ref):
+                   gu_ref, ga_ref, gd_ref, dy_ref):
     hidden = slope_ref.shape[1]
 
     def put(at, dy):
@@ -585,10 +590,10 @@
 def weights_call(near, pair, act_o, dy_o, act, slope, down_w, out_w):
     rows, width = dy_o.shape
     hidden = slope.shape[1]
-    outs = [struct((rows, width), BF16), struct((rows, hidden), BF16), struct((2 * rows, 2 * HEAD_DIM), BF16)]
-    outs.append(unit_struct(hidden, width // 2))
+    outs = [struct((rows, hidden), BF16), struct((2 * rows, 2 * HEAD_DIM), BF16)]
+    outs.append(unit_struct(hidden, width // 2, EXTRA))
     arrays = (near, pair, act_o, dy_o, act, slope, down_w, out_w)
-    return fetched(weights_kernel, arrays, outs, "weights", 4e9)
+    return fetched(weights_kernel, arrays, outs, "weights", 4e9, 0, [pltpu.VMEM((rows, width), BF16)])
 
 
 def in_order(own, other, axis=0):
@@ -652,18 +657,25 @@
 
 
 def attend_kernel(*refs):
-    heads, (att_in, gp_in), later, outs = refs[:10], refs[10:12], refs[12:20], refs[20:26]
-    att_ref, gp_ref, *held, sems = refs[26 + 5 :]
+    heads, (att_in, gp_in), later, outs = refs[:10], refs[10:12], refs[12:21], refs[21:27]
+    att_ref, gp_ref, *held, sems = refs[27 + 5 :]
     keep_ref, send_ref, qk_grad_ref, vo_grad_ref, *up_refs = outs
     n1_o_ref, n1_x_ref, dy_o_ref, dy_x_ref, n2_o_ref, n2_x_ref, gu_o_ref, gu_x_ref = held
     span, hidden = n1_o_ref.shape[0], gu_x_ref.shape[1]
     mine, theirs = half_at(ctx_flag(), span), half_at(1 - ctx_flag(), span)
-    sources = list(later)
-    sources[6] = later[6].at[:, half_at(ctx_flag(), hidden)]
-    copies = [pltpu.make_async_copy(src, dst, sems.at[i]) for i, (src, dst) in enumerate(zip(sources, held))]
+    n1_o, n1_x, dy_o, near, pair, n2_o, n2_x, gu_o, gu_x = later
+    core, half = core_flag(), span // 2
+    copies = [
+        pltpu.make_async_copy(src, dst, sems.at[i])
+        for i, (src, dst) in enumerate((
+            (n1_o, n1_o_ref), (n1_x, n1_x_ref), (dy_o, dy_o_ref),
+            (near, dy_x_ref.at[half_at(core, half)]), (pair, dy_x_ref.at[half_at(1 - core, half)]),
+            (n2_o, n2_o_ref), (n2_x, n2_x_ref), (gu_o.at[:, half_at(ctx_flag(), hidden)], gu_o_ref), (gu_x, gu_x_ref),
+        ))
+    ]
     for copy in copies:
         copy.start()
-    attend_head(1, *heads, *refs[26 : 26 + 5], att_ref, gp_ref)
+    attend_head(1, *heads, *refs[27 : 27 + 5], att_ref, gp_ref)
     for ref, at in ((keep_ref, mine), (send_ref, theirs)):
         ref[0] = att_ref[at] + att_in[at]
         for t in range(3):
@@ -678,7 +690,7 @@
     fill(vo_grad_ref, v_grad, o_grad)
     gu_o, gu_x = gu_o_ref[...], gu_x_ref[...]
     for i, ref in enumerate(up_refs):
-        at = slice(i * (ref.shape[0] - EXTRA), (i + 1) * (ref.shape[0] - EXTRA))
+        at = slice(i * own_rows(ref), (i + 1) * own_rows(ref))
         fill(ref, (dot_tn(n2_o_ref[:, at], gu_o) + dot_tn(n2_x_ref[:, at], gu_x)).astype(BF16))
 
 
@@ -687,7 +699,8 @@
     rows, lanes = ga.shape
     span, width = later[0].shape
     hidden = later[-1].shape[1]
-    outs = [struct((4, span, lanes), BF16)] * 2 + [unit_struct(width // 2, 4 * lanes)] * 2 + [unit_struct(width // 2, hidden)] * 2
+    outs = [struct((4, span, lanes), BF16)] * 2 + [unit_struct(width // 2, 4 * lanes) for _ in range(2)]
+    outs += [unit_struct(width // 2, hidden) for _ in range(2)]
     scratch = head_scratch(rows, lanes) + [pltpu.VMEM((rows, lanes), BF16), pltpu.VMEM((3, rows, lanes), BF16)]
     scratch += [pltpu.VMEM((span, width), BF16)] * 6 + [pltpu.VMEM((span, hidden), BF16)] * 2
     scratch.append(pltpu.SemaphoreType.DMA((len(later),)))
@@ -757,7 +770,7 @@
     grad_ref, vec_ref = refs[-2:]
     count, rows, lanes = grad_ref.shape
     value = jnp.where(ctx_flag() == pl.program_id(0), mine_ref[...], other_ref[...]).astype(F32)
-    folds = rows // (mine_ref.shape[0] - EXTRA)
+    folds = rows // own_rows(mine_ref)
     for t in range(count):
         grad_ref[t] = unfold(value, lanes, t, folds)
     at = slice(mine_ref.shape[0] - EXTRA, mine_ref.shape[0])
@@ -789,7 +802,7 @@
     value = jnp.where(ctx_flag() == pl.program_id(0), mine_ref[...], other_ref[...]).astype(F32)
     heads_ref, out_ref = refs[-2:]
     lanes = heads_ref.shape[2]
-    folds = heads_ref.shape[1] // (mine_ref.shape[0] - EXTRA)
+    folds = heads_ref.shape[1] // own_rows(mine_ref)
     heads_ref[0] = unfold(value, lanes, 0, folds)
     out_ref[...] = unfold(value, lanes, 1, folds).T
 
@@ -993,7 +1006,7 @@
 
     def weights():
         u.dy.advance()
-        s.dyx, s.gux, s.ga, grad = run(
+        s.gux, s.ga, grad = run(
             weights_call, *s.dy, s.act, dy, s.actx, s.slope, down_weight, out_weight)
         open_unit("D1", line_then_ctx, grad, placing(
             ["down"], place_halves_kernel, 2, [(hidden // 2, width // 2)], [lambda i: (i, 1)]))
@@ -1005,7 +1018,7 @@
         s.mine, s.theirs, s.qk, vo_grad, *ups = run(
             lambda *a: attend_call(a[:3], a[3:6], *a[6:10], a[10:12], *a[12:]),
             *s.qkv, *s.qkvx, s.ga, *s.ids, s.table, *s.first,
-            s.n1, s.n1x, dy, s.dyx, s.n2, s.n2x, s.gu, s.gux)
+            s.n1, s.n1x, dy, *s.dy, s.n2, s.n2x, s.gu, s.gux)
         open_unit("Q1", line_then_ctx, vo_grad, placing(
             ["qkv", "out"], place_pair_kernel, 2, [(1, width, lanes), (lanes, width)],
             [lambda i: (2, 0, i), lambda i: (i, 0)]))

time: 166 us -> 166 us (level)
  local copies, waits for them, and re-layouts: 7.11 us -> 5.19 us
  starting transfers between devices: 46.3 us -> 48.1 us
    ppermute x29, waiting for transfers between devices: 35.2 us -> 29.6 us  [advance(): self.message = lax.ppermute(value, axis, perm)]
    ppermute x4, waiting for transfers between devices: 9.31 us -> 14.1 us  [advance_with(): lax.ppermute(self.run(choose, outward, inward), 'dp', INWARD + OUTWARD)]
    unnamed x38, local copies, waits for them, and re-layouts: 5.15 us -> 3.23 us
  transfers between devices with their start and end apart: 35 -> 35, of which waited for: 14 -> 15; matrix products, arithmetic and copies ran while one was open for 1% -> 1% of each run, Pallas kernels for 33% -> 34%
where the time goes in v4:
time: 166 us; the launch traced here: 165 us
  Pallas kernels  57 us (34%)
  waiting for transfers between devices  53.6 us (32%)
  starting transfers between devices  48.1 us (29%)
  local copies, waits for them, and re-layouts  5.19 us (3%)
    ppermute x29, starting transfers between devices, advance(): self.message = lax.ppermute(value, axis, perm)  31.1 us
    ppermute x29, waiting for transfers between devices, advance(): self.message = lax.ppermute(value, axis, perm)  29.6 us
    pallas_call x4, Pallas kernels, fetched(): pl.pallas_call(kernel, grid=(1,), in_specs=[whole(a.shape) for a in array...  26.4 us
    ppermute x4, starting transfers between devices, advance_with(): lax.ppermute(self.run(choose, outward, inward), 'dp', INWARD + OUTWARD)  15.8 us
    ppermute x4, waiting for transfers between devices, advance_with(): lax.ppermute(self.run(choose, outward, inward), 'dp', INWARD + OUTWARD)  14.1 us
    pallas_call x33, Pallas kernels, small(): pl.pallas_call(kernel, in_specs=[resident()] * len(arrays), out_specs=[re...  12.6 us
    ppermute x2, waiting for transfers between devices, send(): return lax.ppermute(self.tied(value), axis, perm)  9.87 us
    pallas_call x7, Pallas kernels, step(): pl.pallas_call(kernel, grid=(count,), in_specs=[resident()] * 2 + [pl.Blo...  9.2 us
  transfers between devices with their start and end apart: 35, of which 15 were waited for; matrix products, arithmetic and copies ran while one was open for 1% of the time, Pallas kernels for 34%

profile of v4, /device:TPU:0, one launch (start us, length us, event | category | flops | bytes accessed | tf_op | source)
XLA Modules:
  0.0 165.5 jit_solution(2541190922680360489)
XLA Ops:
  0.7 1.1 dynamic-slice_bitcast_fusion
  1.7 3.0 %collective-permute-start = (bf16[256,1024]{1,0:T(8,128)(2,1)S(1)}, bf16[256,1024]{1,0:T(8,128)(2,1)S(1)}, u32[]{:S(2)}, u32[]{:S(2)}) collective-permute-start(bf16[256,1024]{1,0:T(8,128)(2,1)S(1)} %dynamic-slice_bitcast_fusion), channel_id=1, source_target_pairs={{0,4},{4,0},{1,5},{5,1},{2,6},{6,2},{3,7},{7,3},{8,12},{12,8},{9,1... | collective-permute-start | bytes 1572872 | tf_op jit(solution)/shard_map/ppermute | solution.py:919
  4.8 0.8 stack.31.pack_ref
  5.6 1.2 copy-done.4
  6.8 5.2 %early.1 = (bf16[512,1024]{1,0:T(8,128)(2,1)S(1)}, bf16[512,1024]{1,0:T(8,128)(2,1)S(1)}, bf16[512,1024]{1,0:T(8,128)(2,1)S(1)}, bf16[512,1024]{1,0:T(8,128)(2,1...) custom-call(bf16[512,1024]{1,0:T(8,128)(2,1)S(1)} %bitcast.29, bf16[512,1024]{1,0:T(8,128)(2,1)} %bitcast.22, ...), custom_call_target="tpu_custom_call" | custom-call | flops 1024 | bytes 1024 | tf_op jit(solution)/shard_map/early/pallas_call | solution.py:474
  12.0 1.0 copy-done.9
  13.0 3.5 %collective-permute-start.3 = (bf16[528,512]{1,0:T(8,128)(2,1)S(1)}, bf16[528,512]{1,0:T(8,128)(2,1)S(1)}, u32[]{:S(2)}, u32[]{:S(2)}) collective-permute-start(bf16[528,512]{1,0:T(8,128)(2,1)S(1)} %get-tuple-element.276.a_ref), channel_id=1, source_target_pairs={{0,8},{24,16},{1,9},{25,17},{2,10},{26,18},{3,11},{27,19},{4,12},{... | collective-permute-start | bytes 1622024 | tf_op jit(solution)/shard_map/ppermute | solution.py:919
  16.5 3.7 %own.1 = (bf16[512,1024]{1,0:T(8,128)(2,1)S(1)}, bf16[512,1024]{1,0:T(8,128)(2,1)S(1)}, f32[1,1024]{1,0:T(1,128)S(1)}, bf16[528,512]{1,0:T(8,128)(2,1)S(1)}) custom-call(bf16[512,1024]{1,0:T(8,128)(2,1)S(1)} %get-tuple-element.330.n2_ref.refs_17_, bf16[512,1024]{1,0:T(8,128)(2,1)S(1)} %bitcast.24, ...), custom_call_target="tpu_custom_call", output_to_operand_aliasing={{0}: (5, {}), {1}: (6, {}), {2}: (7, {})} | custom-call | flops 1024 | bytes 1024 | tf_op jit(solution)/shard_map/own/pallas_call | solution.py:474
  20.6 0.6 collective-permute-start.2
  21.2 1.3 collective-permute-done.1.pair_ref
  22.5 6.4 %other.1 = (bf16[512,1024]{1,0:T(8,128)(2,1)S(1)}, bf16[512,1024]{1,0:T(8,128)(2,1)S(1)}, bf16[512,128]{1,0:T(8,128)(2,1)S(1)}, bf16[512,128]{1,0:T(8,128)(2,1)S...) custom-call(bf16[256,1024]{1,0:T(8,128)(2,1)S(1)} %collective-permut, ...), custom_call_target="tpu_custom_call" | custom-call | flops 1024 | bytes 1024 | tf_op jit(solution)/shard_map/other/pallas_call | solution.py:371
  28.9 1.0 copy-done.14
  30.0 0.7 collective-permute-start.7
  30.7 5.1 %collective-permute-start.6 = (bf16[528,512]{1,0:T(8,128)(2,1)S(1)}, bf16[528,512]{1,0:T(8,128)(2,1)S(1)}, u32[]{:S(2)}, u32[]{:S(2)}) collective-permute-start(bf16[528,512]{1,0:T(8,128)(2,1)S(1)} %get-tuple-element.311.a_ref), channel_id=1, source_target_pairs={{0,8},{24,16},{1,9},{25,17},{2,10},{26,18},{3,11},{27,19},{4,12},{... | collective-permute-start | bytes 1622024 | tf_op jit(solution)/shard_map/ppermute | solution.py:919
  35.9 0.6 collective-permute-start.5
  36.5 1.3 collective-permute-done.4.pair_ref.refs_16_
  37.8 3.8 %weights.1 = (bf16[512,512]{1,0:T(8,128)(2,1)S(1)}, bf16[1024,128]{1,0:T(8,128)(2,1)S(1)}, bf16[528,512]{1,0:T(8,128)(2,1)S(1)}) custom-call(bf16[256,1024]{1,0:T(8,128)(2,1)S(1)} %collective-permute-done.2.near_ref.refs_15_, bf16[256,1024]{1,0:T(8,128)(2,1)S(1)} %collective-permute-done.4.pair_ref.refs_16_, ...), custom_call_target="tpu_custom_call" | custom-call | flops 1024 | bytes 1024 | tf_op jit(solution)/shard_map/weights/pallas_call | solution.py:371
  41.6 1.5 collective-permute-start.10
  43.1 5.5 %first_head.1 = (bf16[1024,128]{1,0:T(8,128)(2,1)S(1)}, bf16[3,1024,128]{2,1,0:T(8,128)(2,1)S(1)}) custom-call(bf16[512,128]{1,0:T(8,128)(2,1)S(1)} %get-tuple-element.313.refs_0_, bf16[512,128]{1,0:T(8,128)(2,1)S(1)} %get-tuple-element.314.refs_1_, bf16[512,128]{1,0:T(8,128)(2,1)S(1)} %get-tuple-element.315.refs_2_, ...), custom_call_target="tpu_custom_call" | custom-call | flops 1024 | bytes 1024 | tf_op jit(solution)/shard_map/first_head/pallas_call | solution.py:371
  48.9 0.7 collective-permute-start.11
  49.6 1.3 collective-permute-start.9
  51.0 10.7 %attend.1 = (bf16[4,512,128]{2,1,0:T(8,128)(2,1)S(1)}, bf16[4,512,128]{2,1,0:T(8,128)(2,1)}, bf16[528,512]{1,0:T(8,128)(2,1)S(1)}, bf16[528,512]{1,0:T(8,128)(2,...) custom-call(bf16[512,128]{1,0:T(8,128)(2,1)S(1)} %get-tuple-element.313.refs_0_, ...), custom_call_target="tpu_custom_call" | custom-call | flops 1024 | bytes 1024 | tf_op jit(solution)/shard_map/attend/pallas_call | solution.py:371
  62.0 3.9 %collective-permute-start.12 = (bf16[528,512]{1,0:T(8,128)(2,1)S(1)}, bf16[528,512]{1,0:T(8,128)(2,1)S(1)}, u32[]{:S(2)}, u32[]{:S(2)}) collective-permute-start(bf16[528,512]{1,0:T(8,128)(2,1)S(1)} %choose.11), channel_id=1, source_target_pairs={{0,8},{24,16},{8,0},{16,24},{1,9},{25,17},{9,1},{17,25},{2,10},{26... | collective-permute-start | bytes 1622024 | tf_op jit(solution)/shard_map/ppermute | solution.py:923
  65.9 0.9 collective-permute-start.13
  66.9 0.6 collective-permute-start.8
  67.5 3.0 %branch_sums.1 = (f32[512,1024]{1,0:T(8,128)S(1)}, f32[512,1024]{1,0:T(8,128)S(1)}, f32[8,1024]{1,0:T(8,128)S(1)}) custom-call(bf16[512,1024]{1,0:T(8,128)(2,1)S(1)} %get-tuple-element.348.act_o_ref.act_ref, bf16[512,1024]{1,0:T(8,128)(2,1)S(1)} %copy-done.7, bf16[512,1024]{1,0:T(8,128)(2,1)S(1)} %bitcast.27, bf16[512,1024]{1,0:T(8,128)(2,1)S(1)} %bitcast.30, ...), custom_call_target="tpu_custom_call" | custom-call | flops 1024 | bytes 1024 | tf_op jit(solution)/shard_map/branch_sums/pallas_call | solution.py:358
  70.6 1.5 collective-permute-start.16
  72.2 9.9 %collective-permute-done.8.recv_ref = bf16[4,512,128]{2,1,0:T(8,128)(2,1)S(1)} collective-permute-done((bf16[4,512,128]{2,1,0:T(8,128)(2,1)}, bf16[4,512,128]{2,1,0:T(8,128)(2,1)S(1)}, u32[]{:S(2)}, u32[]{:S(2)}) %collective-permute-start.8) | collective-permute-done | bytes 524320 | tf_op jit(solution)/shard_map/ppermute | solution.py:855
  82.0 3.2 %sums.1 = (bf16[512,1024]{1,0:T(8,128)(2,1)S(1)}, bf16[512,1024]{1,0:T(8,128)(2,1)S(1)}, bf16[16,512]{1,0:T(8,128)(2,1)S(1)}) custom-call(bf16[4,512,128]{2,1,0:T(8,128)(2,1)S(1)} %get-tuple-element.362.mine_ref, bf16[4,512,128]{2,1,0:T(8,128)(2,1)S(1)} %collective-permute-done.8.recv_ref, f32[512,1024]{1,0:T(8,128)S(1)} %get-tuple-element.364.out_ref, ...), custom_call_target="tpu_custom_call" | custom-call | flops 1024 | bytes 1024 | tf_op jit(solution)/shard_map/sums/pallas_call | solution.py:358
  85.6 3.2 %collective-permute-start.15 = (bf16[528,512]{1,0:T(8,128)(2,1)S(1)}, bf16[528,512]{1,0:T(8,128)(2,1)S(1)}, u32[]{:S(2)}, u32[]{:S(2)}) collective-permute-start(bf16[528,512]{1,0:T(8,128)(2,1)S(1)} %choose.13), channel_id=1, source_target_pairs={{0,8},{24,16},{8,0},{16,24},{1,9},{25,17},{9,1},{17,25},{2,10},{26... | collective-permute-start | bytes 1622024 | tf_op jit(solution)/shard_map/ppermute | solution.py:923
  88.8 0.7 collective-permute-start.17
  89.7 0.6 collective-permute-start.21
  90.2 0.8 collective-permute-done.16.other_ref
  91.0 1.1 place.7.refs_0_
  92.1 5.6 %collective-permute-done.15.b_ref = bf16[528,512]{1,0:T(8,128)(2,1)S(1)} collective-permute-done((bf16[528,512]{1,0:T(8,128)(2,1)S(1)}, bf16[528,512]{1,0:T(8,128)(2,1)S(1)}, u32[]{:S(2)}, u32[]{:S(2)}) %collective-permute-start.15) | collective-permute-done | bytes 540704 | tf_op jit(solution)/shard_map/ppermute | solution.py:923
  97.9 4.4 %collective-permute-start.20 = (bf16[528,512]{1,0:T(8,128)(2,1)S(1)}, bf16[528,512]{1,0:T(8,128)(2,1)S(1)}, u32[]{:S(2)}, u32[]{:S(2)}) collective-permute-start(bf16[528,512]{1,0:T(8,128)(2,1)S(1)} %choose.15), channel_id=1, source_target_pairs={{0,8},{24,16},{8,0},{16,24},{1,9},{25,17},{9,1},{17,25},{2,10},{26... | collective-permute-start | bytes 1622024 | tf_op jit(solution)/shard_map/ppermute | solution.py:923
  102.4 0.7 collective-permute-start.19
  103.3 0.2 add.39.a_ref
  103.5 1.3 collective-permute-done.21.other_ref
  104.8 1.1 place.8.refs_0_
  105.9 5.3 %collective-permute-done.20.b_ref = bf16[528,512]{1,0:T(8,128)(2,1)S(1)} collective-permute-done((bf16[528,512]{1,0:T(8,128)(2,1)S(1)}, bf16[528,512]{1,0:T(8,128)(2,1)S(1)}, u32[]{:S(2)}, u32[]{:S(2)}) %collective-permute-start.20) | collective-permute-done | bytes 540704 | tf_op jit(solution)/shard_map/ppermute | solution.py:923
  111.4 4.4 %collective-permute-start.22 = (bf16[528,512]{1,0:T(8,128)(2,1)S(1)}, bf16[528,512]{1,0:T(8,128)(2,1)S(1)}, u32[]{:S(2)}, u32[]{:S(2)}) collective-permute-start(bf16[528,512]{1,0:T(8,128)(2,1)S(1)} %choose.17), channel_id=1, source_target_pairs={{0,8},{24,16},{8,0},{16,24},{1,9},{25,17},{9,1},{17,25},{2,10},{26... | collective-permute-start | bytes 1622024 | tf_op jit(solution)/shard_map/ppermute | solution.py:923
  115.9 0.7 collective-permute-start.23
  116.6 1.5 collective-permute-start.18
  118.5 1.4 place.9
  119.8 3.3 %collective-permute-done.22.b_ref = bf16[528,512]{1,0:T(8,128)(2,1)S(1)} collective-permute-done((bf16[528,512]{1,0:T(8,128)(2,1)S(1)}, bf16[528,512]{1,0:T(8,128)(2,1)S(1)}, u32[]{:S(2)}, u32[]{:S(2)}) %collective-permute-start.22) | collective-permute-done | bytes 540704 | tf_op jit(solution)/shard_map/ppermute | solution.py:923
  123.5 0.7 collective-permute-start.26
  124.2 1.3 collective-permute-start.30
  125.5 7.3 %collective-permute-done.18.b_ref = bf16[512,1024]{1,0:T(8,128)(2,1)S(1)} collective-permute-done((bf16[512,1024]{1,0:T(8,128)(2,1)S(1)}, bf16[512,1024]{1,0:T(8,128)(2,1)S(1)}, u32[]{:S(2)}, u32[]{:S(2)}) %collective-permute-start.18) | collective-permute-done | bytes 1048608 | tf_op jit(solution)/shard_map/ppermute | solution.py:919
  132.8 0.2 add.44.mine_ref
  133.3 1.4 place.10.refs_0_
  134.7 4.4 %collective-permute-done.27.other_ref = bf16[528,512]{1,0:T(8,128)(2,1)S(1)} collective-permute-done((bf16[528,512]{1,0:T(8,128)(2,1)S(1)}, bf16[528,512]{1,0:T(8,128)(2,1)S(1)}, u32[]{:S(2)}, u32[]{:S(2)}) %collective-permute-start.27) | collective-permute-done | bytes 540704 | tf_op jit(solution)/shard_map/ppermute | solution.py:919
  139.1 1.4 place.11
  140.7 1.6 collective-permute-start.29
  142.3 1.2 collective-permute-start.32
  143.6 9.5 %collective-permute-done.29.b_ref = bf16[528,512]{1,0:T(8,128)(2,1)S(1)} collective-permute-done((bf16[528,512]{1,0:T(8,128)(2,1)S(1)}, bf16[528,512]{1,0:T(8,128)(2,1)S(1)}, u32[]{:S(2)}, u32[]{:S(2)}) %collective-permute-start.29) | collective-permute-done | bytes 540704 | tf_op jit(solution)/shard_map/ppermute | solution.py:919
  153.1 1.3 collective-permute-start.34
  154.5 2.6 %results.1 = (bf16[512,1024]{1,0:T(8,128)(2,1)}, bf16[512,1024]{1,0:T(8,128)(2,1)}) custom-call(bf16[512,1024]{1,0:T(8,128)(2,1)S(1)} %add.44.mine_ref, bf16[512,1024]{1,0:T(8,128)(2,1)S(1)} %collective-permute-done.25.other_ref, bf16[512,1024]{1,0:T(8,128)(2,1)S(1)} %bitcast.32, bf16[512,1024]{1,0:T(8,128)(2,1)S(1)} %bitcast.28, f32[7,1024]{1,0:T(8,128)S(1)} %stack.31.pack_ref), custom_call_target="tpu_custom_call" | custom-call | flops 1024 | bytes 1024 | tf_op jit(solution)/shard_map/results/pallas_call | solution.py:358
  157.1 1.5 place.12
  158.6 1.5 collective-permute-start.33
  160.1 2.5 %collective-permute-done.33.b_ref = f32[16,512]{1,0:T(8,128)S(1)} collective-permute-done((f32[16,512]{1,0:T(8,128)S(1)}, f32[16,512]{1,0:T(8,128)S(1)}, u32[]{:S(2)}, u32[]{:S(2)}) %collective-permute-start.33) | collective-permute-done | bytes 32800 | tf_op jit(solution)/shard_map/ppermute | solution.py:919
  162.6 0.6 rows.1
  163.2 0.9 collective-permute-done.34.other_ref
  164.1 1.4 place.13
  (99 shorter events, 3.9 us)
Async XLA Ops:
  1.7 18.7 %collective-permute-start = (bf16[256,1024]{1,0:T(8,128)(2,1)S(1)}, bf16[256,1024]{1,0:T(8,128)(2,1)S(1)}, u32[]{:S(2)}, u32[]{:S(2)}) collective-permute-start(bf16[256,1024]{1,0:T(8,128)(2,1)S(1)} %dynamic-slice_bitcast_fusion), channel_id=1, source_target_pairs={{0,4},{4,0},{1,5},{5,1},{2,6},{6,2},{3,7},{7,3},{8,12},{12,8},{9,1... | collective-permute-start | bytes 1572872 | tf_op jit(solution)/shard_map/ppermute | solution.py:919
  5.6 1.2 copy-start.4
  6.8 9.7 %copy-start = (bf16[1,512,1024]{2,1,0:T(8,128)(2,1)S(1)}, bf16[1,512,1024]{2,1,0:T(8,128)(2,1)}, u32[]{:S(2)}) copy-start(bf16[1,512,1024]{2,1,0:T(8,128)(2,1)} %param.19) | copy-start | bytes 3145732
  12.0 1.0 copy-start.9
  13.0 7.2 %copy-start.10 = (bf16[512,1024]{1,0:T(8,128)(2,1)}, bf16[512,1024]{1,0:T(8,128)(2,1)S(1)}, u32[]{:S(2)}) copy-start(bf16[512,1024]{1,0:T(8,128)(2,1)S(1)} %get-tuple-element.330.n2_ref.refs_17_) | copy-start | bytes 3145732
  13.0 16.8 %collective-permute-start.3 = (bf16[528,512]{1,0:T(8,128)(2,1)S(1)}, bf16[528,512]{1,0:T(8,128)(2,1)S(1)}, u32[]{:S(2)}, u32[]{:S(2)}) collective-permute-start(bf16[528,512]{1,0:T(8,128)(2,1)S(1)} %get-tuple-element.276.a_ref), channel_id=1, source_target_pairs={{0,8},{24,16},{1,9},{25,17},{2,10},{26,18},{3,11},{27,19},{4,12},{... | collective-permute-start | bytes 1622024 | tf_op jit(solution)/shard_map/ppermute | solution.py:919
  16.5 5.9 %copy-start.16 = (f32[3,256]{1,0:T(4,128)S(1)}, f32[3,256]{1,0:T(4,128)}, u32[]{:S(2)}) copy-start(f32[3,256]{1,0:T(4,128)} %b_ref) | copy-start | bytes 9220
  20.2 8.7 %copy-start.6 = (bf16[512,1024]{1,0:T(8,128)(2,1)}, bf16[512,1024]{1,0:T(8,128)(2,1)S(1)}, u32[]{:S(2)}) copy-start(bf16[512,1024]{1,0:T(8,128)(2,1)S(1)} %get-tuple-element.349.refs_19_.gu_ref) | copy-start | bytes 3145732
  20.5 2.0 %collective-permute-start.1 = (bf16[256,1024]{1,0:T(8,128)(2,1)S(1)}, bf16[256,1024]{1,0:T(8,128)(2,1)S(1)}, u32[]{:S(2)}, u32[]{:S(2)}) collective-permute-start(bf16[256,1024]{1,0:T(8,128)(2,1)S(1)} %collective-permute-done.near_ref), channel_id=1, source_target_pairs={{0,1},{1,0},{2,3},{3,2},{4,5},{5,4},{6,7},{7,6},{8,9},{9,8},{10,11... | collective-permute-start | bytes 1572872 | tf_op jit(solution)/shard_map/ppermute | solution.py:919
  20.6 15.2 %collective-permute-start.2 = (bf16[256,1024]{1,0:T(8,128)(2,1)S(1)}, bf16[256,1024]{1,0:T(8,128)(2,1)S(1)}, u32[]{:S(2)}, u32[]{:S(2)}) collective-permute-start(bf16[256,1024]{1,0:T(8,128)(2,1)S(1)} %constant_dynamic-slice_fusion), channel_id=1, source_target_pairs={{0,4},{4,0},{1,5},{5,1},{2,6},{6,2},{3,7},{7,3},{8,12},{12,8},{9,1... | collective-permute-start | bytes 1572872 | tf_op jit(solution)/shard_map/ppermute | solution.py:919
  22.5 13.4 %copy-start.17 = (s32[1,512]{1,0:T(1,128)S(1)}, s32[1,512]{1,0:T(1,128)}, u32[]{:S(2)}) copy-start(s32[1,512]{1,0:T(1,128)} %param.18) | copy-start | bytes 6148
  22.5 13.4 %copy-start.18 = (s32[1,512]{1,0:T(1,128)S(1)}, s32[1,512]{1,0:T(1,128)}, u32[]{:S(2)}) copy-start(s32[1,512]{1,0:T(1,128)} %param.17) | copy-start | bytes 6148
  22.5 15.3 %copy-start.11 = (bf16[256,1024]{1,0:T(8,128)(2,1)S(1)}, bf16[256,1024]{1,0:T(8,128)(2,1)}, u32[]{:S(2)}) copy-start(bf16[256,1024]{1,0:T(8,128)(2,1)} %ow_ref.1) | copy-start | bytes 1572868
  28.9 1.0 copy-start.14
  29.8 7.9 %copy-start.12 = (f32[512,512]{1,0:T(8,128)}, f32[512,512]{1,0:T(8,128)S(1)}, u32[]{:S(2)}) copy-start(f32[512,512]{1,0:T(8,128)S(1)} %get-tuple-element.286.slope_ref) | copy-start | bytes 3145732
  29.8 11.8 %copy-start.13 = (bf16[512,1024]{1,0:T(8,128)(2,1)}, bf16[512,1024]{1,0:T(8,128)(2,1)S(1)}, u32[]{:S(2)}) copy-start(bf16[512,1024]{1,0:T(8,128)(2,1)S(1)} %get-tuple-element.326.refs_13_) | copy-start | bytes 3145732
  30.0 18.7 %collective-permute-start.7 = (bf16[528,512]{1,0:T(8,128)(2,1)S(1)}, bf16[528,512]{1,0:T(8,128)(2,1)S(1)}, u32[]{:S(2)}, u32[]{:S(2)}) collective-permute-start(bf16[528,512]{1,0:T(8,128)(2,1)S(1)} %add.30.a_ref), channel_id=1, source_target_pairs={{8,16},{16,8},{9,17},{17,9},{10,18},{18,10},{11,19},{19,11},{12,20... | collective-permute-start | bytes 1622024 | tf_op jit(solution)/shard_map/ppermute | solution.py:919
  30.7 18.1 %collective-permute-start.6 = (bf16[528,512]{1,0:T(8,128)(2,1)S(1)}, bf16[528,512]{1,0:T(8,128)(2,1)S(1)}, u32[]{:S(2)}, u32[]{:S(2)}) collective-permute-start(bf16[528,512]{1,0:T(8,128)(2,1)S(1)} %get-tuple-element.311.a_ref), channel_id=1, source_target_pairs={{0,8},{24,16},{1,9},{25,17},{2,10},{26,18},{3,11},{27,19},{4,12},{... | collective-permute-start | bytes 1622024 | tf_op jit(solution)/shard_map/ppermute | solution.py:919
  35.8 2.0 %collective-permute-start.4 = (bf16[256,1024]{1,0:T(8,128)(2,1)S(1)}, bf16[256,1024]{1,0:T(8,128)(2,1)S(1)}, u32[]{:S(2)}, u32[]{:S(2)}) collective-permute-start(bf16[256,1024]{1,0:T(8,128)(2,1)S(1)} %collective-permute-done.2.near_ref.refs_15_), channel_id=1, source_target_pairs={{0,1},{1,0},{2,3},{3,2},{4,5},{5,4},{6,7},{7,6},{8,9},{9,8},{10,11... | collective-permute-start | bytes 1572872 | tf_op jit(solution)/shard_map/ppermute | solution.py:919
  35.9 5.7 %collective-permute-start.5 = (s32[2,512]{1,0:T(2,128)S(1)}, s32[2,512]{1,0:T(2,128)S(1)}, u32[]{:S(2)}, u32[]{:S(2)}) collective-permute-start(s32[2,512]{1,0:T(2,128)S(1)} %pad_add_fusion.refs_7_), channel_id=1, source_target_pairs={{0,4},{4,0},{1,5},{5,1},{2,6},{6,2},{3,7},{7,3},{8,12},{12,8},{9,1... | collective-permute-start | bytes 12296 | tf_op jit(solution)/shard_map/ppermute | solution.py:855
  41.6 20.1 %collective-permute-start.10 = (bf16[528,512]{1,0:T(8,128)(2,1)S(1)}, bf16[528,512]{1,0:T(8,128)(2,1)S(1)}, u32[]{:S(2)}, u32[]{:S(2)}) collective-permute-start(bf16[528,512]{1,0:T(8,128)(2,1)S(1)} %get-tuple-element.346.a_ref), channel_id=1, source_target_pairs={{0,8},{24,16},{1,9},{25,17},{2,10},{26,18},{3,11},{27,19},{4,12},{... | collective-permute-start | bytes 1622024 | tf_op jit(solution)/shard_map/ppermute | solution.py:919
  48.6 2.3 %copy-start.15 = (bf16[3,1024,128]{2,1,0:T(8,128)(2,1)}, bf16[3,1024,128]{2,1,0:T(8,128)(2,1)S(1)}, u32[]{:S(2)}) copy-start(bf16[3,1024,128]{2,1,0:T(8,128)(2,1)S(1)} %get-tuple-element.324.refs_11_) | copy-start | bytes 2359300
  48.9 12.8 %collective-permute-start.11 = (bf16[528,512]{1,0:T(8,128)(2,1)S(1)}, bf16[528,512]{1,0:T(8,128)(2,1)S(1)}, u32[]{:S(2)}, u32[]{:S(2)}) collective-permute-start(bf16[528,512]{1,0:T(8,128)(2,1)S(1)} %add.32.a_ref), channel_id=1, source_target_pairs={{8,16},{16,8},{9,17},{17,9},{10,18},{18,10},{11,19},{19,11},{12,20... | collective-permute-start | bytes 1622024 | tf_op jit(solution)/shard_map/ppermute | solution.py:919
  49.6 20.9 %collective-permute-start.9 = (bf16[528,512]{1,0:T(8,128)(2,1)S(1)}, bf16[528,512]{1,0:T(8,128)(2,1)S(1)}, u32[]{:S(2)}, u32[]{:S(2)}) collective-permute-start(bf16[528,512]{1,0:T(8,128)(2,1)S(1)} %add.31.a_ref), channel_id=1, source_target_pairs={{8,0},{16,24},{9,1},{17,25},{10,2},{18,26},{11,3},{19,27},{12,4},{... | collective-permute-start | bytes 1622024 | tf_op jit(solution)/shard_map/ppermute | solution.py:919
  51.0 16.6 %copy-start.3 = (bf16[1024,1024]{1,0:T(8,128)(2,1)S(1)}, bf16[1024,1024]{1,0:T(8,128)(2,1)}, u32[]{:S(2)}) copy-start(bf16[1024,1024]{1,0:T(8,128)(2,1)} %down_ref.4) | copy-start | bytes 6291460
  51.0 16.5 %copy-start.7 = (bf16[512,1024]{1,0:T(8,128)(2,1)S(1)}, bf16[512,1024]{1,0:T(8,128)(2,1)}, u32[]{:S(2)}) copy-start(bf16[512,1024]{1,0:T(8,128)(2,1)} %copy-done.6) | copy-start | bytes 3145732
  61.7 5.8 %copy-start.1 = (bf16[1,512,1024]{2,1,0:T(8,128)(2,1)S(1)}, bf16[1,512,1024]{2,1,0:T(8,128)(2,1)}, u32[]{:S(2)}) copy-start(bf16[1,512,1024]{2,1,0:T(8,128)(2,1)} %param.19) | copy-start | bytes 3145732
  61.7 5.8 %copy-start.2 = (bf16[1024,1024]{1,0:T(8,128)(2,1)S(1)}, bf16[1024,1024]{1,0:T(8,128)(2,1)}, u32[]{:S(2)}) copy-start(bf16[1024,1024]{1,0:T(8,128)(2,1)} %up_ref.4) | copy-start | bytes 6291460
  61.7 5.8 %copy-start.5 = (bf16[1,512,1024]{2,1,0:T(8,128)(2,1)S(1)}, bf16[1,512,1024]{2,1,0:T(8,128)(2,1)}, u32[]{:S(2)}) copy-start(bf16[1,512,1024]{2,1,0:T(8,128)(2,1)} %param.16) | copy-start | bytes 3145732
  62.0 23.4 %collective-permute-start.12 = (bf16[528,512]{1,0:T(8,128)(2,1)S(1)}, bf16[528,512]{1,0:T(8,128)(2,1)S(1)}, u32[]{:S(2)}, u32[]{:S(2)}) collective-permute-start(bf16[528,512]{1,0:T(8,128)(2,1)S(1)} %choose.11), channel_id=1, source_target_pairs={{0,8},{24,16},{8,0},{16,24},{1,9},{25,17},{9,1},{17,25},{2,10},{26... | collective-permute-start | bytes 1622024 | tf_op jit(solution)/shard_map/ppermute | solution.py:923
  65.9 19.4 %collective-permute-start.13 = (bf16[528,512]{1,0:T(8,128)(2,1)S(1)}, bf16[528,512]{1,0:T(8,128)(2,1)S(1)}, u32[]{:S(2)}, u32[]{:S(2)}) collective-permute-start(bf16[528,512]{1,0:T(8,128)(2,1)S(1)} %add.34.a_ref), channel_id=1, source_target_pairs={{8,16},{16,8},{9,17},{17,9},{10,18},{18,10},{11,19},{19,11},{12,20... | collective-permute-start | bytes 1622024 | tf_op jit(solution)/shard_map/ppermute | solution.py:919
  66.9 15.2 %copy-start.8 = (bf16[1024,3,256]{2,0,1:T(8,128)(2,1)S(1)}, bf16[1024,3,256]{2,0,1:T(8,128)(2,1)}, u32[]{:S(2)}) copy-start(bf16[1024,3,256]{2,0,1:T(8,128)(2,1)} %param.24) | copy-start | bytes 4718596
  66.9 15.1 %collective-permute-start.8 = (bf16[4,512,128]{2,1,0:T(8,128)(2,1)}, bf16[4,512,128]{2,1,0:T(8,128)(2,1)S(1)}, u32[]{:S(2)}, u32[]{:S(2)}) collective-permute-start(bf16[4,512,128]{2,1,0:T(8,128)(2,1)} %get-tuple-element.336), channel_id=1, source_target_pairs={{0,4},{4,0},{1,5},{5,1},{2,6},{6,2},{3,7},{7,3},{8,12},{12,8},{9,1... | collective-permute-start | bytes 1572872 | tf_op jit(solution)/shard_map/ppermute | solution.py:855
  70.6 20.4 %collective-permute-start.16 = (bf16[528,512]{1,0:T(8,128)(2,1)S(1)}, bf16[528,512]{1,0:T(8,128)(2,1)S(1)}, u32[]{:S(2)}, u32[]{:S(2)}) collective-permute-start(bf16[528,512]{1,0:T(8,128)(2,1)S(1)} %choose.12.mine_ref), channel_id=1, source_target_pairs={{0,4},{4,0},{1,5},{5,1},{2,6},{6,2},{3,7},{7,3},{8,12},{12,8},{9,1... | collective-permute-start | bytes 1622024 | tf_op jit(solution)/shard_map/ppermute | solution.py:919
  85.6 12.1 %collective-permute-start.15 = (bf16[528,512]{1,0:T(8,128)(2,1)S(1)}, bf16[528,512]{1,0:T(8,128)(2,1)S(1)}, u32[]{:S(2)}, u32[]{:S(2)}) collective-permute-start(bf16[528,512]{1,0:T(8,128)(2,1)S(1)} %choose.13), channel_id=1, source_target_pairs={{0,8},{24,16},{8,0},{16,24},{1,9},{25,17},{9,1},{17,25},{2,10},{26... | collective-permute-start | bytes 1622024 | tf_op jit(solution)/shard_map/ppermute | solution.py:923
  88.8 8.8 %collective-permute-start.17 = (bf16[528,512]{1,0:T(8,128)(2,1)S(1)}, bf16[528,512]{1,0:T(8,128)(2,1)S(1)}, u32[]{:S(2)}, u32[]{:S(2)}) collective-permute-start(bf16[528,512]{1,0:T(8,128)(2,1)S(1)} %add.36.a_ref), channel_id=1, source_target_pairs={{8,16},{16,8},{9,17},{17,9},{10,18},{18,10},{11,19},{19,11},{12,20... | collective-permute-start | bytes 1622024 | tf_op jit(solution)/shard_map/ppermute | solution.py:919
  89.6 13.6 %collective-permute-start.14 = (bf16[512,1024]{1,0:T(8,128)(2,1)S(1)}, bf16[512,1024]{1,0:T(8,128)(2,1)S(1)}, u32[]{:S(2)}, u32[]{:S(2)}) collective-permute-start(bf16[512,1024]{1,0:T(8,128)(2,1)S(1)} %get-tuple-element.388), channel_id=1, source_target_pairs={{0,1},{1,0},{2,3},{3,2},{4,5},{5,4},{6,7},{7,6},{8,9},{9,8},{10,11... | collective-permute-start | bytes 3145736 | tf_op jit(solution)/shard_map/ppermute | solution.py:919
  89.7 15.1 %collective-permute-start.21 = (bf16[528,512]{1,0:T(8,128)(2,1)S(1)}, bf16[528,512]{1,0:T(8,128)(2,1)S(1)}, u32[]{:S(2)}, u32[]{:S(2)}) collective-permute-start(bf16[528,512]{1,0:T(8,128)(2,1)S(1)} %choose.14.mine_ref), channel_id=1, source_target_pairs={{0,4},{4,0},{1,5},{5,1},{2,6},{6,2},{3,7},{7,3},{8,12},{12,8},{9,1... | collective-permute-start | bytes 1622024 | tf_op jit(solution)/shard_map/ppermute | solution.py:919
  97.9 13.3 %collective-permute-start.20 = (bf16[528,512]{1,0:T(8,128)(2,1)S(1)}, bf16[528,512]{1,0:T(8,128)(2,1)S(1)}, u32[]{:S(2)}, u32[]{:S(2)}) collective-permute-start(bf16[528,512]{1,0:T(8,128)(2,1)S(1)} %choose.15), channel_id=1, source_target_pairs={{0,8},{24,16},{8,0},{16,24},{1,9},{25,17},{9,1},{17,25},{2,10},{26... | collective-permute-start | bytes 1622024 | tf_op jit(solution)/shard_map/ppermute | solution.py:923
  102.4 8.8 %collective-permute-start.19 = (bf16[528,512]{1,0:T(8,128)(2,1)S(1)}, bf16[528,512]{1,0:T(8,128)(2,1)S(1)}, u32[]{:S(2)}, u32[]{:S(2)}) collective-permute-start(bf16[528,512]{1,0:T(8,128)(2,1)S(1)} %add.38.a_ref), channel_id=1, source_target_pairs={{8,16},{16,8},{9,17},{17,9},{10,18},{18,10},{11,19},{19,11},{12,20... | collective-permute-start | bytes 1622024 | tf_op jit(solution)/shard_map/ppermute | solution.py:919
  103.2 15.3 %collective-permute-start.24 = (bf16[528,512]{1,0:T(8,128)(2,1)S(1)}, bf16[528,512]{1,0:T(8,128)(2,1)S(1)}, u32[]{:S(2)}, u32[]{:S(2)}) collective-permute-start(bf16[528,512]{1,0:T(8,128)(2,1)S(1)} %choose.16.mine_ref), channel_id=1, source_target_pairs={{0,4},{4,0},{1,5},{5,1},{2,6},{6,2},{3,7},{7,3},{8,12},{12,8},{9,1... | collective-permute-start | bytes 1622024 | tf_op jit(solution)/shard_map/ppermute | solution.py:919
  111.4 11.7 %collective-permute-start.22 = (bf16[528,512]{1,0:T(8,128)(2,1)S(1)}, bf16[528,512]{1,0:T(8,128)(2,1)S(1)}, u32[]{:S(2)}, u32[]{:S(2)}) collective-permute-start(bf16[528,512]{1,0:T(8,128)(2,1)S(1)} %choose.17), channel_id=1, source_target_pairs={{0,8},{24,16},{8,0},{16,24},{1,9},{25,17},{9,1},{17,25},{2,10},{26... | collective-permute-start | bytes 1622024 | tf_op jit(solution)/shard_map/ppermute | solution.py:923
  115.9 7.3 %collective-permute-start.23 = (bf16[528,512]{1,0:T(8,128)(2,1)S(1)}, bf16[528,512]{1,0:T(8,128)(2,1)S(1)}, u32[]{:S(2)}, u32[]{:S(2)}) collective-permute-start(bf16[528,512]{1,0:T(8,128)(2,1)S(1)} %add.41.a_ref), channel_id=1, source_target_pairs={{8,16},{16,8},{9,17},{17,9},{10,18},{18,10},{11,19},{19,11},{12,20... | collective-permute-start | bytes 1622024 | tf_op jit(solution)/shard_map/ppermute | solution.py:919
  116.6 16.2 %collective-permute-start.18 = (bf16[512,1024]{1,0:T(8,128)(2,1)S(1)}, bf16[512,1024]{1,0:T(8,128)(2,1)S(1)}, u32[]{:S(2)}, u32[]{:S(2)}) collective-permute-start(bf16[512,1024]{1,0:T(8,128)(2,1)S(1)} %add.39.a_ref), channel_id=1, source_target_pairs={{0,2},{1,3},{2,0},{3,1},{4,6},{5,7},{6,4},{7,5},{8,10},{9,11},{10,... | collective-permute-start | bytes 3145736 | tf_op jit(solution)/shard_map/ppermute | solution.py:919
  118.2 15.2 %collective-permute-start.28 = (bf16[528,512]{1,0:T(8,128)(2,1)S(1)}, bf16[528,512]{1,0:T(8,128)(2,1)S(1)}, u32[]{:S(2)}, u32[]{:S(2)}) collective-permute-start(bf16[528,512]{1,0:T(8,128)(2,1)S(1)} %choose.18.mine_ref), channel_id=1, source_target_pairs={{0,4},{4,0},{1,5},{5,1},{2,6},{6,2},{3,7},{7,3},{8,12},{12,8},{9,1... | collective-permute-start | bytes 1622024 | tf_op jit(solution)/shard_map/ppermute | solution.py:919
  123.5 15.7 %collective-permute-start.27 = (bf16[528,512]{1,0:T(8,128)(2,1)S(1)}, bf16[528,512]{1,0:T(8,128)(2,1)S(1)}, u32[]{:S(2)}, u32[]{:S(2)}) collective-permute-start(bf16[528,512]{1,0:T(8,128)(2,1)S(1)} %choose.19.mine_ref), channel_id=1, source_target_pairs={{0,4},{4,0},{1,5},{5,1},{2,6},{6,2},{3,7},{7,3},{8,12},{12,8},{9,1... | collective-permute-start | bytes 1622024 | tf_op jit(solution)/shard_map/ppermute | solution.py:919
  123.5 17.0 %collective-permute-start.26 = (bf16[528,512]{1,0:T(8,128)(2,1)S(1)}, bf16[528,512]{1,0:T(8,128)(2,1)S(1)}, u32[]{:S(2)}, u32[]{:S(2)}) collective-permute-start(bf16[528,512]{1,0:T(8,128)(2,1)S(1)} %add.42.a_ref), channel_id=1, source_target_pairs={{8,16},{16,8},{9,17},{17,9},{10,18},{18,10},{11,19},{19,11},{12,20... | collective-permute-start | bytes 1622024 | tf_op jit(solution)/shard_map/ppermute | solution.py:919
  124.2 18.0 %collective-permute-start.30 = (bf16[528,512]{1,0:T(8,128)(2,1)S(1)}, bf16[528,512]{1,0:T(8,128)(2,1)S(1)}, u32[]{:S(2)}, u32[]{:S(2)}) collective-permute-start(bf16[528,512]{1,0:T(8,128)(2,1)S(1)} %add.43.a_ref), channel_id=1, source_target_pairs={{8,0},{16,24},{9,1},{17,25},{10,2},{18,26},{11,3},{19,27},{12,4},{... | collective-permute-start | bytes 1622024 | tf_op jit(solution)/shard_map/ppermute | solution.py:919
  133.1 21.4 %collective-permute-start.25 = (bf16[512,1024]{1,0:T(8,128)(2,1)S(1)}, bf16[512,1024]{1,0:T(8,128)(2,1)S(1)}, u32[]{:S(2)}, u32[]{:S(2)}) collective-permute-start(bf16[512,1024]{1,0:T(8,128)(2,1)S(1)} %add.44.mine_ref), channel_id=1, source_target_pairs={{0,1},{1,0},{2,3},{3,2},{4,5},{5,4},{6,7},{7,6},{8,9},{9,8},{10,11... | collective-permute-start | bytes 3145736 | tf_op jit(solution)/shard_map/ppermute | solution.py:919
  140.7 12.4 %collective-permute-start.29 = (bf16[528,512]{1,0:T(8,128)(2,1)S(1)}, bf16[528,512]{1,0:T(8,128)(2,1)S(1)}, u32[]{:S(2)}, u32[]{:S(2)}) collective-permute-start(bf16[528,512]{1,0:T(8,128)(2,1)S(1)} %add.45.a_ref), channel_id=1, source_target_pairs={{8,0},{16,24},{9,1},{17,25},{10,2},{18,26},{11,3},{19,27},{12,4},{... | collective-permute-start | bytes 1622024 | tf_op jit(solution)/shard_map/ppermute | solution.py:919
  142.3 14.8 %collective-permute-start.32 = (bf16[528,512]{1,0:T(8,128)(2,1)S(1)}, bf16[528,512]{1,0:T(8,128)(2,1)S(1)}, u32[]{:S(2)}, u32[]{:S(2)}) collective-permute-start(bf16[528,512]{1,0:T(8,128)(2,1)S(1)} %choose.20.mine_ref), channel_id=1, source_target_pairs={{0,4},{4,0},{1,5},{5,1},{2,6},{6,2},{3,7},{7,3},{8,12},{12,8},{9,1... | collective-permute-start | bytes 1622024 | tf_op jit(solution)/shard_map/ppermute | solution.py:919
  153.1 11.0 %collective-permute-start.34 = (bf16[528,512]{1,0:T(8,128)(2,1)S(1)}, bf16[528,512]{1,0:T(8,128)(2,1)S(1)}, u32[]{:S(2)}, u32[]{:S(2)}) collective-permute-start(bf16[528,512]{1,0:T(8,128)(2,1)S(1)} %choose.21.mine_ref), channel_id=1, source_target_pairs={{0,4},{4,0},{1,5},{5,1},{2,6},{6,2},{3,7},{7,3},{8,12},{12,8},{9,1... | collective-permute-start | bytes 1622024 | tf_op jit(solution)/shard_map/ppermute | solution.py:919
  154.5 4.1 %collective-permute-start.31 = (f32[16,512]{1,0:T(8,128)S(1)}, f32[16,512]{1,0:T(8,128)S(1)}, u32[]{:S(2)}, u32[]{:S(2)}) collective-permute-start(f32[16,512]{1,0:T(8,128)S(1)} %get-tuple-element.455.a_ref.v_ref), channel_id=1, source_target_pairs={{0,1},{1,0},{2,3},{3,2},{4,5},{5,4},{6,7},{7,6},{8,9},{9,8},{10,11... | collective-permute-start | bytes 98312 | tf_op jit(solution)/shard_map/ppermute | solution.py:919
  158.6 4.0 %collective-permute-start.33 = (f32[16,512]{1,0:T(8,128)S(1)}, f32[16,512]{1,0:T(8,128)S(1)}, u32[]{:S(2)}, u32[]{:S(2)}) collective-permute-start(f32[16,512]{1,0:T(8,128)S(1)} %add.46.a_ref), channel_id=1, source_target_pairs={{0,2},{1,3},{2,0},{3,1},{4,6},{5,7},{6,4},{7,5},{8,10},{9,11},{10,... | collective-permute-start | bytes 98312 | tf_op jit(solution)/shard_map/ppermute | solution.py:919
